TPU v7x, 128 devices: a whole 4x4x4 slice. The times are simulated.
128 devices in a mesh: seq: 16 (over y, x_hi, core), tp: 8 (over z, x_lo).
Axes of the slice: x: 4 (x_hi: 2, x_lo: 2; x = x_hi * 2 + x_lo), y: 4, z: 4, core: 2. Of those that a mesh axis runs over, the one named last changes fastest.
Arguments:
- resid: bfloat16 [32, 8192], P(None, 'seq'), may hold values from -40 to 40
- attn_gain: bfloat16 [8192], P('seq'), may hold values from 0.5 to 1.5
- ffn_gain: bfloat16 [8192], P('seq'), may hold values from 0.5 to 1.5
- w_query: bfloat16 [8192, 8192], P('seq', 'tp'), may hold values from -0.0625 to 0.0625
- w_key: bfloat16 [8192, 1024], P('seq', 'tp'), may hold values from -0.625 to 0.625
- w_value: bfloat16 [8192, 1024], P('seq', 'tp'), may hold values from -0.0625 to 0.0625
- w_out: bfloat16 [8192, 8192], P('tp', 'seq'), may hold values from -0.0625 to 0.0625
- rope_angle: float32 [32, 64], replicated, may hold values from -3.140625 to 3.140625
- positions: int32 [32], replicated, may hold values from 0 to 31
- cache_keys: bfloat16 [8, 262144, 128], P('tp', 'seq'), may hold values from -210 to 210
- cache_values: bfloat16 [8, 262144, 128], P('tp', 'seq'), may hold values from -6 to 6
- valid_lengths: int32 [16], P('seq'), may hold values from 1 to 16384, 196608 in all
- w_gate: bfloat16 [8192, 28672], P('seq', 'tp'), may hold values from -0.0625 to 0.0625
- w_up: bfloat16 [8192, 28672], P('seq', 'tp'), may hold values from -0.0625 to 0.0625
- w_down: bfloat16 [28672, 8192], P('tp', 'seq'), may hold values from -0.03125 to 0.03125
Outputs:
- attn_out: bfloat16 [32, 8192], P(None, 'seq')
- layer_out: bfloat16 [32, 8192], P(None, 'seq')
Inputs may be any that keep to these rules, and one draw needn't show every extreme that they name: `valid_lengths`: each block's valid tokens fill its first slots; at least one block is full.
All inputs are finite; a program needn't handle non-finite values.
Results may differ from a plain program's by a relative error of at most 0.012.
The roundings to bfloat16 on the way count: a program that leaves them out, or rounds other values in their place, can miss the bound.
Values may be sent and summed in bfloat16 or wider, within the bound.
No kernel may reach another device: no remote copies, remote signals or barrier semaphores. Data moves between devices by JAX's collectives and lax.ppermute only.
A program may use at most 128 MiB of HBM per device.

v0:
```python
import jax
import jax.numpy as jnp
from jax import lax
from jax.sharding import PartitionSpec as P

EPS = 1e-05


def shifted(shard, axis, by):
    count = lax.axis_size(axis)
    return lax.ppermute(shard, axis, [(i, (i + by) % count) for i in range(count)])


def rotate(values, angle):
    half = values.shape[-1] // 2
    cosine = jnp.cos(angle)[:, None, :]
    sine = jnp.sin(angle)[:, None, :]
    first = values[..., :half]
    second = values[..., half:]
    return jnp.concatenate(
        [first * cosine - second * sine, second * cosine + first * sine], axis=-1
    )


def merge_parts(left, right):
    top = jnp.maximum(left[0], right[0])
    f_left = jnp.exp(left[0] - top)
    f_right = jnp.exp(right[0] - top)
    return (
        top,
        left[1] * f_left + right[1] * f_right,
        left[2] * f_left[..., None] + right[2] * f_right[..., None],
    )


def body(
    resid,
    attn_gain,
    ffn_gain,
    w_query,
    w_key,
    w_value,
    w_out,
    rope_angle,
    positions,
    cache_keys,
    cache_values,
    valid_lengths,
    w_gate,
    w_up,
    w_down,
):
    width = resid.shape[1] * lax.axis_size("seq")
    rows = resid.shape[0]
    kv_local = cache_keys.shape[0]
    block_len = cache_keys.shape[1]
    head_dim = cache_keys.shape[2]
    heads_local = w_query.shape[1] // head_dim
    group = heads_local // kv_local
    scale = 1.0 / head_dim**0.5
    resid32 = resid.astype(jnp.float32)
    normed_in = (resid32 * attn_gain.astype(jnp.float32)).astype(jnp.bfloat16)
    q_part = jnp.dot(normed_in, w_query, preferred_element_type=jnp.float32)
    k_part = jnp.dot(normed_in, w_key, preferred_element_type=jnp.float32)
    v_part = jnp.dot(normed_in, w_value, preferred_element_type=jnp.float32)
    square_part = jnp.sum(resid32 * resid32, axis=1)
    q_sum, k_sum, v_sum, square_sum = lax.psum((q_part, k_part, v_part, square_part), "seq")
    inv_first = lax.rsqrt(square_sum / width + EPS)[:, None]
    query = rotate((q_sum * inv_first).reshape(rows, heads_local, head_dim), rope_angle).astype(
        jnp.bfloat16
    )
    key_new = rotate((k_sum * inv_first).reshape(rows, kv_local, head_dim), rope_angle).astype(
        jnp.bfloat16
    )
    value_new = (v_sum * inv_first).reshape(rows, kv_local, head_dim).astype(jnp.bfloat16)
    grouped = query.reshape(rows, kv_local, group, head_dim)
    scores = (
        jnp.einsum("rkgd,ktd->kgrt", grouped, cache_keys, preferred_element_type=jnp.float32)
        * scale
    )
    live = jnp.arange(block_len, dtype=jnp.int32) < valid_lengths[0]
    scores = jnp.where(live, scores, jnp.float32(-1e30))
    top = jnp.max(scores, axis=-1)
    weights = jnp.exp(scores - top[..., None]).astype(jnp.bfloat16)
    total = jnp.sum(weights.astype(jnp.float32), axis=-1)
    summed = jnp.einsum("kgrt,ktd->kgrd", weights, cache_values, preferred_element_type=jnp.float32)
    local = (top, total, summed)

    def cycle_turn(turn, carry):
        gathered, moving = carry
        moving = shifted((moving[0], moving[1], moving[2]), "seq", 1)
        return (merge_parts(gathered, moving), moving)

    combined, moving = lax.fori_loop(0, lax.axis_size("seq") - 1, cycle_turn, (local, local))
    new_scores = (
        jnp.einsum("rkgd,skd->kgrs", grouped, key_new, preferred_element_type=jnp.float32) * scale
    )
    allowed = positions[None, :] <= positions[:, None]
    new_scores = jnp.where(allowed, new_scores, jnp.float32(-1e30))
    new_top = jnp.max(new_scores, axis=-1)
    new_weights = jnp.exp(new_scores - new_top[..., None]).astype(jnp.bfloat16)
    new_total = jnp.sum(new_weights.astype(jnp.float32), axis=-1)
    new_summed = jnp.einsum(
        "kgrs,skd->kgrd", new_weights, value_new, preferred_element_type=jnp.float32
    )
    top, total, summed = merge_parts(combined, (new_top, new_total, new_summed))
    attn = (
        (summed / total[..., None])
        .transpose(2, 0, 1, 3)
        .reshape(rows, heads_local * head_dim)
        .astype(jnp.bfloat16)
    )
    out_part = jnp.dot(attn, w_out, preferred_element_type=jnp.float32)
    attn_out = lax.psum(out_part, "tp").astype(jnp.bfloat16)
    hidden_mid = (resid32 + lax.optimization_barrier(attn_out).astype(jnp.float32)).astype(
        jnp.bfloat16
    )
    mid32 = lax.optimization_barrier(hidden_mid).astype(jnp.float32)
    normed_mid = (mid32 * ffn_gain.astype(jnp.float32)).astype(jnp.bfloat16)
    gate_part = jnp.dot(normed_mid, w_gate, preferred_element_type=jnp.float32)
    up_part = jnp.dot(normed_mid, w_up, preferred_element_type=jnp.float32)
    mid_square = jnp.sum(mid32 * mid32, axis=1)
    gate_sum, up_sum, mid_sum = lax.psum((gate_part, up_part, mid_square), "seq")
    inv_second = lax.rsqrt(mid_sum / width + EPS)[:, None]
    act = (jax.nn.silu(gate_sum * inv_second) * (up_sum * inv_second)).astype(jnp.bfloat16)
    down_part = jnp.dot(act, w_down, preferred_element_type=jnp.float32)
    down_sum = lax.psum(down_part, "tp")
    layer_out = (mid32 + down_sum).astype(jnp.bfloat16)
    return (attn_out, layer_out)


def solution(mesh):
    in_specs = (
        P(None, "seq"),
        P("seq"),
        P("seq"),
        P("seq", "tp"),
        P("seq", "tp"),
        P("seq", "tp"),
        P("tp", "seq"),
        P(),
        P(),
        P("tp", "seq", None),
        P("tp", "seq", None),
        P("seq"),
        P("seq", "tp"),
        P("seq", "tp"),
        P("tp", "seq"),
    )
    out_specs = (P(None, "seq"), P(None, "seq"))
    return jax.shard_map(body, mesh=mesh, in_specs=in_specs, out_specs=out_specs, check_vma=False)
```

profile of v0, /device:TPU:1, one launch (start us, length us, event | category | flops | bytes accessed | tf_op | source)
XLA Modules:
  0.0 568.4 jit_solution(13304408959356991381)
XLA Ops:
  8.4 1.7 fusion.43
  10.2 0.9 fusion.25
  11.1 1.1 fusion.41
  12.1 1.1 fusion.39
  13.2 65.3 %all-reduce = (f32[32]{0:T(128)S(1)}, f32[32,128]{1,0:T(8,128)S(1)}, f32[32,128]{1,0:T(8,128)S(1)}) all-reduce(f32[32]{0:T(128)S(1)} %fusion.25, f32[32,128]{1,0:T(8,128)S(1)} %fusion.41, f32[32,128]{1,0:T(8,128)S(1)} %fusion.39), channel_id=1, replica_groups=mesh['seq'=16,'tp'=8] {'seq'}, use_global_device_ids=true, to_apply=%region_2.0 | all-reduce | flops 8224 | bytes 65792 | tf_op jit(solution)/shard_map/psum | solution.py:67
  78.5 0.8 fusion.64
  80.8 0.8 broadcast_compare_fusion
  81.6 68.4 %all-reduce.6.cloned.1.call-done = f32[32,1024]{1,0:T(8,128)} async-done(((f32[32,1024]{1,0:T(8,128)}), f32[32,1024]{1,0:T(8,128)}) %all-reduce.6.cloned.1.call-update) | async-done | bytes 131088 | tf_op jit(solution)/shard_map/psum | solution.py:67
  150.0 1.0 multiply_bitcast_fusion
  151.3 9.3 %fusion.65 = (f32[8,32]{0,1:T(8,128)S(1)}, f32[1,8,32,16384]{3,1,2,0:T(8,128)}) fusion(bf16[32,8,128]{2,1,0:T(8,128)(2,1)S(1)} %pad_maximum_fusion, bf16[1,16384,128]{2,1,0:T(8,128)(2,1)} %param.26, pred[16384]{0:T(1024)(128)(4,1)S(1)} %iota_compare_fusion), kind=kOutput, calls=%fused_computation.91 | convolution fusion | flops 1086324480 | bytes 21054464 | tf_op jit(solution)/shard_map/rkgd,ktd->kgrt/dot_general | solution.py:78
  160.6 8.1 %convert_reduce_fusion = f32[8,32]{0,1:T(8,128)S(1)} fusion(f32[1,8,32,16384]{3,1,2,0:T(8,128)} %get-tuple-element.84, f32[8,32]{0,1:T(8,128)S(1)} %get-tuple-element.83), kind=kLoop, calls=%fused_computation.10 | loop fusion | flops 16776960 | bytes 16779264 | tf_op jit(solution)/shard_map/reduce_sum | solution.py:85
  168.8 8.4 %fusion.9 = f32[1,8,32,128]{3,1,2,0:T(8,128)S(1)} fusion(bf16[1,16384,128]{2,1,0:T(8,128)(2,1)} %param.27, f32[1,8,32,16384]{3,1,2,0:T(8,128)} %get-tuple-element.84, f32[8,32]{0,1:T(8,128)S(1)} %get-tuple-element.83), kind=kOutput, calls=%fused_computation.16 | convolution fusion | flops 1082130432 | bytes 21103616 | tf_op jit(solution)/shard_map/kgrt,ktd->kgrd/dot_general | solution.py:86
  177.7 131.0 %while.20 = (s32[]{:T(128)}, f32[1,8,32]{2,1,0:T(8,128)S(1)}, f32[1,8,32]{2,1,0:T(8,128)S(1)}, f32[1,8,32,128]{3,2,1,0:T(8,128)S(1)}, f32[1,8,32]{2,1,0:T(8,128)...) while((s32[]{:T(128)}, f32[1,8,32]{2,1,0:T(8,128)S(1)}, ...), condition=%wide.region_6.7_spmd, body=%wide.region_5.6_spmd.sunk | while | flops 100098 | bytes 1207501 | solution.py:94
  177.9 1.1 collective-permute-done
  180.0 4.0 collective-permute-start
  184.2 3.2 collective-permute-done
  188.0 2.4 collective-permute-start
  190.5 1.2 collective-permute-start.2
  191.6 4.2 collective-permute-done
  196.4 1.4 collective-permute-start
  197.9 1.8 collective-permute-start.2
  199.7 4.6 collective-permute-done
  204.8 1.0 collective-permute-start
  206.6 4.8 collective-permute-start.2
  211.5 1.3 collective-permute-done
  213.6 4.0 collective-permute-start
  217.6 1.0 collective-permute-start.1
  218.7 4.8 collective-permute-start.2
  223.6 1.9 collective-permute-done.2
  225.6 4.0 collective-permute-start
  230.1 4.8 collective-permute-start.2
  235.0 1.9 collective-permute-done.2
  237.1 4.0 collective-permute-start
  241.2 2.2 collective-permute-start.2
  243.4 1.9 collective-permute-done.2
  245.5 4.0 collective-permute-start
  249.6 2.2 collective-permute-start.2
  251.9 1.9 collective-permute-done.2
  254.0 4.0 collective-permute-start
  258.1 2.2 collective-permute-start.2
  260.3 1.9 collective-permute-done.2
  262.4 4.0 collective-permute-start
  266.5 2.2 collective-permute-start.2
  268.8 1.9 collective-permute-done.2
  270.8 4.0 collective-permute-start
  274.9 2.2 collective-permute-start.2
  277.2 1.9 collective-permute-done.2
  279.3 4.0 collective-permute-start
  283.4 2.2 collective-permute-start.2
  285.6 1.9 collective-permute-done.2
  287.7 4.0 collective-permute-start
  291.8 3.3 collective-permute-start.2
  295.1 1.9 collective-permute-done.2
  297.2 4.0 collective-permute-start
  301.7 4.8 collective-permute-start.2
  306.6 1.9 collective-permute-done.2
  309.2 27.9 %psum.67 = bf16[32,512]{1,0:T(8,128)(2,1)S(1)} all-reduce(f32[32,512]{1,0:T(8,128)S(1)} %fusion.30), channel_id=1, replica_groups=mesh['seq'=16,'tp'=8] {'tp'}, use_global_device_ids=true, to_apply=%region_11.12 | all-reduce | flops 16384 | bytes 98304 | tf_op jit(solution)/shard_map/psum | solution.py:114
  337.2 3.7 fusion.35
  340.9 1.5 fusion.37
  342.6 40.8 %psum.69 = f32[32]{0:T(128)S(1)} all-reduce(f32[32]{0:T(128)S(1)} %fusion.28), channel_id=1, replica_groups=mesh['seq'=16,'tp'=8] {'seq'}, use_global_device_ids=true, to_apply=%region_14.15 | all-reduce | flops 32 | bytes 256 | tf_op jit(solution)/shard_map/psum | solution.py:123
  383.4 104.1 %all-reduce.10.cloned.1.call-done = (f32[32,3584]{1,0:T(8,128)}, f32[32,3584]{1,0:T(8,128)}) async-done(((f32[32,3584]{1,0:T(8,128)}, f32[32,3584]{1,0:T(8,128)}), (f32[32,3584]{1,0:T(8,128)}, f32[32,3584]{1,0:T(8,128)})) %all-reduce.10.cloned.1.call-update) | async-done | bytes 917520 | tf_op jit(solution)/shard_map/psum | solution.py:123
  487.5 3.7 fusion.21
  491.3 69.1 %all-reduce.8.cloned.1.call-done = f32[32,512]{1,0:T(8,128)} async-done(((f32[32,512]{1,0:T(8,128)}), f32[32,512]{1,0:T(8,128)}) %all-reduce.8.cloned.1.call-update) | async-done | bytes 65552 | tf_op jit(solution)/shard_map/psum | solution.py:127
  560.4 1.5 fusion.29
  (192 shorter events, 11.7 us)
Async XLA Ops:
  7.2 1.2 copy-start
  7.2 142.8 %all-reduce.6.cloned.1.call-start = ((), (), s32[]{:S(2)}) async-start(), calls=%async_computation | async-start | bytes 262144 | tf_op jit(solution)/shard_map/psum | solution.py:67
  10.1 477.4 %all-reduce.10.cloned.1.call-start = ((), (), s32[]{:S(2)}) async-start(), calls=%async_computation.2 | async-start | bytes 1835008 | tf_op jit(solution)/shard_map/psum | solution.py:123
  177.2 131.7 %copy-start.2 = (bf16[1024,512]{1,0:T(8,128)(2,1)S(1)}, bf16[1024,512]{1,0:T(8,128)(2,1)}, u32[]{:S(2)}) copy-start(bf16[1024,512]{1,0:T(8,128)(2,1)} %param.23) | copy-start | bytes 3145732
  177.3 159.9 %copy-start.3 = (bf16[32,512]{1,0:T(8,128)(2,1)S(1)}, bf16[32,512]{1,0:T(8,128)(2,1)}, u32[]{:S(2)}) copy-start(bf16[32,512]{1,0:T(8,128)(2,1)} %param.17) | copy-start | bytes 98308
  177.7 1.3 collective-permute-start
  177.7 1.3 collective-permute-start.1
  177.8 2.0 collective-permute-start.2
  180.0 7.4 %collective-permute-start = (f32[1,8,32]{2,1,0:T(8,128)S(1)}, f32[1,8,32]{2,1,0:T(8,128)S(1)}, u32[]{:S(2)}, u32[]{:S(2)}) collective-permute-start(f32[1,8,32]{2,1,0:T(8,128)S(1)} %get-tuple-element.150), channel_id=1, source_target_pairs={{0,8},{8,16},{16,24},{24,32},{32,40},{40,48},{48,56},{56,64},{64,7... | collective-permute-start | bytes 3080 | tf_op jit(solution)/shard_map/while/body/eval_jaxpr/ppermute | solution.py:11
  184.1 3.4 collective-permute-start.1
  184.2 3.6 collective-permute-start.2
  188.0 7.9 %collective-permute-start = (f32[1,8,32]{2,1,0:T(8,128)S(1)}, f32[1,8,32]{2,1,0:T(8,128)S(1)}, u32[]{:S(2)}, u32[]{:S(2)}) collective-permute-start(f32[1,8,32]{2,1,0:T(8,128)S(1)} %get-tuple-element.150), channel_id=1, source_target_pairs={{0,8},{8,16},{16,24},{24,32},{32,40},{40,48},{48,56},{56,64},{64,7... | collective-permute-start | bytes 3080 | tf_op jit(solution)/shard_map/while/body/eval_jaxpr/ppermute | solution.py:11
  190.4 5.5 collective-permute-start.1
  190.5 5.7 %collective-permute-start.2 = (f32[1,8,32,128]{3,2,1,0:T(8,128)S(1)}, f32[1,8,32,128]{3,2,1,0:T(8,128)S(1)}, u32[]{:S(2)}, u32[]{:S(2)}) collective-permute-start(f32[1,8,32,128]{3,2,1,0:T(8,128)S(1)} %get-tuple-element.152), channel_id=1, source_target_pairs={{0,8},{8,16},{16,24},{24,32},{32,40},{40,48},{48,56},{56,64},{64,7... | collective-permute-start | bytes 393224 | tf_op jit(solution)/shard_map/while/body/eval_jaxpr/ppermute | solution.py:11
  196.4 7.9 %collective-permute-start = (f32[1,8,32]{2,1,0:T(8,128)S(1)}, f32[1,8,32]{2,1,0:T(8,128)S(1)}, u32[]{:S(2)}, u32[]{:S(2)}) collective-permute-start(f32[1,8,32]{2,1,0:T(8,128)S(1)} %get-tuple-element.150), channel_id=1, source_target_pairs={{0,8},{8,16},{16,24},{24,32},{32,40},{40,48},{48,56},{56,64},{64,7... | collective-permute-start | bytes 3080 | tf_op jit(solution)/shard_map/while/body/eval_jaxpr/ppermute | solution.py:11
  197.8 6.6 %collective-permute-start.1 = (f32[1,8,32]{2,1,0:T(8,128)S(1)}, f32[1,8,32]{2,1,0:T(8,128)S(1)}, u32[]{:S(2)}, u32[]{:S(2)}) collective-permute-start(f32[1,8,32]{2,1,0:T(8,128)S(1)} %get-tuple-element.151), channel_id=1, source_target_pairs={{0,8},{8,16},{16,24},{24,32},{32,40},{40,48},{48,56},{56,64},{64,7... | collective-permute-start | bytes 3080 | tf_op jit(solution)/shard_map/while/body/eval_jaxpr/ppermute | solution.py:11
  197.9 6.8 %collective-permute-start.2 = (f32[1,8,32,128]{3,2,1,0:T(8,128)S(1)}, f32[1,8,32,128]{3,2,1,0:T(8,128)S(1)}, u32[]{:S(2)}, u32[]{:S(2)}) collective-permute-start(f32[1,8,32,128]{3,2,1,0:T(8,128)S(1)} %get-tuple-element.152), channel_id=1, source_target_pairs={{0,8},{8,16},{16,24},{24,32},{32,40},{40,48},{48,56},{56,64},{64,7... | collective-permute-start | bytes 393224 | tf_op jit(solution)/shard_map/while/body/eval_jaxpr/ppermute | solution.py:11
  204.8 7.9 %collective-permute-start = (f32[1,8,32]{2,1,0:T(8,128)S(1)}, f32[1,8,32]{2,1,0:T(8,128)S(1)}, u32[]{:S(2)}, u32[]{:S(2)}) collective-permute-start(f32[1,8,32]{2,1,0:T(8,128)S(1)} %get-tuple-element.150), channel_id=1, source_target_pairs={{0,8},{8,16},{16,24},{24,32},{32,40},{40,48},{48,56},{56,64},{64,7... | collective-permute-start | bytes 3080 | tf_op jit(solution)/shard_map/while/body/eval_jaxpr/ppermute | solution.py:11
  205.9 7.0 %collective-permute-start.1 = (f32[1,8,32]{2,1,0:T(8,128)S(1)}, f32[1,8,32]{2,1,0:T(8,128)S(1)}, u32[]{:S(2)}, u32[]{:S(2)}) collective-permute-start(f32[1,8,32]{2,1,0:T(8,128)S(1)} %get-tuple-element.151), channel_id=1, source_target_pairs={{0,8},{8,16},{16,24},{24,32},{32,40},{40,48},{48,56},{56,64},{64,7... | collective-permute-start | bytes 3080 | tf_op jit(solution)/shard_map/while/body/eval_jaxpr/ppermute | solution.py:11
  206.6 6.8 %collective-permute-start.2 = (f32[1,8,32,128]{3,2,1,0:T(8,128)S(1)}, f32[1,8,32,128]{3,2,1,0:T(8,128)S(1)}, u32[]{:S(2)}, u32[]{:S(2)}) collective-permute-start(f32[1,8,32,128]{3,2,1,0:T(8,128)S(1)} %get-tuple-element.152), channel_id=1, source_target_pairs={{0,8},{8,16},{16,24},{24,32},{32,40},{40,48},{48,56},{56,64},{64,7... | collective-permute-start | bytes 393224 | tf_op jit(solution)/shard_map/while/body/eval_jaxpr/ppermute | solution.py:11
  213.6 9.9 %collective-permute-start = (f32[1,8,32]{2,1,0:T(8,128)S(1)}, f32[1,8,32]{2,1,0:T(8,128)S(1)}, u32[]{:S(2)}, u32[]{:S(2)}) collective-permute-start(f32[1,8,32]{2,1,0:T(8,128)S(1)} %get-tuple-element.150), channel_id=1, source_target_pairs={{0,8},{8,16},{16,24},{24,32},{32,40},{40,48},{48,56},{56,64},{64,7... | collective-permute-start | bytes 3080 | tf_op jit(solution)/shard_map/while/body/eval_jaxpr/ppermute | solution.py:11
  217.6 5.9 %collective-permute-start.1 = (f32[1,8,32]{2,1,0:T(8,128)S(1)}, f32[1,8,32]{2,1,0:T(8,128)S(1)}, u32[]{:S(2)}, u32[]{:S(2)}) collective-permute-start(f32[1,8,32]{2,1,0:T(8,128)S(1)} %get-tuple-element.151), channel_id=1, source_target_pairs={{0,8},{8,16},{16,24},{24,32},{32,40},{40,48},{48,56},{56,64},{64,7... | collective-permute-start | bytes 3080 | tf_op jit(solution)/shard_map/while/body/eval_jaxpr/ppermute | solution.py:11
  218.7 6.8 %collective-permute-start.2 = (f32[1,8,32,128]{3,2,1,0:T(8,128)S(1)}, f32[1,8,32,128]{3,2,1,0:T(8,128)S(1)}, u32[]{:S(2)}, u32[]{:S(2)}) collective-permute-start(f32[1,8,32,128]{3,2,1,0:T(8,128)S(1)} %get-tuple-element.152), channel_id=1, source_target_pairs={{0,8},{8,16},{16,24},{24,32},{32,40},{40,48},{48,56},{56,64},{64,7... | collective-permute-start | bytes 393224 | tf_op jit(solution)/shard_map/while/body/eval_jaxpr/ppermute | solution.py:11
  225.6 9.3 %collective-permute-start = (f32[1,8,32]{2,1,0:T(8,128)S(1)}, f32[1,8,32]{2,1,0:T(8,128)S(1)}, u32[]{:S(2)}, u32[]{:S(2)}) collective-permute-start(f32[1,8,32]{2,1,0:T(8,128)S(1)} %get-tuple-element.150), channel_id=1, source_target_pairs={{0,8},{8,16},{16,24},{24,32},{32,40},{40,48},{48,56},{56,64},{64,7... | collective-permute-start | bytes 3080 | tf_op jit(solution)/shard_map/while/body/eval_jaxpr/ppermute | solution.py:11
  229.7 5.3 collective-permute-start.1
  230.1 6.8 %collective-permute-start.2 = (f32[1,8,32,128]{3,2,1,0:T(8,128)S(1)}, f32[1,8,32,128]{3,2,1,0:T(8,128)S(1)}, u32[]{:S(2)}, u32[]{:S(2)}) collective-permute-start(f32[1,8,32,128]{3,2,1,0:T(8,128)S(1)} %get-tuple-element.152), channel_id=1, source_target_pairs={{0,8},{8,16},{16,24},{24,32},{32,40},{40,48},{48,56},{56,64},{64,7... | collective-permute-start | bytes 393224 | tf_op jit(solution)/shard_map/while/body/eval_jaxpr/ppermute | solution.py:11
  237.1 6.3 %collective-permute-start = (f32[1,8,32]{2,1,0:T(8,128)S(1)}, f32[1,8,32]{2,1,0:T(8,128)S(1)}, u32[]{:S(2)}, u32[]{:S(2)}) collective-permute-start(f32[1,8,32]{2,1,0:T(8,128)S(1)} %get-tuple-element.150), channel_id=1, source_target_pairs={{0,8},{8,16},{16,24},{24,32},{32,40},{40,48},{48,56},{56,64},{64,7... | collective-permute-start | bytes 3080 | tf_op jit(solution)/shard_map/while/body/eval_jaxpr/ppermute | solution.py:11
  241.1 2.3 collective-permute-start.1
  241.2 4.1 collective-permute-start.2
  245.5 6.3 %collective-permute-start = (f32[1,8,32]{2,1,0:T(8,128)S(1)}, f32[1,8,32]{2,1,0:T(8,128)S(1)}, u32[]{:S(2)}, u32[]{:S(2)}) collective-permute-start(f32[1,8,32]{2,1,0:T(8,128)S(1)} %get-tuple-element.150), channel_id=1, source_target_pairs={{0,8},{8,16},{16,24},{24,32},{32,40},{40,48},{48,56},{56,64},{64,7... | collective-permute-start | bytes 3080 | tf_op jit(solution)/shard_map/while/body/eval_jaxpr/ppermute | solution.py:11
  249.5 2.3 collective-permute-start.1
  249.6 4.1 collective-permute-start.2
  254.0 6.3 %collective-permute-start = (f32[1,8,32]{2,1,0:T(8,128)S(1)}, f32[1,8,32]{2,1,0:T(8,128)S(1)}, u32[]{:S(2)}, u32[]{:S(2)}) collective-permute-start(f32[1,8,32]{2,1,0:T(8,128)S(1)} %get-tuple-element.150), channel_id=1, source_target_pairs={{0,8},{8,16},{16,24},{24,32},{32,40},{40,48},{48,56},{56,64},{64,7... | collective-permute-start | bytes 3080 | tf_op jit(solution)/shard_map/while/body/eval_jaxpr/ppermute | solution.py:11
  258.0 2.3 collective-permute-start.1
  258.1 4.1 collective-permute-start.2
  262.4 6.3 %collective-permute-start = (f32[1,8,32]{2,1,0:T(8,128)S(1)}, f32[1,8,32]{2,1,0:T(8,128)S(1)}, u32[]{:S(2)}, u32[]{:S(2)}) collective-permute-start(f32[1,8,32]{2,1,0:T(8,128)S(1)} %get-tuple-element.150), channel_id=1, source_target_pairs={{0,8},{8,16},{16,24},{24,32},{32,40},{40,48},{48,56},{56,64},{64,7... | collective-permute-start | bytes 3080 | tf_op jit(solution)/shard_map/while/body/eval_jaxpr/ppermute | solution.py:11
  266.4 2.3 collective-permute-start.1
  266.5 4.1 collective-permute-start.2
  270.8 6.3 %collective-permute-start = (f32[1,8,32]{2,1,0:T(8,128)S(1)}, f32[1,8,32]{2,1,0:T(8,128)S(1)}, u32[]{:S(2)}, u32[]{:S(2)}) collective-permute-start(f32[1,8,32]{2,1,0:T(8,128)S(1)} %get-tuple-element.150), channel_id=1, source_target_pairs={{0,8},{8,16},{16,24},{24,32},{32,40},{40,48},{48,56},{56,64},{64,7... | collective-permute-start | bytes 3080 | tf_op jit(solution)/shard_map/while/body/eval_jaxpr/ppermute | solution.py:11
  274.9 2.3 collective-permute-start.1
  274.9 4.1 collective-permute-start.2
  279.3 6.3 %collective-permute-start = (f32[1,8,32]{2,1,0:T(8,128)S(1)}, f32[1,8,32]{2,1,0:T(8,128)S(1)}, u32[]{:S(2)}, u32[]{:S(2)}) collective-permute-start(f32[1,8,32]{2,1,0:T(8,128)S(1)} %get-tuple-element.150), channel_id=1, source_target_pairs={{0,8},{8,16},{16,24},{24,32},{32,40},{40,48},{48,56},{56,64},{64,7... | collective-permute-start | bytes 3080 | tf_op jit(solution)/shard_map/while/body/eval_jaxpr/ppermute | solution.py:11
  283.3 2.3 collective-permute-start.1
  283.4 4.1 collective-permute-start.2
  287.7 7.4 %collective-permute-start = (f32[1,8,32]{2,1,0:T(8,128)S(1)}, f32[1,8,32]{2,1,0:T(8,128)S(1)}, u32[]{:S(2)}, u32[]{:S(2)}) collective-permute-start(f32[1,8,32]{2,1,0:T(8,128)S(1)} %get-tuple-element.150), channel_id=1, source_target_pairs={{0,8},{8,16},{16,24},{24,32},{32,40},{40,48},{48,56},{56,64},{64,7... | collective-permute-start | bytes 3080 | tf_op jit(solution)/shard_map/while/body/eval_jaxpr/ppermute | solution.py:11
  291.7 3.4 collective-permute-start.1
  291.8 5.2 collective-permute-start.2
  297.2 9.3 %collective-permute-start = (f32[1,8,32]{2,1,0:T(8,128)S(1)}, f32[1,8,32]{2,1,0:T(8,128)S(1)}, u32[]{:S(2)}, u32[]{:S(2)}) collective-permute-start(f32[1,8,32]{2,1,0:T(8,128)S(1)} %get-tuple-element.150), channel_id=1, source_target_pairs={{0,8},{8,16},{16,24},{24,32},{32,40},{40,48},{48,56},{56,64},{64,7... | collective-permute-start | bytes 3080 | tf_op jit(solution)/shard_map/while/body/eval_jaxpr/ppermute | solution.py:11
  301.2 5.3 collective-permute-start.1
  301.7 6.8 %collective-permute-start.2 = (f32[1,8,32,128]{3,2,1,0:T(8,128)S(1)}, f32[1,8,32,128]{3,2,1,0:T(8,128)S(1)}, u32[]{:S(2)}, u32[]{:S(2)}) collective-permute-start(f32[1,8,32,128]{3,2,1,0:T(8,128)S(1)} %get-tuple-element.152), channel_id=1, source_target_pairs={{0,8},{8,16},{16,24},{24,32},{32,40},{40,48},{48,56},{56,64},{64,7... | collective-permute-start | bytes 393224 | tf_op jit(solution)/shard_map/while/body/eval_jaxpr/ppermute | solution.py:11
  337.2 5.3 copy-start.4
  337.2 3.7 copy-start.1
  342.5 217.9 %all-reduce.8.cloned.1.call-start = ((), (), s32[]{:S(2)}) async-start(), calls=%async_computation.1 | async-start | bytes 131072 | tf_op jit(solution)/shard_map/psum | solution.py:127
Sparse Core Ops, SparseCore 0:
  10.5 139.5 all-reduce.5
  342.6 144.8 all-reduce.9
  491.4 68.9 all-reduce.7
where the time goes:
time: 573 us; the launch traced here: 568 us
  waiting for transfers between devices  277 us (48%)
  blocking collectives  134 us (23%)
  starting transfers between devices  91.7 us (16%)
  matrix products  31.3 us (5%)
  other arithmetic  17 us (3%)
  between operations  14.6 us (3%)
    psum x1, waiting for transfers between devices, body(): lax.psum((gate_part, up_part, mid_square), 'seq')  104 us
    ppermute x45, starting transfers between devices, shifted(): lax.ppermute(shard, axis, [(i, (i + by) % count) for i in range(count)])  91.6 us
    psum x1, waiting for transfers between devices, body(): down_sum = lax.psum(down_part, 'tp')  69.1 us
    psum x1, waiting for transfers between devices, body(): lax.psum((q_part, k_part, v_part, square_part), 'seq')  68.4 us
    psum x1, blocking collectives, body(): lax.psum((q_part, k_part, v_part, square_part), 'seq')  65.3 us
    psum x1, blocking collectives, body(): lax.psum((gate_part, up_part, mid_square), 'seq')  40.8 us
    ppermute x45, waiting for transfers between devices, shifted(): lax.ppermute(shard, axis, [(i, (i + by) % count) for i in range(count)])  35.5 us
    psum x1, blocking collectives, body(): attn_out = lax.psum(out_part, 'tp').astype(jnp.bfloat16)  27.9 us
  transfers between devices with their start and end apart: 48, of which 28 were waited for; matrix products, arithmetic and copies ran while one was open for 1% of the time, Pallas kernels for 0%

commit v1 on v0

v1 whole, which is shorter than its diff:
```python
import functools

import jax
import jax.numpy as jnp
from jax import lax
from jax.experimental import pallas as pl
from jax.experimental.pallas import tpu as pltpu
from jax.sharding import PartitionSpec as P

EPS = 1e-05
LOW = -1e30
TINY = 1e-30
FULL = 32766.0
F32 = jnp.float32
BF16 = jnp.bfloat16
LANES = 128
CHUNK = 4096
VMEM = pl.BlockSpec(memory_space=pltpu.VMEM)
SMEM = pl.BlockSpec(memory_space=pltpu.SMEM)
HBM = pl.BlockSpec(memory_space=pltpu.HBM)


def call(kernel, out_shape, in_specs, scratch=(), limit=4):
    many = isinstance(out_shape, (tuple, list))
    inner = pl.pallas_call(
        kernel,
        out_shape=out_shape,
        in_specs=in_specs,
        out_specs=[VMEM] * len(out_shape) if many else VMEM,
        scratch_shapes=list(scratch),
        compiler_params=pltpu.CompilerParams(vmem_limit_bytes=limit << 20),
    )

    def run(*args):
        return inner(
            *(pltpu.with_memory_space_constraint(x, pltpu.HBM) if s is HBM else x for x, s in zip(args, in_specs))
        )

    return run


def dot(a, b):
    return jnp.dot(a, b, preferred_element_type=F32)


def dot_t(a, b):
    return lax.dot_general(a, b, (((1,), (1,)), ((), ())), preferred_element_type=F32)


def split2(x):
    high = x.astype(BF16)
    return high, (x - high.astype(F32)).astype(BF16)


def lane_split(square):
    high, low = split2(square)
    lane = lax.broadcasted_iota(jnp.int32, square.shape, 1)
    return jnp.where(lane < LANES // 2, high.astype(F32), low.astype(F32)).astype(BF16)


def lane_join(pair):
    return pair + pltpu.roll(pair, LANES // 2, 1)


def core_index():
    return lax.rem(lax.axis_index("seq"), 2)


def project_kernel(
    resid,
    gain,
    w_query,
    w_key,
    w_value,
    angle,
    keep,
    send,
    cos,
    sin,
    x_buf,
    gain_buf,
    q_buf,
    kv_buf,
    angle_buf,
    sems,
):
    mine = core_index()
    pairs = [
        (angle, angle_buf),
        (resid, x_buf),
        (gain, gain_buf),
        (w_key, kv_buf.at[0]),
        (w_value, kv_buf.at[1]),
        (w_query, q_buf),
    ]
    loads = [pltpu.make_async_copy(src, dst, sems.at[i]) for i, (src, dst) in enumerate(pairs)]
    for load in loads:
        load.start()
    loads[0].wait()
    cosine, sine = jnp.cos(angle_buf[...]), jnp.sin(angle_buf[...])
    cos[...] = jnp.concatenate([cosine, cosine], axis=1)
    sin[...] = jnp.concatenate([-sine, sine], axis=1)
    loads[1].wait()
    loads[2].wait()
    x32 = x_buf[...].astype(F32)
    x = (x32 * gain_buf[...].astype(F32)[None, :]).astype(BF16)
    square = jnp.broadcast_to(jnp.sum(x32 * x32, axis=1, keepdims=True), (32, LANES))
    for load in loads[3:]:
        load.wait()
    for target, half in ((keep, mine), (send, 1 - mine)):
        cols = pl.ds(pl.multiple_of(half * 512, LANES), 512)
        target[:, 0:512] = dot(x, q_buf[:, cols])
        target[:, 512:640] = dot(x, kv_buf[half])
        target[:, 640:768] = square


def project_pair_kernel(own, other, copies):
    total = own[...] + other[...]
    row_log = jnp.log2(total[:, 640:768] + TINY)
    meta = [jnp.floor(row_log * 256 + 0.5)]
    meta.append(jnp.floor((row_log * 256 - meta[0]) * 16384 + 0.5))
    coded = []
    for cols in (slice(0, 512), slice(512, 640)):
        x = total[:, cols]
        grade = jnp.ceil(jnp.log2(jnp.max(jnp.abs(x), axis=1, keepdims=True) + TINY))
        coded.append(jnp.floor(x * (FULL * jnp.exp2(-grade)) + 0.5))
        meta.append(jnp.broadcast_to(grade, (32, LANES)))
    lane = lax.broadcasted_iota(jnp.int32, (32, LANES), 1)
    last = jnp.where(lane < 2, jnp.where(lane == 0, meta[0], meta[1]), jnp.where(lane == 2, meta[2], meta[3]))
    sent = jnp.concatenate(coded + [last], axis=1).astype(jnp.int32).astype(jnp.int16)
    for j in range(8):
        copies[j] = sent


def rotate_kernel(parts, cos, sin, out):
    total = jnp.zeros((32, 640), F32)
    square = jnp.zeros((32, 1), F32)
    for j in range(8):
        part = parts[j].astype(jnp.int32).astype(F32)
        meta = part[:, 640:768]
        square += jnp.exp2(meta[:, 0:1] / 256 + meta[:, 1:2] / (256 * 16384))
        step = jnp.exp2(meta) / FULL
        total += jnp.concatenate([part[:, 0:512] * step[:, 2:3], part[:, 512:640] * step[:, 3:4]], axis=1)
    total = total * lax.rsqrt(square / 8192 + EPS)
    turned = []
    for g in range(5):
        x = total[:, g * 128 : (g + 1) * 128]
        turned.append(x * cos[...] + pltpu.roll(x, LANES // 2, 1) * sin[...])
    last = jnp.where(core_index() == 0, turned[4], total[:, 512:640])
    for g, x in enumerate(turned[:4] + [last]):
        out[g * 32 : (g + 1) * 32, :] = x.astype(BF16)


def fold(x, op):
    out = x[:, 0:LANES]
    for i in range(1, x.shape[1] // LANES):
        out = op(out, x[:, i * LANES : (i + 1) * LANES])
    return out


def attend_kernel(
    own, other, positions, valid, keys, values, keep, send, query, scores, acc, o_acc, v_buf, v_sem
):
    scale = 128.0**-0.5
    power = scale * 1.4426950408889634
    mine = core_index()
    length = valid[0]
    whole = lax.div(length, CHUNK)
    used = lax.div(length + (CHUNK - 1), CHUNK)

    def load(c):
        rows = pl.ds(pl.multiple_of(c * CHUNK, CHUNK), CHUNK)
        return pltpu.make_async_copy(values.at[0, rows, :], v_buf.at[rows, :], v_sem.at[c])

    @pl.loop(0, used)
    def _(c):
        load(c).start()

    row = lax.broadcasted_iota(jnp.int32, (32, LANES), 0)
    lane = lax.broadcasted_iota(jnp.int32, (32, LANES), 1)
    of_row = jnp.zeros((32, LANES), jnp.int32)
    of_lane = jnp.full((32, LANES), 1 << 20, jnp.int32)
    for i in range(32):
        of_row = jnp.where(row == i, positions[i], of_row)
        of_lane = jnp.where(lane == i, positions[i], of_lane)
    allowed = (of_lane <= of_row) & (lax.axis_index("seq") == 0)
    query[pl.ds(pl.multiple_of(mine * 128, 128), 128), :] = own[0:128, :]
    query[pl.ds(pl.multiple_of((1 - mine) * 128, 128), 128), :] = other[0:128, :]
    q = query[...]
    pad = jnp.zeros((96, LANES), BF16)
    a, b = own[128:160, :].astype(F32), other[128:160, :].astype(F32)
    k_new = jnp.concatenate([jnp.where(mine == 0, a, b).astype(BF16), pad], axis=0)
    v_new = jnp.concatenate([jnp.where(mine == 0, b, a).astype(BF16), pad], axis=0)

    def score(c):
        rows = pl.ds(pl.multiple_of(c * CHUNK, CHUNK), CHUNK)
        return dot_t(q, keys[0, rows, :])

    acc[...] = jnp.full((256, LANES), LOW, F32)

    @pl.loop(0, whole)
    def _(c):
        s = score(c)
        scores[c] = s
        acc[...] = jnp.maximum(acc[...], fold(s, jnp.maximum))

    @pl.when(used > whole)
    def _():
        slot = lax.broadcasted_iota(jnp.int32, (256, CHUNK), 1) + whole * CHUNK
        s = jnp.where(slot < length, score(whole), LOW)
        scores[whole] = s
        acc[...] = jnp.maximum(acc[...], fold(s, jnp.maximum))

    top = jnp.max(acc[...], axis=1, keepdims=True)
    shift = top * power
    acc[...] = jnp.zeros((256, LANES), F32)
    o_acc[...] = jnp.zeros((256, LANES), F32)

    @pl.loop(0, used)
    def _(c):
        rows = pl.ds(pl.multiple_of(c * CHUNK, CHUNK), CHUNK)
        e = jnp.exp2(scores[c] * power - shift).astype(BF16)
        acc[...] += fold(e.astype(F32), jnp.add)
        load(c).wait()
        o_acc[...] += dot(e, v_buf[rows, :])

    total_l = jnp.sum(acc[...], axis=1, keepdims=True)
    lse = top * scale + jnp.log(total_l)
    summed = o_acc[...] / total_l

    hold = jnp.concatenate([jnp.where(allowed, 0.0, -1.0)] * 8, axis=0)
    s_new = jnp.where(hold < 0, LOW, dot_t(q, k_new) * scale)
    top_new = jnp.max(s_new, axis=1, keepdims=True)
    e_new = jnp.exp(s_new - top_new).astype(BF16)
    l_new = jnp.sum(e_new.astype(F32), axis=1, keepdims=True)
    o_new = dot(e_new, v_new) / l_new
    lse_new = top_new + jnp.log(l_new)

    high = jnp.maximum(lse, lse_new)
    f_old = jnp.exp(lse - high)
    f_new = jnp.exp(lse_new - high)
    both = f_old + f_new
    o_acc[...] = (summed * f_old + o_new * f_new) / both
    acc[...] = jnp.broadcast_to(high + jnp.log(both), (256, LANES))
    for target, half in ((keep, mine), (send, 1 - mine)):
        rows = pl.ds(pl.multiple_of(half * 128, 128), 128)
        target[0:128, :] = o_acc[rows, :]
        target[128:256, :] = acc[rows, :]


def merge_pair_kernel(own, other, copies):
    la, lb = own[128:256, :], other[128:256, :]
    high = jnp.maximum(la, lb)
    fa, fb = jnp.exp(la - high), jnp.exp(lb - high)
    both = fa + fb
    o = ((own[0:128, :] * fa + other[0:128, :] * fb) / both).astype(BF16)
    lanes = jnp.transpose(high + jnp.log(both))[0:8]
    row = lax.broadcasted_iota(jnp.int32, (8, LANES), 0)
    p0 = lanes.astype(BF16).astype(F32)
    rest = lanes - p0
    p1 = rest.astype(BF16).astype(F32)
    p2 = rest - p1
    tail = jnp.where(row == 0, p0, jnp.where(row == 1, p1, p2))
    tail = jnp.concatenate([tail, jnp.zeros((8, LANES), F32)], axis=0).astype(BF16)
    for j in range(8):
        copies[j, 0:128, :] = o
        copies[j, 128:144, :] = tail


def merge_kernel(parts, attn):
    rows = []
    for j in range(8):
        tail = parts[j, 128:144, :].astype(F32)
        rows.append(tail[0:1] + tail[1:2] + tail[2:3])
    lse = jnp.concatenate(rows, axis=0)
    weight = jnp.exp(lse - jnp.max(lse, axis=0, keepdims=True))
    weight = weight / jnp.sum(weight, axis=0, keepdims=True)
    weight = jnp.transpose(jnp.concatenate([weight, jnp.zeros((120, LANES), F32)], axis=0))
    total = parts[0, 0:128, :].astype(F32) * weight[:, 0:1]
    for j in range(1, 8):
        total += parts[j, 0:128, :].astype(F32) * weight[:, j : j + 1]
    for g in range(4):
        attn[:, g * 128 : (g + 1) * 128] = total[g * 32 : (g + 1) * 32].astype(BF16)


def out_kernel(own, other, w_out, copies):
    mine = core_index()
    total = jnp.zeros((32, 512), F32)
    for source, half in ((own, mine), (other, 1 - mine)):
        total += dot(source[...], w_out[pl.ds(pl.multiple_of(half * 512, LANES), 512), :])
    part = total.astype(BF16)
    for j in range(8):
        copies[j] = part


def sum_parts(parts):
    total = parts[0].astype(F32)
    for j in range(1, 8):
        total = total + parts[j].astype(F32)
    return total


def gate_up_kernel(parts, resid, gain, w_gate, w_up, attn_out, mid, keep, send):
    branch = sum_parts(parts).astype(BF16)
    attn_out[...] = branch
    hidden = (resid[...].astype(F32) + branch.astype(F32)).astype(BF16)
    mid[...] = hidden
    x32 = hidden.astype(F32)
    x = (x32 * gain[...].astype(F32)[None, :]).astype(BF16)
    square = jnp.broadcast_to(jnp.sum(x32 * x32, axis=1, keepdims=True), (32, LANES))
    mine = core_index()
    for target, half in ((keep, mine), (send, 1 - mine)):
        for i in range(2):
            cols = pl.ds(pl.multiple_of(half * 1792 + i * 896, LANES), 896)
            target[:, i * 896 : (i + 1) * 896] = dot(x, w_gate[:, cols]).astype(target.dtype)
            target[:, 1792 + i * 896 : 1792 + (i + 1) * 896] = dot(x, w_up[:, cols]).astype(target.dtype)
    keep[:, 3584:3712] = square
    send[:, 3584:3712] = lane_split(square)


def gate_up_pair_kernel(keep, got, pieces):
    square = keep[:, 3584:3712] + lane_join(got[:, 3584:3712].astype(F32))
    high = square.astype(BF16).astype(F32)
    low = square - high
    for j in range(8):
        rows = slice((j // 2) * 8, (j // 2) * 8 + 8)
        block = []
        for base in (0, 1792):
            cols = slice(base + (j % 2) * 896, base + (j % 2 + 1) * 896)
            block.append(keep[rows, cols] + got[:, cols].astype(F32)[rows])
        pieces[j, :, 0:896] = jnp.concatenate(block, axis=0).astype(BF16)
        pieces[j, :, 896:1024] = jnp.concatenate([high[rows], low[rows]], axis=0).astype(BF16)


def act_kernel(parts, copies):
    total = sum_parts(parts)
    square = (total[0:8] + total[8:16])[:, 896:897]
    inv = lax.rsqrt(square / 8192 + EPS)
    gate = total[0:8, 0:896] * inv
    up = total[8:16, 0:896] * inv
    act = gate / (1.0 + jnp.exp(-gate)) * up
    packed = jnp.concatenate(
        [act[:, 0:512], jnp.concatenate([act[:, 512:896], jnp.zeros((8, LANES), F32)], axis=1)], axis=0
    ).astype(BF16)
    for j in range(8):
        copies[j] = packed


def down_kernel(own, other, w_down, copies):
    total = jnp.zeros((32, 512), F32)
    mine = core_index()
    for source, half in ((own, mine), (other, 1 - mine)):
        for ch in range(2):
            wide = []
            for rg in range(4):
                piece = source[rg * 2 + ch].astype(F32)
                wide.append(jnp.concatenate([piece[0:8], piece[8:16, 0:384]], axis=1))
            act = jnp.concatenate(wide, axis=0).astype(BF16)
            rows = pl.ds(pl.multiple_of(half * 1792 + ch * 896, LANES), 896)
            total += dot(act, w_down[rows, :])
    part = total.astype(BF16)
    for j in range(8):
        copies[j] = part


def final_kernel(parts, mid, layer_out):
    layer_out[...] = (mid[...].astype(F32) + sum_parts(parts)).astype(BF16)


def body(
    resid,
    attn_gain,
    ffn_gain,
    w_query,
    w_key,
    w_value,
    w_out,
    rope_angle,
    positions,
    cache_keys,
    cache_values,
    valid_lengths,
    w_gate,
    w_up,
    w_down,
):
    shape = jax.ShapeDtypeStruct
    near = pltpu.VMEM
    same_core = [[2 * j + c for j in range(8)] for c in range(2)]
    swap = [(i, i ^ 1) for i in range(16)]

    def to_other_core(x):
        return lax.ppermute(x, "seq", swap)

    def over_chips(x):
        return lax.all_to_all(x, "seq", 0, 0, axis_index_groups=same_core)

    def over_tp(x):
        return lax.all_to_all(x, "tp", 0, 0)

    table = near((32, LANES), F32)
    keep, send, cos, sin = call(
        project_kernel,
        (near((32, 768), F32), near((32, 768), F32), table, table),
        [HBM] * 6,
        scratch=[
            pltpu.VMEM((32, 512), BF16),
            pltpu.VMEM((512,), BF16),
            pltpu.VMEM((512, 1024), BF16),
            pltpu.VMEM((2, 512, LANES), BF16),
            pltpu.VMEM((32, 64), F32),
            pltpu.SemaphoreType.DMA((6,)),
        ],
    )(resid, attn_gain, w_query, w_key, w_value, rope_angle)
    copies = call(project_pair_kernel, near((8, 32, 768), jnp.int16), [VMEM] * 2)(keep, to_other_core(send))
    turned = call(rotate_kernel, near((160, LANES), BF16), [VMEM] * 3)(over_chips(copies), cos, sin)

    chunks = 16384 // CHUNK
    keep, send = call(
        attend_kernel,
        (near((256, LANES), F32), near((256, LANES), F32)),
        [VMEM] * 2 + [SMEM] * 2 + [VMEM, HBM],
        scratch=[
            pltpu.VMEM((256, LANES), BF16),
            pltpu.VMEM((chunks, 256, CHUNK), F32),
            pltpu.VMEM((256, LANES), F32),
            pltpu.VMEM((256, LANES), F32),
            pltpu.VMEM((16384, LANES), BF16),
            pltpu.SemaphoreType.DMA((chunks,)),
        ],
        limit=30,
    )(turned, to_other_core(turned), positions, valid_lengths, cache_keys, cache_values)
    copies = call(merge_pair_kernel, near((8, 144, LANES), BF16), [VMEM] * 2)(keep, to_other_core(send))
    attn = call(merge_kernel, near((32, 512), BF16), [VMEM])(over_chips(copies))
    copies = call(out_kernel, near((8, 32, 512), BF16), [VMEM] * 3)(attn, to_other_core(attn), w_out)
    parts = over_tp(copies)

    attn_out, mid, keep, send = call(
        gate_up_kernel,
        (shape((32, 512), BF16), near((32, 512), BF16), near((32, 3712), F32), near((32, 3712), BF16)),
        [VMEM] * 5,
        limit=12,
    )(parts, resid, ffn_gain, w_gate, w_up)
    pieces = call(gate_up_pair_kernel, near((8, 16, 1024), BF16), [VMEM] * 2)(keep, to_other_core(send))
    parts = over_chips(pieces)
    copies = call(act_kernel, near((8, 16, 512), BF16), [VMEM])(parts)
    acts = over_chips(copies)
    copies = call(down_kernel, near((8, 32, 512), BF16), [VMEM] * 3, limit=8)(acts, to_other_core(acts), w_down)
    parts = over_tp(copies)
    layer_out = call(final_kernel, shape((32, 512), BF16), [VMEM] * 2)(parts, mid)
    return (attn_out, layer_out)


def solution(mesh):
    in_specs = (
        P(None, "seq"),
        P("seq"),
        P("seq"),
        P("seq", "tp"),
        P("seq", "tp"),
        P("seq", "tp"),
        P("tp", "seq"),
        P(),
        P(),
        P("tp", "seq", None),
        P("tp", "seq", None),
        P("seq"),
        P("seq", "tp"),
        P("seq", "tp"),
        P("tp", "seq"),
    )
    out_specs = (P(None, "seq"), P(None, "seq"))
    return jax.shard_map(body, mesh=mesh, in_specs=in_specs, out_specs=out_specs, check_vma=False)
```

time: 573 us -> 105 us (0.18)
  waiting for transfers between devices: 277 us -> 5.14 us
  starting transfers between devices: 91.7 us -> 9.69 us
  blocking collectives: 134 us -> 70.4 us
  matrix products: 31.3 us -> 0 us
  other arithmetic: 17 us -> 0 us
  Pallas kernels: 0 us -> 14.6 us
  between operations: 14.6 us -> 1.38 us
    psum x3 -> x0, waiting for transfers between devices: 242 us -> none  [the longest x1 104 us: body(): lax.psum((gate_part, up_part, mid_square), 'seq')]
    psum x3 -> x0, blocking collectives: 134 us -> none  [the longest x1 65.3 us: body(): lax.psum((q_part, k_part, v_part, square_part), 'seq')]
    ppermute x45 -> x6, starting transfers between devices: 91.6 us -> 9.69 us  [to_other_core(): return lax.ppermute(x, 'seq', swap)]
    all_to_all x0 -> x6, blocking collectives: none -> 70.4 us  [the longest x4 49.4 us: over_chips(): return lax.all_to_all(x, 'seq', 0, 0, axis_index_groups=same_core)]
    dot_general x11 -> x0, matrix products: 31.3 us -> none  [the longest x1 9.27 us: body(): jnp.einsum('rkgd,ktd->kgrt', grouped, cache_keys, preferred_element_type=...]
    ppermute x45 -> x6, waiting for transfers between devices: 35.5 us -> 5.14 us  [to_other_core(): return lax.ppermute(x, 'seq', swap)]
    pallas_call x0 -> x12, Pallas kernels: none -> 14.6 us  [run(): inner(*(pltpu.with_memory_space_constraint(x, pltpu.HBM) if s is HBM else...]
    reduce_sum x4 -> x0, other arithmetic: 9.17 us -> none  [the longest x1 8.14 us: body(): total = jnp.sum(weights.astype(jnp.float32), axis=-1)]
  transfers between devices with their start and end apart: 48 -> 6, of which waited for: 28 -> 6; matrix products, arithmetic and copies ran while one was open for 1% -> 0% of each run, Pallas kernels for 0% -> 0%
where the time goes in v1:
time: 105 us; the launch traced here: 104 us
  blocking collectives  70.4 us (67%)
  Pallas kernels  14.6 us (14%)
  starting transfers between devices  9.69 us (9%)
  waiting for transfers between devices  5.14 us (5%)
  local copies, waits for them, and re-layouts  2.87 us (3%)
  between operations  1.38 us (1%)
    all_to_all x4, blocking collectives, over_chips(): return lax.all_to_all(x, 'seq', 0, 0, axis_index_groups=same_core)  49.4 us
    all_to_all x2, blocking collectives, over_tp(): return lax.all_to_all(x, 'tp', 0, 0)  21 us
    pallas_call x12, Pallas kernels, run(): inner(*(pltpu.with_memory_space_constraint(x, pltpu.HBM) if s is HBM else...  14.6 us
    ppermute x6, starting transfers between devices, to_other_core(): return lax.ppermute(x, 'seq', swap)  9.69 us
    ppermute x6, waiting for transfers between devices, to_other_core(): return lax.ppermute(x, 'seq', swap)  5.14 us
    unnamed x16, local copies, waits for them, and re-layouts  2.87 us
  transfers between devices with their start and end apart: 6, of which 6 were waited for; matrix products, arithmetic and copies ran while one was open for 0% of the time, Pallas kernels for 0%

profile of v1, /device:TPU:1, one launch (start us, length us, event | category | flops | bytes accessed | tf_op | source)
XLA Modules:
  0.0 104.1 jit_solution(5654211105756634947)
XLA Ops:
  0.6 1.8 %shard_map.158 = (f32[32,768]{1,0:T(8,128)S(1)}, f32[32,768]{1,0:T(8,128)S(1)}, f32[32,128]{1,0:T(8,128)S(1)}, f32[32,128]{1,0:T(8,128)S(1)}) custom-call(bf16[32,512]{1,0:T(8,128)(2,1)} %resid.3, bf16[512]{0:T(512)(128)(2,1)} %gain.2, bf16[512,1024]{1,0:T(8,128)(2,1)} %w_query.1, bf16[512,128]{1,0:T(8,128)(2,1)} %w_key.1, bf16[512,128]{1,0:T(8,128)(2,1)} %w_value.1, ...), custom_call_target="tpu_custom_call" | custom-call | tf_op jit(solution)/shard_map/pallas_call | solution.py:35
  2.4 1.5 %collective-permute-start = (f32[32,768]{1,0:T(8,128)S(1)}, f32[32,768]{1,0:T(8,128)S(1)}, u32[]{:S(2)}, u32[]{:S(2)}) collective-permute-start(f32[32,768]{1,0:T(8,128)S(1)} %get-tuple-element.13), channel_id=1, source_target_pairs={{0,8},{8,0},{16,24},{24,16},{32,40},{40,32},{48,56},{56,48},{64,72... | collective-permute-start | bytes 294920 | tf_op jit(solution)/shard_map/ppermute | solution.py:393
  4.0 0.9 collective-permute-done.other
  4.9 0.1 shard_map.159
  5.0 15.9 %all_to_all.30.parts = s16[8,32,768]{2,1,0:T(8,128)(2,1)S(1)} all-to-all(s16[8,32,768]{2,1,0:T(8,128)(2,1)S(1)} %shard_map.159), channel_id=1, replica_groups={{0,16,32,48,64,80,96,112},{8,24,40,56,72,88,104,120},{1,17,33,49,65,81,..., dimensions={0} | all-to-all | bytes 786432 | tf_op jit(solution)/shard_map/all_to_all | solution.py:396
  20.9 0.3 shard_map.160.own
  21.2 2.0 %collective-permute-start.1 = (bf16[160,128]{1,0:T(8,128)(2,1)S(1)}, bf16[160,128]{1,0:T(8,128)(2,1)S(1)}, u32[]{:S(2)}, u32[]{:S(2)}) collective-permute-start(bf16[160,128]{1,0:T(8,128)(2,1)S(1)} %shard_map.160.own), channel_id=1, source_target_pairs={{0,8},{8,0},{16,24},{24,16},{32,40},{40,32},{48,56},{56,48},{64,72... | collective-permute-start | bytes 122888 | tf_op jit(solution)/shard_map/ppermute | solution.py:393
  23.9 0.2 collective-permute-done.1.other
  24.1 0.0 copy-start
  24.1 2.2 %copy-done = bf16[1,16384,128]{2,1,0:T(8,128)(2,1)S(1)} copy-done((bf16[1,16384,128]{2,1,0:T(8,128)(2,1)S(1)}, bf16[1,16384,128]{2,1,0:T(8,128)(2,1)}, u32[]{:S(2)}) %copy-start) | copy-done | bytes 4194328
  26.3 0.0 copy-start.7
  26.3 0.7 copy-done.7
  26.9 0.0 copy-start.4
  26.9 0.0 copy-start.1
  26.9 0.0 copy-start.2
  26.9 0.0 copy-start.5
  26.9 0.0 copy-start.6
  27.0 8.2 %shard_map.161 = (f32[256,128]{1,0:T(8,128)S(1)}, f32[256,128]{1,0:T(8,128)S(1)}) custom-call(bf16[160,128]{1,0:T(8,128)(2,1)S(1)} %shard_map.160.own, bf16[160,128]{1,0:T(8,128)(2,1)S(1)} %collective-permute-done.1.other, s32[32]{0:T(128)S(1)} %copy-done.7, s32[1]{0:T(128)S(6)} %copy.17.valid, bf16[1,16384,128]{2,1,0:T(8,128)(2,1)S(1)} %copy-done, ...), custom_call_target="tpu_custom_call" | custom-call | tf_op jit(solution)/shard_map/pallas_call | solution.py:35
  35.1 0.4 collective-permute-start.2
  35.5 1.0 collective-permute-done.2.other
  36.5 0.1 shard_map.162
  36.6 13.0 %all_to_all.31.parts = bf16[8,144,128]{2,1,0:T(8,128)(2,1)S(1)} all-to-all(bf16[8,144,128]{2,1,0:T(8,128)(2,1)S(1)} %shard_map.162), channel_id=1, replica_groups={{0,16,32,48,64,80,96,112},{8,24,40,56,72,88,104,120},{1,17,33,49,65,81,..., dimensions={0} | all-to-all | bytes 589824 | tf_op jit(solution)/shard_map/all_to_all | solution.py:396
  49.6 0.4 shard_map.163.own
  50.0 1.7 %collective-permute-start.3 = (bf16[32,512]{1,0:T(8,128)(2,1)S(1)}, bf16[32,512]{1,0:T(8,128)(2,1)S(1)}, u32[]{:S(2)}, u32[]{:S(2)}) collective-permute-start(bf16[32,512]{1,0:T(8,128)(2,1)S(1)} %shard_map.163.own), channel_id=1, source_target_pairs={{0,8},{8,0},{16,24},{24,16},{32,40},{40,32},{48,56},{56,48},{64,72... | collective-permute-start | bytes 98312 | tf_op jit(solution)/shard_map/ppermute | solution.py:393
  51.7 0.9 collective-permute-done.3.other
  52.5 0.0 copy-done.4
  52.5 0.3 shard_map.164
  52.8 11.6 %all_to_all.32.parts = bf16[8,32,512]{2,1,0:T(8,128)(2,1)S(1)} all-to-all(bf16[8,32,512]{2,1,0:T(8,128)(2,1)S(1)} %shard_map.164), channel_id=1, replica_groups=mesh['seq'=16,'tp'=8] {'tp'}, dimensions={0} | all-to-all | bytes 524288 | tf_op jit(solution)/shard_map/all_to_all | solution.py:399
  64.4 0.0 copy-done.1
  64.4 0.0 copy-done.2
  64.4 0.0 copy-done.5
  64.4 0.0 copy-done.6
  64.4 0.0 copy-start.3
  64.4 1.8 %shard_map.165 = (bf16[32,512]{1,0:T(8,128)(2,1)}, bf16[32,512]{1,0:T(8,128)(2,1)S(1)}, f32[32,3712]{1,0:T(8,128)S(1)}, bf16[32,3712]{1,0:T(8,128)(2,1)S(1)}) custom-call(bf16[8,32,512]{2,1,0:T(8,128)(2,1)S(1)} %all_to_all.32.parts, bf16[32,512]{1,0:T(8,128)(2,1)S(1)} %copy-done.5, bf16[512]{0:T(512)(128)(2,1)S(1)} %copy-done.6, ...), custom_call_target="tpu_custom_call" | custom-call | tf_op jit(solution)/shard_map/pallas_call | solution.py:35
  66.3 1.5 %collective-permute-start.4 = (bf16[32,3712]{1,0:T(8,128)(2,1)S(1)}, bf16[32,3712]{1,0:T(8,128)(2,1)S(1)}, u32[]{:S(2)}, u32[]{:S(2)}) collective-permute-start(bf16[32,3712]{1,0:T(8,128)(2,1)S(1)} %get-tuple-element.20), channel_id=1, source_target_pairs={{0,8},{8,0},{16,24},{24,16},{32,40},{40,32},{48,56},{56,48},{64,72... | collective-permute-start | bytes 712712 | tf_op jit(solution)/shard_map/ppermute | solution.py:393
  67.8 1.1 %collective-permute-done.4.got = bf16[32,3712]{1,0:T(8,128)(2,1)S(1)} collective-permute-done((bf16[32,3712]{1,0:T(8,128)(2,1)S(1)}, bf16[32,3712]{1,0:T(8,128)(2,1)S(1)}, u32[]{:S(2)}, u32[]{:S(2)}) %collective-permute-start.4) | collective-permute-done | bytes 237600 | tf_op jit(solution)/shard_map/ppermute | solution.py:393
  68.9 0.1 shard_map.166
  69.0 10.6 %all_to_all.33.parts = bf16[8,16,1024]{2,1,0:T(8,128)(2,1)S(1)} all-to-all(bf16[8,16,1024]{2,1,0:T(8,128)(2,1)S(1)} %shard_map.166), channel_id=1, replica_groups={{0,16,32,48,64,80,96,112},{8,24,40,56,72,88,104,120},{1,17,33,49,65,81,..., dimensions={0} | all-to-all | bytes 524288 | tf_op jit(solution)/shard_map/all_to_all | solution.py:396
  79.5 0.1 shard_map.167
  79.7 10.0 %all_to_all.34.own = bf16[8,16,512]{2,1,0:T(8,128)(2,1)S(1)} all-to-all(bf16[8,16,512]{2,1,0:T(8,128)(2,1)S(1)} %shard_map.167), channel_id=1, replica_groups={{0,16,32,48,64,80,96,112},{8,24,40,56,72,88,104,120},{1,17,33,49,65,81,..., dimensions={0} | all-to-all | bytes 262144 | tf_op jit(solution)/shard_map/all_to_all | solution.py:396
  89.6 2.6 %collective-permute-start.5 = (bf16[8,16,512]{2,1,0:T(8,128)(2,1)S(1)}, bf16[8,16,512]{2,1,0:T(8,128)(2,1)S(1)}, u32[]{:S(2)}, u32[]{:S(2)}) collective-permute-start(bf16[8,16,512]{2,1,0:T(8,128)(2,1)S(1)} %all_to_all.34.own), channel_id=1, source_target_pairs={{0,8},{8,0},{16,24},{24,16},{32,40},{40,32},{48,56},{56,48},{64,72... | collective-permute-start | bytes 393224 | tf_op jit(solution)/shard_map/ppermute | solution.py:393
  92.2 1.0 collective-permute-done.5.other
  93.2 0.0 copy-done.3
  93.2 0.8 shard_map.168
  94.0 9.5 %all_to_all.35.parts = bf16[8,32,512]{2,1,0:T(8,128)(2,1)S(1)} all-to-all(bf16[8,32,512]{2,1,0:T(8,128)(2,1)S(1)} %shard_map.168), channel_id=1, replica_groups=mesh['seq'=16,'tp'=8] {'tp'}, dimensions={0} | all-to-all | bytes 524288 | tf_op jit(solution)/shard_map/all_to_all | solution.py:399
  103.4 0.7 shard_map.169
Async XLA Ops:
  2.4 2.4 %collective-permute-start = (f32[32,768]{1,0:T(8,128)S(1)}, f32[32,768]{1,0:T(8,128)S(1)}, u32[]{:S(2)}, u32[]{:S(2)}) collective-permute-start(f32[32,768]{1,0:T(8,128)S(1)} %get-tuple-element.13), channel_id=1, source_target_pairs={{0,8},{8,0},{16,24},{24,16},{32,40},{40,32},{48,56},{56,48},{64,72... | collective-permute-start | bytes 294920 | tf_op jit(solution)/shard_map/ppermute | solution.py:393
  21.2 2.9 %collective-permute-start.1 = (bf16[160,128]{1,0:T(8,128)(2,1)S(1)}, bf16[160,128]{1,0:T(8,128)(2,1)S(1)}, u32[]{:S(2)}, u32[]{:S(2)}) collective-permute-start(bf16[160,128]{1,0:T(8,128)(2,1)S(1)} %shard_map.160.own), channel_id=1, source_target_pairs={{0,8},{8,0},{16,24},{24,16},{32,40},{40,32},{48,56},{56,48},{64,72... | collective-permute-start | bytes 122888 | tf_op jit(solution)/shard_map/ppermute | solution.py:393
  24.1 2.2 %copy-start = (bf16[1,16384,128]{2,1,0:T(8,128)(2,1)S(1)}, bf16[1,16384,128]{2,1,0:T(8,128)(2,1)}, u32[]{:S(2)}) copy-start(bf16[1,16384,128]{2,1,0:T(8,128)(2,1)} %keys.1) | copy-start | bytes 12582916
  26.3 0.7 copy-start.7
  26.9 25.6 %copy-start.4 = (bf16[1024,512]{1,0:T(8,128)(2,1)S(1)}, bf16[1024,512]{1,0:T(8,128)(2,1)}, u32[]{:S(2)}) copy-start(bf16[1024,512]{1,0:T(8,128)(2,1)} %w_out.1) | copy-start | bytes 3145732
  26.9 37.5 %copy-start.1 = (bf16[512,3584]{1,0:T(8,128)(2,1)S(1)}, bf16[512,3584]{1,0:T(8,128)(2,1)}, u32[]{:S(2)}) copy-start(bf16[512,3584]{1,0:T(8,128)(2,1)} %w_gate.1) | copy-start | bytes 11010052
  26.9 37.5 %copy-start.2 = (bf16[512,3584]{1,0:T(8,128)(2,1)S(1)}, bf16[512,3584]{1,0:T(8,128)(2,1)}, u32[]{:S(2)}) copy-start(bf16[512,3584]{1,0:T(8,128)(2,1)} %w_up.1) | copy-start | bytes 11010052
  26.9 37.5 %copy-start.5 = (bf16[32,512]{1,0:T(8,128)(2,1)S(1)}, bf16[32,512]{1,0:T(8,128)(2,1)}, u32[]{:S(2)}) copy-start(bf16[32,512]{1,0:T(8,128)(2,1)} %resid.3) | copy-start | bytes 98308
  26.9 37.5 %copy-start.6 = (bf16[512]{0:T(512)(128)(2,1)S(1)}, bf16[512]{0:T(512)(128)(2,1)}, u32[]{:S(2)}) copy-start(bf16[512]{0:T(512)(128)(2,1)} %gain.3) | copy-start | bytes 3076
  35.1 1.4 %collective-permute-start.2 = (f32[256,128]{1,0:T(8,128)S(1)}, f32[256,128]{1,0:T(8,128)S(1)}, u32[]{:S(2)}, u32[]{:S(2)}) collective-permute-start(f32[256,128]{1,0:T(8,128)S(1)} %get-tuple-element.17), channel_id=1, source_target_pairs={{0,8},{8,0},{16,24},{24,16},{32,40},{40,32},{48,56},{56,48},{64,72... | collective-permute-start | bytes 393224 | tf_op jit(solution)/shard_map/ppermute | solution.py:393
  50.0 2.5 %collective-permute-start.3 = (bf16[32,512]{1,0:T(8,128)(2,1)S(1)}, bf16[32,512]{1,0:T(8,128)(2,1)S(1)}, u32[]{:S(2)}, u32[]{:S(2)}) collective-permute-start(bf16[32,512]{1,0:T(8,128)(2,1)S(1)} %shard_map.163.own), channel_id=1, source_target_pairs={{0,8},{8,0},{16,24},{24,16},{32,40},{40,32},{48,56},{56,48},{64,72... | collective-permute-start | bytes 98312 | tf_op jit(solution)/shard_map/ppermute | solution.py:393
  64.4 28.8 %copy-start.3 = (bf16[3584,512]{1,0:T(8,128)(2,1)S(1)}, bf16[3584,512]{1,0:T(8,128)(2,1)}, u32[]{:S(2)}) copy-start(bf16[3584,512]{1,0:T(8,128)(2,1)} %w_down.1) | copy-start | bytes 11010052
  66.3 2.6 %collective-permute-start.4 = (bf16[32,3712]{1,0:T(8,128)(2,1)S(1)}, bf16[32,3712]{1,0:T(8,128)(2,1)S(1)}, u32[]{:S(2)}, u32[]{:S(2)}) collective-permute-start(bf16[32,3712]{1,0:T(8,128)(2,1)S(1)} %get-tuple-element.20), channel_id=1, source_target_pairs={{0,8},{8,0},{16,24},{24,16},{32,40},{40,32},{48,56},{56,48},{64,72... | collective-permute-start | bytes 712712 | tf_op jit(solution)/shard_map/ppermute | solution.py:393
  89.6 3.6 %collective-permute-start.5 = (bf16[8,16,512]{2,1,0:T(8,128)(2,1)S(1)}, bf16[8,16,512]{2,1,0:T(8,128)(2,1)S(1)}, u32[]{:S(2)}, u32[]{:S(2)}) collective-permute-start(bf16[8,16,512]{2,1,0:T(8,128)(2,1)S(1)} %all_to_all.34.own), channel_id=1, source_target_pairs={{0,8},{8,0},{16,24},{24,16},{32,40},{40,32},{48,56},{56,48},{64,72... | collective-permute-start | bytes 393224 | tf_op jit(solution)/shard_map/ppermute | solution.py:393

commit v2 on v1

--- a/solution.py
+++ b/solution.py
@@ -1,4 +1,5 @@
 import functools
+import math
 
 import jax
 import jax.numpy as jnp
@@ -14,13 +15,14 @@
 F32 = jnp.float32
 BF16 = jnp.bfloat16
 LANES = 128
-CHUNK = 4096
+CHUNK = 8192
+PIECE = 1024
 VMEM = pl.BlockSpec(memory_space=pltpu.VMEM)
 SMEM = pl.BlockSpec(memory_space=pltpu.SMEM)
 HBM = pl.BlockSpec(memory_space=pltpu.HBM)
 
 
-def call(kernel, out_shape, in_specs, scratch=(), limit=4):
+def call(kernel, out_shape, in_specs, scratch=(), limit=4, moved=0):
     many = isinstance(out_shape, (tuple, list))
     inner = pl.pallas_call(
         kernel,
@@ -29,6 +31,7 @@
         out_specs=[VMEM] * len(out_shape) if many else VMEM,
         scratch_shapes=list(scratch),
         compiler_params=pltpu.CompilerParams(vmem_limit_bytes=limit << 20),
+        cost_estimate=pl.CostEstimate(flops=0, bytes_accessed=moved, transcendentals=0) if moved else None,
     )
 
     def run(*args):
@@ -45,6 +48,10 @@
 
 def dot_t(a, b):
     return lax.dot_general(a, b, (((1,), (1,)), ((), ())), preferred_element_type=F32)
+
+
+def dot_tt(a, b):
+    return lax.dot_general(a, b, (((0,), (0,)), ((), ())), preferred_element_type=F32)
 
 
 def split2(x):
@@ -114,7 +121,7 @@
         target[:, 640:768] = square
 
 
-def project_pair_kernel(own, other, copies):
+def project_pair_kernel(own, other, w1, w2, w3, copies):
     total = own[...] + other[...]
     row_log = jnp.log2(total[:, 640:768] + TINY)
     meta = [jnp.floor(row_log * 256 + 0.5)]
@@ -151,115 +158,117 @@
         out[g * 32 : (g + 1) * 32, :] = x.astype(BF16)
 
 
-def fold(x, op):
-    out = x[:, 0:LANES]
-    for i in range(1, x.shape[1] // LANES):
-        out = op(out, x[:, i * LANES : (i + 1) * LANES])
-    return out
-
-
-def attend_kernel(
-    own, other, positions, valid, keys, values, keep, send, query, scores, acc, o_acc, v_buf, v_sem
-):
+def attend_kernel(own, other, positions, valid, keys, values, keep, send, query, shift, total_l, total_o):
     scale = 128.0**-0.5
     power = scale * 1.4426950408889634
     mine = core_index()
     length = valid[0]
-    whole = lax.div(length, CHUNK)
-    used = lax.div(length + (CHUNK - 1), CHUNK)
-
-    def load(c):
-        rows = pl.ds(pl.multiple_of(c * CHUNK, CHUNK), CHUNK)
-        return pltpu.make_async_copy(values.at[0, rows, :], v_buf.at[rows, :], v_sem.at[c])
-
-    @pl.loop(0, used)
-    def _(c):
-        load(c).start()
-
-    row = lax.broadcasted_iota(jnp.int32, (32, LANES), 0)
-    lane = lax.broadcasted_iota(jnp.int32, (32, LANES), 1)
-    of_row = jnp.zeros((32, LANES), jnp.int32)
-    of_lane = jnp.full((32, LANES), 1 << 20, jnp.int32)
-    for i in range(32):
-        of_row = jnp.where(row == i, positions[i], of_row)
-        of_lane = jnp.where(lane == i, positions[i], of_lane)
-    allowed = (of_lane <= of_row) & (lax.axis_index("seq") == 0)
+
     query[pl.ds(pl.multiple_of(mine * 128, 128), 128), :] = own[0:128, :]
     query[pl.ds(pl.multiple_of((1 - mine) * 128, 128), 128), :] = other[0:128, :]
     q = query[...]
-    pad = jnp.zeros((96, LANES), BF16)
     a, b = own[128:160, :].astype(F32), other[128:160, :].astype(F32)
-    k_new = jnp.concatenate([jnp.where(mine == 0, a, b).astype(BF16), pad], axis=0)
-    v_new = jnp.concatenate([jnp.where(mine == 0, b, a).astype(BF16), pad], axis=0)
-
-    def score(c):
-        rows = pl.ds(pl.multiple_of(c * CHUNK, CHUNK), CHUNK)
-        return dot_t(q, keys[0, rows, :])
-
-    acc[...] = jnp.full((256, LANES), LOW, F32)
+    k_new = jnp.where(mine == 0, a, b).astype(BF16)
+    v_new = jnp.where(mine == 0, b, a).astype(BF16)
+
+    def score(start):
+        return dot_t(keys[0, pl.ds(start, PIECE), :], q)
+
+    def only_valid(s, start):
+        slot = lax.broadcasted_iota(jnp.int32, (PIECE, 256), 0) + start
+        return jnp.where(slot < length, s, LOW)
+
+    def weigh(s, start, carry):
+        sums, o = carry
+        e = jnp.exp2(s * power - shift[0:1, :]).astype(BF16)
+        sums = sums + jnp.sum(e.astype(F32).reshape(PIECE // 8, 8, 256), axis=0)
+        return sums, o + dot_tt(values[0, pl.ds(start, PIECE), :], e)
+
+    def run(first, pieces, masked):
+        carry = (total_l[...], total_o[...])
+        starts = [pl.multiple_of(first + i * PIECE, PIECE) for i in range(pieces)]
+        s = score(starts[0])
+        for i in range(pieces):
+            ahead = score(starts[i + 1]) if i + 1 < pieces else None
+            carry = weigh(only_valid(s, starts[i]) if masked else s, starts[i], carry)
+            s = ahead
+        total_l[...], total_o[...] = carry
+
+    def restart(top):
+        shift[...] = jnp.broadcast_to(top * power, (8, 256))
+        total_l[...] = jnp.zeros((8, 256), F32)
+        total_o[...] = jnp.zeros((LANES, 256), F32)
+
+    restart(jnp.max(only_valid(score(0), 0), axis=0, keepdims=True))
+    whole = lax.div(length, CHUNK)
 
     @pl.loop(0, whole)
     def _(c):
-        s = score(c)
-        scores[c] = s
-        acc[...] = jnp.maximum(acc[...], fold(s, jnp.maximum))
-
-    @pl.when(used > whole)
+        run(pl.multiple_of(c * CHUNK, CHUNK), CHUNK // PIECE, False)
+
+    @pl.when(whole * CHUNK < length)
     def _():
-        slot = lax.broadcasted_iota(jnp.int32, (256, CHUNK), 1) + whole * CHUNK
-        s = jnp.where(slot < length, score(whole), LOW)
-        scores[whole] = s
-        acc[...] = jnp.maximum(acc[...], fold(s, jnp.maximum))
-
-    top = jnp.max(acc[...], axis=1, keepdims=True)
-    shift = top * power
-    acc[...] = jnp.zeros((256, LANES), F32)
-    o_acc[...] = jnp.zeros((256, LANES), F32)
-
-    @pl.loop(0, used)
-    def _(c):
-        rows = pl.ds(pl.multiple_of(c * CHUNK, CHUNK), CHUNK)
-        e = jnp.exp2(scores[c] * power - shift).astype(BF16)
-        acc[...] += fold(e.astype(F32), jnp.add)
-        load(c).wait()
-        o_acc[...] += dot(e, v_buf[rows, :])
-
-    total_l = jnp.sum(acc[...], axis=1, keepdims=True)
-    lse = top * scale + jnp.log(total_l)
-    summed = o_acc[...] / total_l
-
-    hold = jnp.concatenate([jnp.where(allowed, 0.0, -1.0)] * 8, axis=0)
-    s_new = jnp.where(hold < 0, LOW, dot_t(q, k_new) * scale)
-    top_new = jnp.max(s_new, axis=1, keepdims=True)
+        run(pl.multiple_of(whole * CHUNK, CHUNK), CHUNK // PIECE, True)
+
+    @pl.when(jnp.logical_not(jnp.max(total_l[...]) < 1e30))
+    def _():
+        pieces = lax.div(length + (PIECE - 1), PIECE)
+        shift[...] = jnp.full((8, 256), LOW, F32)
+
+        @pl.loop(0, pieces)
+        def _(c):
+            start = pl.multiple_of(c * PIECE, PIECE)
+            top = jnp.max(only_valid(score(start), start), axis=0, keepdims=True)
+            shift[...] = jnp.maximum(shift[...], top)
+
+        restart(shift[0:1, :])
+
+        @pl.loop(0, pieces)
+        def _(c):
+            run(pl.multiple_of(c * PIECE, PIECE), 1, True)
+
+    l_old = jnp.sum(total_l[...], axis=0, keepdims=True)
+    lse_old = shift[0:1, :] * math.log(2.0) + jnp.log(l_old)
+
+    lane = lax.broadcasted_iota(jnp.int32, (8, 256), 1) & 31
+    row = lax.broadcasted_iota(jnp.int32, (32, LANES), 0)
+    of_query = jnp.zeros((8, 256), jnp.int32)
+    of_key = jnp.zeros((32, LANES), jnp.int32)
+    for i in range(32):
+        of_query = jnp.where(lane == i, positions[i], of_query)
+        of_key = jnp.where(row == i, positions[i], of_key)
+    of_key = jnp.concatenate([of_key, of_key], axis=1)
+    allowed = (of_key <= of_query[0:1, :]) & (lax.axis_index("seq") == 0)
+    s_new = jnp.where(allowed, dot_t(k_new, q) * scale, LOW)
+    top_new = jnp.max(s_new, axis=0, keepdims=True)
     e_new = jnp.exp(s_new - top_new).astype(BF16)
-    l_new = jnp.sum(e_new.astype(F32), axis=1, keepdims=True)
-    o_new = dot(e_new, v_new) / l_new
+    l_new = jnp.sum(e_new.astype(F32), axis=0, keepdims=True)
     lse_new = top_new + jnp.log(l_new)
-
-    high = jnp.maximum(lse, lse_new)
-    f_old = jnp.exp(lse - high)
+    o_new = dot_tt(v_new, e_new)
+
+    high = jnp.maximum(lse_old, lse_new)
+    f_old = jnp.exp(lse_old - high)
     f_new = jnp.exp(lse_new - high)
     both = f_old + f_new
-    o_acc[...] = (summed * f_old + o_new * f_new) / both
-    acc[...] = jnp.broadcast_to(high + jnp.log(both), (256, LANES))
-    for target, half in ((keep, mine), (send, 1 - mine)):
-        rows = pl.ds(pl.multiple_of(half * 128, 128), 128)
-        target[0:128, :] = o_acc[rows, :]
-        target[128:256, :] = acc[rows, :]
+    o = total_o[...] * (f_old / (l_old * both)) + o_new * (f_new / (l_new * both))
+    lse = jnp.broadcast_to(high + jnp.log(both), (8, 256))
+    for target, first in ((keep, mine == 0), (send, mine != 0)):
+        target[0:128, :] = jnp.where(first, o[:, 0:128], o[:, 128:256])
+        target[128:136, :] = jnp.where(first, lse[:, 0:128], lse[:, 128:256])
 
 
 def merge_pair_kernel(own, other, copies):
-    la, lb = own[128:256, :], other[128:256, :]
+    la, lb = own[128:136, :], other[128:136, :]
     high = jnp.maximum(la, lb)
     fa, fb = jnp.exp(la - high), jnp.exp(lb - high)
     both = fa + fb
-    o = ((own[0:128, :] * fa + other[0:128, :] * fb) / both).astype(BF16)
-    lanes = jnp.transpose(high + jnp.log(both))[0:8]
-    row = lax.broadcasted_iota(jnp.int32, (8, LANES), 0)
-    p0 = lanes.astype(BF16).astype(F32)
-    rest = lanes - p0
+    o = (own[0:128, :] * (fa / both)[0:1] + other[0:128, :] * (fb / both)[0:1]).astype(BF16)
+    lse = high + jnp.log(both)
+    p0 = lse.astype(BF16).astype(F32)
+    rest = lse - p0
     p1 = rest.astype(BF16).astype(F32)
     p2 = rest - p1
+    row = lax.broadcasted_iota(jnp.int32, (8, LANES), 0)
     tail = jnp.where(row == 0, p0, jnp.where(row == 1, p1, p2))
     tail = jnp.concatenate([tail, jnp.zeros((8, LANES), F32)], axis=0).astype(BF16)
     for j in range(8):
@@ -272,13 +281,13 @@
     for j in range(8):
         tail = parts[j, 128:144, :].astype(F32)
         rows.append(tail[0:1] + tail[1:2] + tail[2:3])
-    lse = jnp.concatenate(rows, axis=0)
-    weight = jnp.exp(lse - jnp.max(lse, axis=0, keepdims=True))
-    weight = weight / jnp.sum(weight, axis=0, keepdims=True)
-    weight = jnp.transpose(jnp.concatenate([weight, jnp.zeros((120, LANES), F32)], axis=0))
-    total = parts[0, 0:128, :].astype(F32) * weight[:, 0:1]
+    high = functools.reduce(jnp.maximum, rows)
+    weights = [jnp.exp(r - high) for r in rows]
+    both = functools.reduce(jnp.add, weights)
+    total = parts[0, 0:128, :].astype(F32) * (weights[0] / both)
     for j in range(1, 8):
-        total += parts[j, 0:128, :].astype(F32) * weight[:, j : j + 1]
+        total += parts[j, 0:128, :].astype(F32) * (weights[j] / both)
+    total = jnp.transpose(total)
     for g in range(4):
         attn[:, g * 128 : (g + 1) * 128] = total[g * 32 : (g + 1) * 32].astype(BF16)
 
@@ -412,23 +421,22 @@
             pltpu.SemaphoreType.DMA((6,)),
         ],
     )(resid, attn_gain, w_query, w_key, w_value, rope_angle)
-    copies = call(project_pair_kernel, near((8, 32, 768), jnp.int16), [VMEM] * 2)(keep, to_other_core(send))
+    copies = call(project_pair_kernel, near((8, 32, 768), jnp.int16), [VMEM] * 2 + [HBM] * 3)(
+        keep, to_other_core(send), w_gate, w_up, w_down
+    )
     turned = call(rotate_kernel, near((160, LANES), BF16), [VMEM] * 3)(over_chips(copies), cos, sin)
 
-    chunks = 16384 // CHUNK
     keep, send = call(
         attend_kernel,
-        (near((256, LANES), F32), near((256, LANES), F32)),
-        [VMEM] * 2 + [SMEM] * 2 + [VMEM, HBM],
+        (near((136, LANES), F32), near((136, LANES), F32)),
+        [VMEM] * 2 + [SMEM] * 2 + [VMEM] * 2,
         scratch=[
             pltpu.VMEM((256, LANES), BF16),
-            pltpu.VMEM((chunks, 256, CHUNK), F32),
-            pltpu.VMEM((256, LANES), F32),
-            pltpu.VMEM((256, LANES), F32),
-            pltpu.VMEM((16384, LANES), BF16),
-            pltpu.SemaphoreType.DMA((chunks,)),
+            pltpu.VMEM((8, 256), F32),
+            pltpu.VMEM((8, 256), F32),
+            pltpu.VMEM((LANES, 256), F32),
         ],
-        limit=30,
+        limit=24,
     )(turned, to_other_core(turned), positions, valid_lengths, cache_keys, cache_values)
     copies = call(merge_pair_kernel, near((8, 144, LANES), BF16), [VMEM] * 2)(keep, to_other_core(send))
     attn = call(merge_kernel, near((32, 512), BF16), [VMEM])(over_chips(copies))

time: 105 us -> 97.8 us (0.931)
  local copies, waits for them, and re-layouts: 2.87 us -> 0.05 us
  Pallas kernels: 14.6 us -> 12.2 us
  blocking collectives: 70.4 us -> 68.9 us
    unnamed x16 -> x18, local copies, waits for them, and re-layouts: 2.87 us -> 0.05 us
    pallas_call x12, Pallas kernels: 14.6 us -> 12.2 us  [run(): inner(*(pltpu.with_memory_space_constraint(x, pltpu.HBM) if s is HBM else...]
    all_to_all x4, blocking collectives: 49.4 us -> 47.9 us  [over_chips(): return lax.all_to_all(x, 'seq', 0, 0, axis_index_groups=same_core)]
where the time goes in v2:
time: 97.8 us; the launch traced here: 97.3 us
  blocking collectives  68.9 us (70%)
  Pallas kernels  12.2 us (12%)
  starting transfers between devices  9.36 us (10%)
  waiting for transfers between devices  5.35 us (5%)
  between operations  1.42 us (1%)
    all_to_all x4, blocking collectives, over_chips(): return lax.all_to_all(x, 'seq', 0, 0, axis_index_groups=same_core)  47.9 us
    all_to_all x2, blocking collectives, over_tp(): return lax.all_to_all(x, 'tp', 0, 0)  21 us
    pallas_call x12, Pallas kernels, run(): inner(*(pltpu.with_memory_space_constraint(x, pltpu.HBM) if s is HBM else...  12.2 us
    ppermute x6, starting transfers between devices, to_other_core(): return lax.ppermute(x, 'seq', swap)  9.36 us
    ppermute x6, waiting for transfers between devices, to_other_core(): return lax.ppermute(x, 'seq', swap)  5.35 us
  transfers between devices with their start and end apart: 6, of which 6 were waited for; matrix products, arithmetic and copies ran while one was open for 0% of the time, Pallas kernels for 0%

profile of v2, /device:TPU:1, one launch (start us, length us, event | category | flops | bytes accessed | tf_op | source)
XLA Modules:
  0.0 97.3 jit_solution(8000053591498714260)
XLA Ops:
  0.6 1.8 %shard_map.158 = (f32[32,768]{1,0:T(8,128)S(1)}, f32[32,768]{1,0:T(8,128)S(1)}, f32[32,128]{1,0:T(8,128)S(1)}, f32[32,128]{1,0:T(8,128)S(1)}) custom-call(bf16[32,512]{1,0:T(8,128)(2,1)} %resid.3, bf16[512]{0:T(512)(128)(2,1)} %gain.2, bf16[512,1024]{1,0:T(8,128)(2,1)} %w_query.1, bf16[512,128]{1,0:T(8,128)(2,1)} %w_key.1, bf16[512,128]{1,0:T(8,128)(2,1)} %w_value.1, ...), custom_call_target="tpu_custom_call" | custom-call | tf_op jit(solution)/shard_map/pallas_call | solution.py:38
  2.4 1.5 %collective-permute-start = (f32[32,768]{1,0:T(8,128)S(1)}, f32[32,768]{1,0:T(8,128)S(1)}, u32[]{:S(2)}, u32[]{:S(2)}) collective-permute-start(f32[32,768]{1,0:T(8,128)S(1)} %get-tuple-element.13), channel_id=1, source_target_pairs={{0,8},{8,0},{16,24},{24,16},{32,40},{40,32},{48,56},{56,48},{64,72... | collective-permute-start | bytes 294920 | tf_op jit(solution)/shard_map/ppermute | solution.py:402
  4.0 0.9 collective-permute-done.other
  4.9 0.0 copy-start.3
  4.9 0.0 copy-start.4
  4.9 0.0 copy-start.8
  4.9 0.1 shard_map.159
  5.0 16.1 %all_to_all.30.parts = s16[8,32,768]{2,1,0:T(8,128)(2,1)S(1)} all-to-all(s16[8,32,768]{2,1,0:T(8,128)(2,1)S(1)} %shard_map.159), channel_id=1, replica_groups={{0,16,32,48,64,80,96,112},{8,24,40,56,72,88,104,120},{1,17,33,49,65,81,..., dimensions={0} | all-to-all | bytes 786432 | tf_op jit(solution)/shard_map/all_to_all | solution.py:405
  21.2 0.3 shard_map.160.own
  21.5 2.0 %collective-permute-start.1 = (bf16[160,128]{1,0:T(8,128)(2,1)S(1)}, bf16[160,128]{1,0:T(8,128)(2,1)S(1)}, u32[]{:S(2)}, u32[]{:S(2)}) collective-permute-start(bf16[160,128]{1,0:T(8,128)(2,1)S(1)} %shard_map.160.own), channel_id=1, source_target_pairs={{0,8},{8,0},{16,24},{24,16},{32,40},{40,32},{48,56},{56,48},{64,72... | collective-permute-start | bytes 122888 | tf_op jit(solution)/shard_map/ppermute | solution.py:402
  24.1 0.0 copy-start.5
  24.2 0.0 copy-start.6
  24.2 0.0 copy-start.7
  24.2 0.2 collective-permute-done.1.other
  24.4 0.0 copy-done.3
  24.4 0.0 copy-done.4
  24.4 0.0 copy-done.8
  24.4 0.0 copy-start
  24.4 0.0 copy-start.1
  24.4 6.0 %shard_map.161 = (f32[136,128]{1,0:T(8,128)S(1)}, f32[136,128]{1,0:T(8,128)S(1)}) custom-call(bf16[160,128]{1,0:T(8,128)(2,1)S(1)} %shard_map.160.own, bf16[160,128]{1,0:T(8,128)(2,1)S(1)} %collective-permute-done.1.other, s32[32]{0:T(128)S(1)} %copy-done.8, s32[1]{0:T(128)S(6)} %copy.17.valid, bf16[1,16384,128]{2,1,0:T(8,128)(2,1)S(1)} %copy-done.3, ...), custom_call_target="tpu_custom_call" | custom-call | tf_op jit(solution)/shard_map/pallas_call | solution.py:38
  30.4 0.1 collective-permute-start.2
  30.5 1.2 %collective-permute-done.2.other = f32[136,128]{1,0:T(8,128)S(1)} collective-permute-done((f32[136,128]{1,0:T(8,128)S(1)}, f32[136,128]{1,0:T(8,128)S(1)}, u32[]{:S(2)}, u32[]{:S(2)}) %collective-permute-start.2) | collective-permute-done | bytes 69664 | tf_op jit(solution)/shard_map/ppermute | solution.py:402
  31.8 11.2 %all_to_all.31.parts = bf16[8,144,128]{2,1,0:T(8,128)(2,1)S(1)} all-to-all(bf16[8,144,128]{2,1,0:T(8,128)(2,1)S(1)} %shard_map.162), channel_id=1, replica_groups={{0,16,32,48,64,80,96,112},{8,24,40,56,72,88,104,120},{1,17,33,49,65,81,..., dimensions={0} | all-to-all | bytes 589824 | tf_op jit(solution)/shard_map/all_to_all | solution.py:405
  43.0 0.2 shard_map.163.own
  43.2 1.7 %collective-permute-start.3 = (bf16[32,512]{1,0:T(8,128)(2,1)S(1)}, bf16[32,512]{1,0:T(8,128)(2,1)S(1)}, u32[]{:S(2)}, u32[]{:S(2)}) collective-permute-start(bf16[32,512]{1,0:T(8,128)(2,1)S(1)} %shard_map.163.own), channel_id=1, source_target_pairs={{0,8},{8,0},{16,24},{24,16},{32,40},{40,32},{48,56},{56,48},{64,72... | collective-permute-start | bytes 98312 | tf_op jit(solution)/shard_map/ppermute | solution.py:402
  44.9 0.9 collective-permute-done.3.other
  45.7 0.0 copy-done.5
  45.7 0.3 shard_map.164
  46.0 11.6 %all_to_all.32.parts = bf16[8,32,512]{2,1,0:T(8,128)(2,1)S(1)} all-to-all(bf16[8,32,512]{2,1,0:T(8,128)(2,1)S(1)} %shard_map.164), channel_id=1, replica_groups=mesh['seq'=16,'tp'=8] {'tp'}, dimensions={0} | all-to-all | bytes 524288 | tf_op jit(solution)/shard_map/all_to_all | solution.py:408
  57.6 0.0 copy-done.6
  57.6 0.0 copy-done.7
  57.6 0.0 copy-done
  57.6 0.0 copy-done.1
  57.6 0.0 copy-start.2
  57.7 1.8 %shard_map.165 = (bf16[32,512]{1,0:T(8,128)(2,1)}, bf16[32,512]{1,0:T(8,128)(2,1)S(1)}, f32[32,3712]{1,0:T(8,128)S(1)}, bf16[32,3712]{1,0:T(8,128)(2,1)S(1)}) custom-call(bf16[8,32,512]{2,1,0:T(8,128)(2,1)S(1)} %all_to_all.32.parts, bf16[32,512]{1,0:T(8,128)(2,1)S(1)} %copy-done.6, bf16[512]{0:T(512)(128)(2,1)S(1)} %copy-done.7, ...), custom_call_target="tpu_custom_call" | custom-call | tf_op jit(solution)/shard_map/pallas_call | solution.py:38
  59.5 1.5 %collective-permute-start.4 = (bf16[32,3712]{1,0:T(8,128)(2,1)S(1)}, bf16[32,3712]{1,0:T(8,128)(2,1)S(1)}, u32[]{:S(2)}, u32[]{:S(2)}) collective-permute-start(bf16[32,3712]{1,0:T(8,128)(2,1)S(1)} %get-tuple-element.20), channel_id=1, source_target_pairs={{0,8},{8,0},{16,24},{24,16},{32,40},{40,32},{48,56},{56,48},{64,72... | collective-permute-start | bytes 712712 | tf_op jit(solution)/shard_map/ppermute | solution.py:402
  61.0 1.1 %collective-permute-done.4.got = bf16[32,3712]{1,0:T(8,128)(2,1)S(1)} collective-permute-done((bf16[32,3712]{1,0:T(8,128)(2,1)S(1)}, bf16[32,3712]{1,0:T(8,128)(2,1)S(1)}, u32[]{:S(2)}, u32[]{:S(2)}) %collective-permute-start.4) | collective-permute-done | bytes 237600 | tf_op jit(solution)/shard_map/ppermute | solution.py:402
  62.1 0.1 shard_map.166
  62.2 10.6 %all_to_all.33.parts = bf16[8,16,1024]{2,1,0:T(8,128)(2,1)S(1)} all-to-all(bf16[8,16,1024]{2,1,0:T(8,128)(2,1)S(1)} %shard_map.166), channel_id=1, replica_groups={{0,16,32,48,64,80,96,112},{8,24,40,56,72,88,104,120},{1,17,33,49,65,81,..., dimensions={0} | all-to-all | bytes 524288 | tf_op jit(solution)/shard_map/all_to_all | solution.py:405
  72.7 0.1 shard_map.167
  72.9 10.0 %all_to_all.34.own = bf16[8,16,512]{2,1,0:T(8,128)(2,1)S(1)} all-to-all(bf16[8,16,512]{2,1,0:T(8,128)(2,1)S(1)} %shard_map.167), channel_id=1, replica_groups={{0,16,32,48,64,80,96,112},{8,24,40,56,72,88,104,120},{1,17,33,49,65,81,..., dimensions={0} | all-to-all | bytes 262144 | tf_op jit(solution)/shard_map/all_to_all | solution.py:405
  82.8 2.6 %collective-permute-start.5 = (bf16[8,16,512]{2,1,0:T(8,128)(2,1)S(1)}, bf16[8,16,512]{2,1,0:T(8,128)(2,1)S(1)}, u32[]{:S(2)}, u32[]{:S(2)}) collective-permute-start(bf16[8,16,512]{2,1,0:T(8,128)(2,1)S(1)} %all_to_all.34.own), channel_id=1, source_target_pairs={{0,8},{8,0},{16,24},{24,16},{32,40},{40,32},{48,56},{56,48},{64,72... | collective-permute-start | bytes 393224 | tf_op jit(solution)/shard_map/ppermute | solution.py:402
  85.4 1.0 %collective-permute-done.5.other = bf16[8,16,512]{2,1,0:T(8,128)(2,1)S(1)} collective-permute-done((bf16[8,16,512]{2,1,0:T(8,128)(2,1)S(1)}, bf16[8,16,512]{2,1,0:T(8,128)(2,1)S(1)}, u32[]{:S(2)}, u32[]{:S(2)}) %collective-permute-start.5) | collective-permute-done | bytes 131104 | tf_op jit(solution)/shard_map/ppermute | solution.py:402
  86.4 0.0 copy-done.2
  86.4 0.7 shard_map.168
  87.2 9.5 %all_to_all.35.parts = bf16[8,32,512]{2,1,0:T(8,128)(2,1)S(1)} all-to-all(bf16[8,32,512]{2,1,0:T(8,128)(2,1)S(1)} %shard_map.168), channel_id=1, replica_groups=mesh['seq'=16,'tp'=8] {'tp'}, dimensions={0} | all-to-all | bytes 524288 | tf_op jit(solution)/shard_map/all_to_all | solution.py:408
  96.6 0.7 shard_map.169
  (1 shorter events, 0.0 us)
Async XLA Ops:
  2.4 2.4 %collective-permute-start = (f32[32,768]{1,0:T(8,128)S(1)}, f32[32,768]{1,0:T(8,128)S(1)}, u32[]{:S(2)}, u32[]{:S(2)}) collective-permute-start(f32[32,768]{1,0:T(8,128)S(1)} %get-tuple-element.13), channel_id=1, source_target_pairs={{0,8},{8,0},{16,24},{24,16},{32,40},{40,32},{48,56},{56,48},{64,72... | collective-permute-start | bytes 294920 | tf_op jit(solution)/shard_map/ppermute | solution.py:402
  4.9 19.5 %copy-start.3 = (bf16[1,16384,128]{2,1,0:T(8,128)(2,1)S(1)}, bf16[1,16384,128]{2,1,0:T(8,128)(2,1)}, u32[]{:S(2)}) copy-start(bf16[1,16384,128]{2,1,0:T(8,128)(2,1)} %keys.1) | copy-start | bytes 12582916
  4.9 19.5 %copy-start.4 = (bf16[1,16384,128]{2,1,0:T(8,128)(2,1)S(1)}, bf16[1,16384,128]{2,1,0:T(8,128)(2,1)}, u32[]{:S(2)}) copy-start(bf16[1,16384,128]{2,1,0:T(8,128)(2,1)} %values.1) | copy-start | bytes 12582916
  4.9 19.5 %copy-start.8 = (s32[32]{0:T(128)S(1)}, s32[32]{0:T(128)}, u32[]{:S(2)}) copy-start(s32[32]{0:T(128)} %positions.1) | copy-start | bytes 388
  21.5 2.9 %collective-permute-start.1 = (bf16[160,128]{1,0:T(8,128)(2,1)S(1)}, bf16[160,128]{1,0:T(8,128)(2,1)S(1)}, u32[]{:S(2)}, u32[]{:S(2)}) collective-permute-start(bf16[160,128]{1,0:T(8,128)(2,1)S(1)} %shard_map.160.own), channel_id=1, source_target_pairs={{0,8},{8,0},{16,24},{24,16},{32,40},{40,32},{48,56},{56,48},{64,72... | collective-permute-start | bytes 122888 | tf_op jit(solution)/shard_map/ppermute | solution.py:402
  24.1 21.6 %copy-start.5 = (bf16[1024,512]{1,0:T(8,128)(2,1)S(1)}, bf16[1024,512]{1,0:T(8,128)(2,1)}, u32[]{:S(2)}) copy-start(bf16[1024,512]{1,0:T(8,128)(2,1)} %w_out.1) | copy-start | bytes 3145732
  24.2 33.5 %copy-start.6 = (bf16[32,512]{1,0:T(8,128)(2,1)S(1)}, bf16[32,512]{1,0:T(8,128)(2,1)}, u32[]{:S(2)}) copy-start(bf16[32,512]{1,0:T(8,128)(2,1)} %resid.3) | copy-start | bytes 98308
  24.2 33.5 %copy-start.7 = (bf16[512]{0:T(512)(128)(2,1)S(1)}, bf16[512]{0:T(512)(128)(2,1)}, u32[]{:S(2)}) copy-start(bf16[512]{0:T(512)(128)(2,1)} %gain.3) | copy-start | bytes 3076
  24.4 33.3 %copy-start = (bf16[512,3584]{1,0:T(8,128)(2,1)S(1)}, bf16[512,3584]{1,0:T(8,128)(2,1)}, u32[]{:S(2)}) copy-start(bf16[512,3584]{1,0:T(8,128)(2,1)} %w_gate.1) | copy-start | bytes 11010052
  24.4 33.3 %copy-start.1 = (bf16[512,3584]{1,0:T(8,128)(2,1)S(1)}, bf16[512,3584]{1,0:T(8,128)(2,1)}, u32[]{:S(2)}) copy-start(bf16[512,3584]{1,0:T(8,128)(2,1)} %w_up.1) | copy-start | bytes 11010052
  30.4 1.3 %collective-permute-start.2 = (f32[136,128]{1,0:T(8,128)S(1)}, f32[136,128]{1,0:T(8,128)S(1)}, u32[]{:S(2)}, u32[]{:S(2)}) collective-permute-start(f32[136,128]{1,0:T(8,128)S(1)} %get-tuple-element.17), channel_id=1, source_target_pairs={{0,8},{8,0},{16,24},{24,16},{32,40},{40,32},{48,56},{56,48},{64,72... | collective-permute-start | bytes 208904 | tf_op jit(solution)/shard_map/ppermute | solution.py:402
  43.2 2.5 %collective-permute-start.3 = (bf16[32,512]{1,0:T(8,128)(2,1)S(1)}, bf16[32,512]{1,0:T(8,128)(2,1)S(1)}, u32[]{:S(2)}, u32[]{:S(2)}) collective-permute-start(bf16[32,512]{1,0:T(8,128)(2,1)S(1)} %shard_map.163.own), channel_id=1, source_target_pairs={{0,8},{8,0},{16,24},{24,16},{32,40},{40,32},{48,56},{56,48},{64,72... | collective-permute-start | bytes 98312 | tf_op jit(solution)/shard_map/ppermute | solution.py:402
  57.6 28.8 %copy-start.2 = (bf16[3584,512]{1,0:T(8,128)(2,1)S(1)}, bf16[3584,512]{1,0:T(8,128)(2,1)}, u32[]{:S(2)}) copy-start(bf16[3584,512]{1,0:T(8,128)(2,1)} %w_down.1) | copy-start | bytes 11010052
  59.5 2.6 %collective-permute-start.4 = (bf16[32,3712]{1,0:T(8,128)(2,1)S(1)}, bf16[32,3712]{1,0:T(8,128)(2,1)S(1)}, u32[]{:S(2)}, u32[]{:S(2)}) collective-permute-start(bf16[32,3712]{1,0:T(8,128)(2,1)S(1)} %get-tuple-element.20), channel_id=1, source_target_pairs={{0,8},{8,0},{16,24},{24,16},{32,40},{40,32},{48,56},{56,48},{64,72... | collective-permute-start | bytes 712712 | tf_op jit(solution)/shard_map/ppermute | solution.py:402
  82.8 3.6 %collective-permute-start.5 = (bf16[8,16,512]{2,1,0:T(8,128)(2,1)S(1)}, bf16[8,16,512]{2,1,0:T(8,128)(2,1)S(1)}, u32[]{:S(2)}, u32[]{:S(2)}) collective-permute-start(bf16[8,16,512]{2,1,0:T(8,128)(2,1)S(1)} %all_to_all.34.own), channel_id=1, source_target_pairs={{0,8},{8,0},{16,24},{24,16},{32,40},{40,32},{48,56},{56,48},{64,72... | collective-permute-start | bytes 393224 | tf_op jit(solution)/shard_map/ppermute | solution.py:402

commit v3 on v2

--- a/solution.py
+++ b/solution.py
@@ -71,6 +71,10 @@
 
 def core_index():
     return lax.rem(lax.axis_index("seq"), 2)
+
+
+def chip_index():
+    return lax.div(lax.axis_index("seq"), 2)
 
 
 def project_kernel(
@@ -98,8 +102,8 @@
         (gain, gain_buf),
         (w_key, kv_buf.at[0]),
         (w_value, kv_buf.at[1]),
-        (w_query, q_buf),
     ]
+    pairs += [(w_query.at[pl.ds(i * 128, 128), :], q_buf.at[pl.ds(i * 128, 128), :]) for i in range(4)]
     loads = [pltpu.make_async_copy(src, dst, sems.at[i]) for i, (src, dst) in enumerate(pairs)]
     for load in loads:
         load.start()
@@ -134,31 +138,53 @@
         meta.append(jnp.broadcast_to(grade, (32, LANES)))
     lane = lax.broadcasted_iota(jnp.int32, (32, LANES), 1)
     last = jnp.where(lane < 2, jnp.where(lane == 0, meta[0], meta[1]), jnp.where(lane == 2, meta[2], meta[3]))
-    sent = jnp.concatenate(coded + [last], axis=1).astype(jnp.int32).astype(jnp.int16)
-    for j in range(8):
-        copies[j] = sent
-
-
-def rotate_kernel(parts, cos, sin, out):
-    total = jnp.zeros((32, 640), F32)
-    square = jnp.zeros((32, 1), F32)
-    for j in range(8):
-        part = parts[j].astype(jnp.int32).astype(F32)
-        meta = part[:, 640:768]
-        square += jnp.exp2(meta[:, 0:1] / 256 + meta[:, 1:2] / (256 * 16384))
-        step = jnp.exp2(meta) / FULL
-        total += jnp.concatenate([part[:, 0:512] * step[:, 2:3], part[:, 512:640] * step[:, 3:4]], axis=1)
-    total = total * lax.rsqrt(square / 8192 + EPS)
-    turned = []
-    for g in range(5):
-        x = total[:, g * 128 : (g + 1) * 128]
-        turned.append(x * cos[...] + pltpu.roll(x, LANES // 2, 1) * sin[...])
-    last = jnp.where(core_index() == 0, turned[4], total[:, 512:640])
-    for g, x in enumerate(turned[:4] + [last]):
-        out[g * 32 : (g + 1) * 32, :] = x.astype(BF16)
-
-
-def attend_kernel(own, other, positions, valid, keys, values, keep, send, query, shift, total_l, total_o):
+    last = jnp.transpose(jnp.concatenate([last, jnp.zeros((96, LANES), F32)], axis=0))[0:8]
+    heads = jnp.concatenate([coded[0][:, g * 128 : (g + 1) * 128] for g in range(4)], axis=0)
+    heads = heads.astype(jnp.int32).astype(jnp.int16)
+    for j in range(8):
+        four = coded[1][j // 2 * 8 : j // 2 * 8 + 8]
+        four = pltpu.roll(four, 4, 0) if j % 2 else four
+        copies[j, 0:128, :] = heads
+        copies[j, 128:144, :] = jnp.concatenate([four, last], axis=0).astype(jnp.int32).astype(jnp.int16)
+
+
+def rotate_kernel(parts, cos, sin, out, steps):
+    tails = [parts[j, 128:144, :].astype(jnp.int32).astype(F32) for j in range(8)]
+    square = jnp.zeros((1, LANES), F32)
+    for tail in tails:
+        square += jnp.exp2(tail[8:9] / 256 + tail[9:10] / (256 * 16384))
+    inv = lax.rsqrt(square / 8192 + EPS)
+    rows = [jnp.exp2(tail[10:11]) * (inv / FULL) for tail in tails]
+    rows += [jnp.exp2(tail[11:12]) * (inv / FULL) for tail in tails]
+    turned = jnp.transpose(jnp.concatenate(rows + [jnp.zeros((112, LANES), F32)], axis=0))
+    steps[...] = turned[0:32]
+
+    for g in range(4):
+        x = jnp.zeros((32, LANES), F32)
+        for j in range(8):
+            head = parts[j, g * 32 : (g + 1) * 32, :].astype(jnp.int32).astype(F32)
+            x += head * steps[:, j : j + 1]
+        out[g * 32 : (g + 1) * 32, :] = (x * cos[...] + pltpu.roll(x, LANES // 2, 1) * sin[...]).astype(BF16)
+
+    chip = chip_index()
+    base = pl.ds(pl.multiple_of(lax.div(chip, 2) * 8, 8), 8)
+
+    def four(ref):
+        x = ref[base, :]
+        return jnp.where(lax.rem(chip, 2) == 0, x, pltpu.roll(x, 4, 0))
+
+    step = four(steps)
+    x = jnp.zeros((8, LANES), F32)
+    for j in range(8):
+        x += tails[j][0:8] * step[:, 8 + j : 9 + j]
+    key = x * four(cos) + pltpu.roll(x, LANES // 2, 1) * four(sin)
+    x = jnp.where(core_index() == 0, key, x)
+    out[128:144, :] = jnp.concatenate([x, jnp.zeros((8, LANES), F32)], axis=0).astype(BF16)
+
+
+def attend_kernel(
+    own, other, positions, valid, keys, values, keep, send, query, shift, total_l, total_o, new_o, new_lse
+):
     scale = 128.0**-0.5
     power = scale * 1.4426950408889634
     mine = core_index()
@@ -167,15 +193,32 @@
     query[pl.ds(pl.multiple_of(mine * 128, 128), 128), :] = own[0:128, :]
     query[pl.ds(pl.multiple_of((1 - mine) * 128, 128), 128), :] = other[0:128, :]
     q = query[...]
-    a, b = own[128:160, :].astype(F32), other[128:160, :].astype(F32)
+    a, b = own[128:144, :].astype(F32), other[128:144, :].astype(F32)
     k_new = jnp.where(mine == 0, a, b).astype(BF16)
     v_new = jnp.where(mine == 0, b, a).astype(BF16)
 
-    def score(start):
-        return dot_t(keys[0, pl.ds(start, PIECE), :], q)
+    lane = lax.broadcasted_iota(jnp.int32, (8, 256), 1) & 31
+    row = lax.broadcasted_iota(jnp.int32, (16, 256), 0)
+    of_query = jnp.zeros((8, 256), jnp.int32)
+    of_key = jnp.full((16, 256), 1 << 20, jnp.int32)
+    for i in range(32):
+        of_query = jnp.where(lane == i, positions[i], of_query)
+    for i in range(4):
+        of_key = jnp.where(row == i, positions[chip_index() * 4 + i], of_key)
+    allowed = (of_key <= of_query[0:1, :]) & (mine == 0)
+    s_new = jnp.where(allowed, dot_t(k_new, q) * scale, LOW)
+    top_new = jnp.max(s_new, axis=0, keepdims=True)
+    e_new = jnp.exp(s_new - top_new).astype(BF16)
+    l_new = jnp.sum(e_new.astype(F32), axis=0, keepdims=True)
+    lse_new = top_new + jnp.log(l_new)
+    new_o[...] = dot_tt(v_new, e_new) / l_new
+    new_lse[...] = jnp.broadcast_to(lse_new, (8, 256))
+
+    def score(start, count=PIECE):
+        return dot_t(keys[0, pl.ds(start, count), :], q)
 
     def only_valid(s, start):
-        slot = lax.broadcasted_iota(jnp.int32, (PIECE, 256), 0) + start
+        slot = lax.broadcasted_iota(jnp.int32, s.shape, 0) + start
         return jnp.where(slot < length, s, LOW)
 
     def weigh(s, start, carry):
@@ -199,16 +242,23 @@
         total_l[...] = jnp.zeros((8, 256), F32)
         total_o[...] = jnp.zeros((LANES, 256), F32)
 
-    restart(jnp.max(only_valid(score(0), 0), axis=0, keepdims=True))
-    whole = lax.div(length, CHUNK)
-
-    @pl.loop(0, whole)
-    def _(c):
-        run(pl.multiple_of(c * CHUNK, CHUNK), CHUNK // PIECE, False)
-
-    @pl.when(whole * CHUNK < length)
+    restart(jnp.max(only_valid(score(0, 256), 0), axis=0, keepdims=True))
+
+    @pl.when(length == 16384)
     def _():
-        run(pl.multiple_of(whole * CHUNK, CHUNK), CHUNK // PIECE, True)
+        run(0, 16384 // PIECE, False)
+
+    @pl.when(length < 16384)
+    def _():
+        half_full = length >= CHUNK
+
+        @pl.when(half_full)
+        def _():
+            run(0, CHUNK // PIECE, False)
+
+        @pl.when(length != CHUNK)
+        def _():
+            run(pl.multiple_of(jnp.where(half_full, CHUNK, 0), CHUNK), CHUNK // PIECE, True)
 
     @pl.when(jnp.logical_not(jnp.max(total_l[...]) < 1e30))
     def _():
@@ -230,27 +280,12 @@
     l_old = jnp.sum(total_l[...], axis=0, keepdims=True)
     lse_old = shift[0:1, :] * math.log(2.0) + jnp.log(l_old)
 
-    lane = lax.broadcasted_iota(jnp.int32, (8, 256), 1) & 31
-    row = lax.broadcasted_iota(jnp.int32, (32, LANES), 0)
-    of_query = jnp.zeros((8, 256), jnp.int32)
-    of_key = jnp.zeros((32, LANES), jnp.int32)
-    for i in range(32):
-        of_query = jnp.where(lane == i, positions[i], of_query)
-        of_key = jnp.where(row == i, positions[i], of_key)
-    of_key = jnp.concatenate([of_key, of_key], axis=1)
-    allowed = (of_key <= of_query[0:1, :]) & (lax.axis_index("seq") == 0)
-    s_new = jnp.where(allowed, dot_t(k_new, q) * scale, LOW)
-    top_new = jnp.max(s_new, axis=0, keepdims=True)
-    e_new = jnp.exp(s_new - top_new).astype(BF16)
-    l_new = jnp.sum(e_new.astype(F32), axis=0, keepdims=True)
-    lse_new = top_new + jnp.log(l_new)
-    o_new = dot_tt(v_new, e_new)
-
+    lse_new = new_lse[0:1, :]
     high = jnp.maximum(lse_old, lse_new)
     f_old = jnp.exp(lse_old - high)
     f_new = jnp.exp(lse_new - high)
     both = f_old + f_new
-    o = total_o[...] * (f_old / (l_old * both)) + o_new * (f_new / (l_new * both))
+    o = total_o[...] * (f_old / (l_old * both)) + new_o[...] * (f_new / both)
     lse = jnp.broadcast_to(high + jnp.log(both), (8, 256))
     for target, first in ((keep, mine == 0), (send, mine != 0)):
         target[0:128, :] = jnp.where(first, o[:, 0:128], o[:, 128:256])
@@ -309,26 +344,33 @@
     return total
 
 
-def gate_up_kernel(parts, resid, gain, w_gate, w_up, attn_out, mid, keep, send):
+def gate_up(x, w_gate, w_up, half, target):
+    for i in range(2):
+        cols = pl.ds(pl.multiple_of(half * 1792 + i * 896, LANES), 896)
+        target[:, i * 896 : (i + 1) * 896] = dot(x, w_gate[:, cols]).astype(target.dtype)
+        target[:, 1792 + i * 896 : 1792 + (i + 1) * 896] = dot(x, w_up[:, cols]).astype(target.dtype)
+
+
+def gate_up_send_kernel(parts, resid, gain, w_gate, w_up, attn_out, mid, normed, square, send):
     branch = sum_parts(parts).astype(BF16)
     attn_out[...] = branch
     hidden = (resid[...].astype(F32) + branch.astype(F32)).astype(BF16)
     mid[...] = hidden
     x32 = hidden.astype(F32)
     x = (x32 * gain[...].astype(F32)[None, :]).astype(BF16)
-    square = jnp.broadcast_to(jnp.sum(x32 * x32, axis=1, keepdims=True), (32, LANES))
-    mine = core_index()
-    for target, half in ((keep, mine), (send, 1 - mine)):
-        for i in range(2):
-            cols = pl.ds(pl.multiple_of(half * 1792 + i * 896, LANES), 896)
-            target[:, i * 896 : (i + 1) * 896] = dot(x, w_gate[:, cols]).astype(target.dtype)
-            target[:, 1792 + i * 896 : 1792 + (i + 1) * 896] = dot(x, w_up[:, cols]).astype(target.dtype)
-    keep[:, 3584:3712] = square
-    send[:, 3584:3712] = lane_split(square)
-
-
-def gate_up_pair_kernel(keep, got, pieces):
-    square = keep[:, 3584:3712] + lane_join(got[:, 3584:3712].astype(F32))
+    normed[...] = x
+    total = jnp.broadcast_to(jnp.sum(x32 * x32, axis=1, keepdims=True), (32, LANES))
+    square[...] = total
+    gate_up(x, w_gate, w_up, 1 - core_index(), send)
+    send[:, 3584:3712] = lane_split(total)
+
+
+def gate_up_keep_kernel(normed, w_gate, w_up, keep):
+    gate_up(normed[...], w_gate, w_up, core_index(), keep)
+
+
+def gate_up_pair_kernel(keep, own_square, got, pieces):
+    square = own_square[...] + lane_join(got[:, 3584:3712].astype(F32))
     high = square.astype(BF16).astype(F32)
     low = square - high
     for j in range(8):
@@ -355,19 +397,25 @@
         copies[j] = packed
 
 
-def down_kernel(own, other, w_down, copies):
+def down(acts, w_down, half):
     total = jnp.zeros((32, 512), F32)
-    mine = core_index()
-    for source, half in ((own, mine), (other, 1 - mine)):
-        for ch in range(2):
-            wide = []
-            for rg in range(4):
-                piece = source[rg * 2 + ch].astype(F32)
-                wide.append(jnp.concatenate([piece[0:8], piece[8:16, 0:384]], axis=1))
-            act = jnp.concatenate(wide, axis=0).astype(BF16)
-            rows = pl.ds(pl.multiple_of(half * 1792 + ch * 896, LANES), 896)
-            total += dot(act, w_down[rows, :])
-    part = total.astype(BF16)
+    for ch in range(2):
+        wide = []
+        for rg in range(4):
+            piece = acts[rg * 2 + ch].astype(F32)
+            wide.append(jnp.concatenate([piece[0:8], piece[8:16, 0:384]], axis=1))
+        act = jnp.concatenate(wide, axis=0).astype(BF16)
+        rows = pl.ds(pl.multiple_of(half * 1792 + ch * 896, LANES), 896)
+        total += dot(act, w_down[rows, :])
+    return total
+
+
+def down_own_kernel(acts, w_down, part):
+    part[...] = down(acts, w_down, core_index())
+
+
+def down_other_kernel(own, acts, w_down, copies):
+    part = (own[...] + down(acts, w_down, 1 - core_index())).astype(BF16)
     for j in range(8):
         copies[j] = part
 
@@ -418,13 +466,15 @@
             pltpu.VMEM((512, 1024), BF16),
             pltpu.VMEM((2, 512, LANES), BF16),
             pltpu.VMEM((32, 64), F32),
-            pltpu.SemaphoreType.DMA((6,)),
+            pltpu.SemaphoreType.DMA((9,)),
         ],
     )(resid, attn_gain, w_query, w_key, w_value, rope_angle)
-    copies = call(project_pair_kernel, near((8, 32, 768), jnp.int16), [VMEM] * 2 + [HBM] * 3)(
+    copies = call(project_pair_kernel, near((8, 144, LANES), jnp.int16), [VMEM] * 2 + [HBM] * 3)(
         keep, to_other_core(send), w_gate, w_up, w_down
     )
-    turned = call(rotate_kernel, near((160, LANES), BF16), [VMEM] * 3)(over_chips(copies), cos, sin)
+    turned = call(rotate_kernel, near((144, LANES), BF16), [VMEM] * 3, scratch=[pltpu.VMEM((32, LANES), F32)])(
+        over_chips(copies), cos, sin
+    )
 
     keep, send = call(
         attend_kernel,
@@ -435,6 +485,8 @@
             pltpu.VMEM((8, 256), F32),
             pltpu.VMEM((8, 256), F32),
             pltpu.VMEM((LANES, 256), F32),
+            pltpu.VMEM((LANES, 256), F32),
+            pltpu.VMEM((8, 256), F32),
         ],
         limit=24,
     )(turned, to_other_core(turned), positions, valid_lengths, cache_keys, cache_values)
@@ -443,17 +495,21 @@
     copies = call(out_kernel, near((8, 32, 512), BF16), [VMEM] * 3)(attn, to_other_core(attn), w_out)
     parts = over_tp(copies)
 
-    attn_out, mid, keep, send = call(
-        gate_up_kernel,
-        (shape((32, 512), BF16), near((32, 512), BF16), near((32, 3712), F32), near((32, 3712), BF16)),
+    attn_out, mid, normed, square, send = call(
+        gate_up_send_kernel,
+        (shape((32, 512), BF16), near((32, 512), BF16), near((32, 512), BF16), table, near((32, 3712), BF16)),
         [VMEM] * 5,
         limit=12,
     )(parts, resid, ffn_gain, w_gate, w_up)
-    pieces = call(gate_up_pair_kernel, near((8, 16, 1024), BF16), [VMEM] * 2)(keep, to_other_core(send))
+    got = to_other_core(send)
+    keep = call(gate_up_keep_kernel, near((32, 3584), F32), [VMEM] * 3, limit=12)(normed, w_gate, w_up)
+    pieces = call(gate_up_pair_kernel, near((8, 16, 1024), BF16), [VMEM] * 3)(keep, square, got)
     parts = over_chips(pieces)
     copies = call(act_kernel, near((8, 16, 512), BF16), [VMEM])(parts)
     acts = over_chips(copies)
-    copies = call(down_kernel, near((8, 32, 512), BF16), [VMEM] * 3, limit=8)(acts, to_other_core(acts), w_down)
+    got = to_other_core(acts)
+    part = call(down_own_kernel, near((32, 512), F32), [VMEM] * 2, limit=8)(acts, w_down)
+    copies = call(down_other_kernel, near((8, 32, 512), BF16), [VMEM] * 3, limit=8)(part, got, w_down)
     parts = over_tp(copies)
     layer_out = call(final_kernel, shape((32, 512), BF16), [VMEM] * 2)(parts, mid)
     return (attn_out, layer_out)

time: 97.8 us -> 96.2 us (0.984)
  starting transfers between devices: 9.36 us -> 11.5 us
  Pallas kernels: 12.2 us -> 10.5 us
  waiting for transfers between devices: 5.35 us -> 3.89 us
    ppermute x6, starting transfers between devices: 9.36 us -> 11.5 us  [to_other_core(): return lax.ppermute(x, 'seq', swap)]
    pallas_call x12 -> x14, Pallas kernels: 12.2 us -> 10.5 us  [run(): inner(*(pltpu.with_memory_space_constraint(x, pltpu.HBM) if s is HBM else...]
    ppermute x6, waiting for transfers between devices: 5.35 us -> 3.89 us  [to_other_core(): return lax.ppermute(x, 'seq', swap)]
  transfers between devices with their start and end apart: 6 -> 6, of which waited for: 6 -> 6; matrix products, arithmetic and copies ran while one was open for 0% -> 0% of each run, Pallas kernels for 0% -> 1%
where the time goes in v3:
time: 96.2 us; the launch traced here: 95.8 us
  blocking collectives  68.4 us (71%)
  starting transfers between devices  11.5 us (12%)
  Pallas kernels  10.5 us (11%)
  waiting for transfers between devices  3.89 us (4%)
  between operations  1.4 us (1%)
    all_to_all x4, blocking collectives, over_chips(): return lax.all_to_all(x, 'seq', 0, 0, axis_index_groups=same_core)  47.4 us
    all_to_all x2, blocking collectives, over_tp(): return lax.all_to_all(x, 'tp', 0, 0)  21 us
    ppermute x6, starting transfers between devices, to_other_core(): return lax.ppermute(x, 'seq', swap)  11.5 us
    pallas_call x14, Pallas kernels, run(): inner(*(pltpu.with_memory_space_constraint(x, pltpu.HBM) if s is HBM else...  10.5 us
    ppermute x6, waiting for transfers between devices, to_other_core(): return lax.ppermute(x, 'seq', swap)  3.89 us
  transfers between devices with their start and end apart: 6, of which 6 were waited for; matrix products, arithmetic and copies ran while one was open for 0% of the time, Pallas kernels for 1%

profile of v3, /device:TPU:1, one launch (start us, length us, event | category | flops | bytes accessed | tf_op | source)
XLA Modules:
  0.0 95.8 jit_solution(14328103093740898191)
XLA Ops:
  0.6 1.8 %shard_map.158 = (f32[32,768]{1,0:T(8,128)S(1)}, f32[32,768]{1,0:T(8,128)S(1)}, f32[32,128]{1,0:T(8,128)S(1)}, f32[32,128]{1,0:T(8,128)S(1)}) custom-call(bf16[32,512]{1,0:T(8,128)(2,1)} %resid.3, bf16[512]{0:T(512)(128)(2,1)} %gain.2, bf16[512,1024]{1,0:T(8,128)(2,1)} %w_query.1, bf16[512,128]{1,0:T(8,128)(2,1)} %w_key.1, bf16[512,128]{1,0:T(8,128)(2,1)} %w_value.1, ...), custom_call_target="tpu_custom_call" | custom-call | tf_op jit(solution)/shard_map/pallas_call | solution.py:38
  2.4 1.5 %collective-permute-start = (f32[32,768]{1,0:T(8,128)S(1)}, f32[32,768]{1,0:T(8,128)S(1)}, u32[]{:S(2)}, u32[]{:S(2)}) collective-permute-start(f32[32,768]{1,0:T(8,128)S(1)} %get-tuple-element.14), channel_id=1, source_target_pairs={{0,8},{8,0},{16,24},{24,16},{32,40},{40,32},{48,56},{56,48},{64,72... | collective-permute-start | bytes 294920 | tf_op jit(solution)/shard_map/ppermute | solution.py:450
  3.9 0.9 collective-permute-done.other
  4.9 0.0 copy-start.3
  4.9 0.0 copy-start.4
  4.9 0.0 copy-start.8
  4.9 0.2 shard_map.159
  5.0 15.5 %all_to_all.30.parts = s16[8,144,128]{2,1,0:T(8,128)(2,1)S(1)} all-to-all(s16[8,144,128]{2,1,0:T(8,128)(2,1)S(1)} %shard_map.159), channel_id=1, replica_groups={{0,16,32,48,64,80,96,112},{8,24,40,56,72,88,104,120},{1,17,33,49,65,81,..., dimensions={0} | all-to-all | bytes 589824 | tf_op jit(solution)/shard_map/all_to_all | solution.py:453
  20.5 0.6 shard_map.160.own
  21.1 1.6 %collective-permute-start.1 = (bf16[144,128]{1,0:T(8,128)(2,1)S(1)}, bf16[144,128]{1,0:T(8,128)(2,1)S(1)}, u32[]{:S(2)}, u32[]{:S(2)}) collective-permute-start(bf16[144,128]{1,0:T(8,128)(2,1)S(1)} %shard_map.160.own), channel_id=1, source_target_pairs={{0,8},{8,0},{16,24},{24,16},{32,40},{40,32},{48,56},{56,48},{64,72... | collective-permute-start | bytes 110600 | tf_op jit(solution)/shard_map/ppermute | solution.py:450
  23.4 0.0 copy-start.5
  23.4 0.0 copy-start.6
  23.4 0.0 copy-start.7
  23.4 0.2 collective-permute-done.1.other
  23.6 0.0 copy-done.3
  23.6 0.0 copy-done.4
  23.6 0.0 copy-done.8
  23.6 0.0 copy-start
  23.6 0.0 copy-start.1
  23.6 3.9 %shard_map.161 = (f32[136,128]{1,0:T(8,128)S(1)}, f32[136,128]{1,0:T(8,128)S(1)}) custom-call(bf16[144,128]{1,0:T(8,128)(2,1)S(1)} %shard_map.160.own, bf16[144,128]{1,0:T(8,128)(2,1)S(1)} %collective-permute-done.1.other, s32[32]{0:T(128)S(1)} %copy-done.8, s32[1]{0:T(128)S(6)} %copy.17.valid, bf16[1,16384,128]{2,1,0:T(8,128)(2,1)S(1)} %copy-done.3, ...), custom_call_target="tpu_custom_call" | custom-call | tf_op jit(solution)/shard_map/pallas_call | solution.py:38
  27.5 2.8 %collective-permute-start.2 = (f32[136,128]{1,0:T(8,128)S(1)}, f32[136,128]{1,0:T(8,128)S(1)}, u32[]{:S(2)}, u32[]{:S(2)}) collective-permute-start(f32[136,128]{1,0:T(8,128)S(1)} %get-tuple-element.18), channel_id=1, source_target_pairs={{0,8},{8,0},{16,24},{24,16},{32,40},{40,32},{48,56},{56,48},{64,72... | collective-permute-start | bytes 208904 | tf_op jit(solution)/shard_map/ppermute | solution.py:450
  30.3 0.9 collective-permute-done.2.other
  31.2 11.4 %all_to_all.31.parts = bf16[8,144,128]{2,1,0:T(8,128)(2,1)S(1)} all-to-all(bf16[8,144,128]{2,1,0:T(8,128)(2,1)S(1)} %shard_map.162), channel_id=1, replica_groups={{0,16,32,48,64,80,96,112},{8,24,40,56,72,88,104,120},{1,17,33,49,65,81,..., dimensions={0} | all-to-all | bytes 589824 | tf_op jit(solution)/shard_map/all_to_all | solution.py:453
  42.6 0.2 shard_map.163.own
  42.8 1.5 %collective-permute-start.3 = (bf16[32,512]{1,0:T(8,128)(2,1)S(1)}, bf16[32,512]{1,0:T(8,128)(2,1)S(1)}, u32[]{:S(2)}, u32[]{:S(2)}) collective-permute-start(bf16[32,512]{1,0:T(8,128)(2,1)S(1)} %shard_map.163.own), channel_id=1, source_target_pairs={{0,8},{8,0},{16,24},{24,16},{32,40},{40,32},{48,56},{56,48},{64,72... | collective-permute-start | bytes 98312 | tf_op jit(solution)/shard_map/ppermute | solution.py:450
  44.3 0.9 collective-permute-done.3.other
  45.2 0.0 copy-done.5
  45.2 0.3 shard_map.164
  45.5 11.6 %all_to_all.32.parts = bf16[8,32,512]{2,1,0:T(8,128)(2,1)S(1)} all-to-all(bf16[8,32,512]{2,1,0:T(8,128)(2,1)S(1)} %shard_map.164), channel_id=1, replica_groups=mesh['seq'=16,'tp'=8] {'tp'}, dimensions={0} | all-to-all | bytes 524288 | tf_op jit(solution)/shard_map/all_to_all | solution.py:456
  57.1 0.0 copy-done.6
  57.1 0.0 copy-done.7
  57.1 0.0 copy-done
  57.1 0.0 copy-done.1
  57.1 1.2 %shard_map.165 = (bf16[32,512]{1,0:T(8,128)(2,1)}, bf16[32,512]{1,0:T(8,128)(2,1)S(1)}, bf16[32,512]{1,0:T(8,128)(2,1)S(1)}, f32[32,128]{1,0:T(8,128)S(1)}, bf16[32,3712]{1,0:T(8,128)(2,1)S(1)}) custom-call(bf16[8,32,512]{2,1,0:T(8,128)(2,1)S(1)} %all_to_all.32.parts, bf16[32,512]{1,0:T(8,128)(2,1)S(1)} %copy-done.6, bf16[512]{0:T(512)(128)(2,1)S(1)} %copy-done.7, ...), custom_call_target="tpu_custom_call" | custom-call | tf_op jit(solution)/shard_map/pallas_call | solution.py:38
  58.3 1.5 %collective-permute-start.4 = (bf16[32,3712]{1,0:T(8,128)(2,1)S(1)}, bf16[32,3712]{1,0:T(8,128)(2,1)S(1)}, u32[]{:S(2)}, u32[]{:S(2)}) collective-permute-start(bf16[32,3712]{1,0:T(8,128)(2,1)S(1)} %get-tuple-element.22), channel_id=1, source_target_pairs={{0,8},{8,0},{16,24},{24,16},{32,40},{40,32},{48,56},{56,48},{64,72... | collective-permute-start | bytes 712712 | tf_op jit(solution)/shard_map/ppermute | solution.py:450
  59.8 0.0 copy-start.2
  59.8 0.7 shard_map.166.keep
  60.5 0.4 collective-permute-done.4.got
  61.0 0.1 shard_map.167
  61.0 10.5 %all_to_all.33.parts = bf16[8,16,1024]{2,1,0:T(8,128)(2,1)S(1)} all-to-all(bf16[8,16,1024]{2,1,0:T(8,128)(2,1)S(1)} %shard_map.167), channel_id=1, replica_groups={{0,16,32,48,64,80,96,112},{8,24,40,56,72,88,104,120},{1,17,33,49,65,81,..., dimensions={0} | all-to-all | bytes 524288 | tf_op jit(solution)/shard_map/all_to_all | solution.py:453
  71.6 0.1 shard_map.168
  71.7 10.0 %all_to_all.34.acts = bf16[8,16,512]{2,1,0:T(8,128)(2,1)S(1)} all-to-all(bf16[8,16,512]{2,1,0:T(8,128)(2,1)S(1)} %shard_map.168), channel_id=1, replica_groups={{0,16,32,48,64,80,96,112},{8,24,40,56,72,88,104,120},{1,17,33,49,65,81,..., dimensions={0} | all-to-all | bytes 262144 | tf_op jit(solution)/shard_map/all_to_all | solution.py:453
  81.7 2.6 %collective-permute-start.5 = (bf16[8,16,512]{2,1,0:T(8,128)(2,1)S(1)}, bf16[8,16,512]{2,1,0:T(8,128)(2,1)S(1)}, u32[]{:S(2)}, u32[]{:S(2)}) collective-permute-start(bf16[8,16,512]{2,1,0:T(8,128)(2,1)S(1)} %all_to_all.34.acts), channel_id=1, source_target_pairs={{0,8},{8,0},{16,24},{24,16},{32,40},{40,32},{48,56},{56,48},{64,72... | collective-permute-start | bytes 393224 | tf_op jit(solution)/shard_map/ppermute | solution.py:450
  84.3 0.0 copy-done.2
  84.3 0.4 shard_map.169.own
  84.7 0.6 collective-permute-done.5.acts
  85.3 0.4 shard_map.170
  85.7 9.5 %all_to_all.35.parts = bf16[8,32,512]{2,1,0:T(8,128)(2,1)S(1)} all-to-all(bf16[8,32,512]{2,1,0:T(8,128)(2,1)S(1)} %shard_map.170), channel_id=1, replica_groups=mesh['seq'=16,'tp'=8] {'tp'}, dimensions={0} | all-to-all | bytes 524288 | tf_op jit(solution)/shard_map/all_to_all | solution.py:456
  95.1 0.7 shard_map.171
  (1 shorter events, 0.0 us)
Async XLA Ops:
  2.4 2.4 %collective-permute-start = (f32[32,768]{1,0:T(8,128)S(1)}, f32[32,768]{1,0:T(8,128)S(1)}, u32[]{:S(2)}, u32[]{:S(2)}) collective-permute-start(f32[32,768]{1,0:T(8,128)S(1)} %get-tuple-element.14), channel_id=1, source_target_pairs={{0,8},{8,0},{16,24},{24,16},{32,40},{40,32},{48,56},{56,48},{64,72... | collective-permute-start | bytes 294920 | tf_op jit(solution)/shard_map/ppermute | solution.py:450
  4.9 18.7 %copy-start.3 = (bf16[1,16384,128]{2,1,0:T(8,128)(2,1)S(1)}, bf16[1,16384,128]{2,1,0:T(8,128)(2,1)}, u32[]{:S(2)}) copy-start(bf16[1,16384,128]{2,1,0:T(8,128)(2,1)} %keys.1) | copy-start | bytes 12582916
  4.9 18.7 %copy-start.4 = (bf16[1,16384,128]{2,1,0:T(8,128)(2,1)S(1)}, bf16[1,16384,128]{2,1,0:T(8,128)(2,1)}, u32[]{:S(2)}) copy-start(bf16[1,16384,128]{2,1,0:T(8,128)(2,1)} %values.1) | copy-start | bytes 12582916
  4.9 18.7 %copy-start.8 = (s32[32]{0:T(128)S(1)}, s32[32]{0:T(128)}, u32[]{:S(2)}) copy-start(s32[32]{0:T(128)} %positions.1) | copy-start | bytes 388
  21.1 2.5 %collective-permute-start.1 = (bf16[144,128]{1,0:T(8,128)(2,1)S(1)}, bf16[144,128]{1,0:T(8,128)(2,1)S(1)}, u32[]{:S(2)}, u32[]{:S(2)}) collective-permute-start(bf16[144,128]{1,0:T(8,128)(2,1)S(1)} %shard_map.160.own), channel_id=1, source_target_pairs={{0,8},{8,0},{16,24},{24,16},{32,40},{40,32},{48,56},{56,48},{64,72... | collective-permute-start | bytes 110600 | tf_op jit(solution)/shard_map/ppermute | solution.py:450
  23.4 21.8 %copy-start.5 = (bf16[1024,512]{1,0:T(8,128)(2,1)S(1)}, bf16[1024,512]{1,0:T(8,128)(2,1)}, u32[]{:S(2)}) copy-start(bf16[1024,512]{1,0:T(8,128)(2,1)} %w_out.1) | copy-start | bytes 3145732
  23.4 33.7 %copy-start.6 = (bf16[32,512]{1,0:T(8,128)(2,1)S(1)}, bf16[32,512]{1,0:T(8,128)(2,1)}, u32[]{:S(2)}) copy-start(bf16[32,512]{1,0:T(8,128)(2,1)} %resid.3) | copy-start | bytes 98308
  23.4 33.7 %copy-start.7 = (bf16[512]{0:T(512)(128)(2,1)S(1)}, bf16[512]{0:T(512)(128)(2,1)}, u32[]{:S(2)}) copy-start(bf16[512]{0:T(512)(128)(2,1)} %gain.3) | copy-start | bytes 3076
  23.6 33.5 %copy-start = (bf16[512,3584]{1,0:T(8,128)(2,1)S(1)}, bf16[512,3584]{1,0:T(8,128)(2,1)}, u32[]{:S(2)}) copy-start(bf16[512,3584]{1,0:T(8,128)(2,1)} %w_gate.3) | copy-start | bytes 11010052
  23.6 33.5 %copy-start.1 = (bf16[512,3584]{1,0:T(8,128)(2,1)S(1)}, bf16[512,3584]{1,0:T(8,128)(2,1)}, u32[]{:S(2)}) copy-start(bf16[512,3584]{1,0:T(8,128)(2,1)} %w_up.3) | copy-start | bytes 11010052
  27.5 3.7 %collective-permute-start.2 = (f32[136,128]{1,0:T(8,128)S(1)}, f32[136,128]{1,0:T(8,128)S(1)}, u32[]{:S(2)}, u32[]{:S(2)}) collective-permute-start(f32[136,128]{1,0:T(8,128)S(1)} %get-tuple-element.18), channel_id=1, source_target_pairs={{0,8},{8,0},{16,24},{24,16},{32,40},{40,32},{48,56},{56,48},{64,72... | collective-permute-start | bytes 208904 | tf_op jit(solution)/shard_map/ppermute | solution.py:450
  42.8 2.4 %collective-permute-start.3 = (bf16[32,512]{1,0:T(8,128)(2,1)S(1)}, bf16[32,512]{1,0:T(8,128)(2,1)S(1)}, u32[]{:S(2)}, u32[]{:S(2)}) collective-permute-start(bf16[32,512]{1,0:T(8,128)(2,1)S(1)} %shard_map.163.own), channel_id=1, source_target_pairs={{0,8},{8,0},{16,24},{24,16},{32,40},{40,32},{48,56},{56,48},{64,72... | collective-permute-start | bytes 98312 | tf_op jit(solution)/shard_map/ppermute | solution.py:450
  58.3 2.6 %collective-permute-start.4 = (bf16[32,3712]{1,0:T(8,128)(2,1)S(1)}, bf16[32,3712]{1,0:T(8,128)(2,1)S(1)}, u32[]{:S(2)}, u32[]{:S(2)}) collective-permute-start(bf16[32,3712]{1,0:T(8,128)(2,1)S(1)} %get-tuple-element.22), channel_id=1, source_target_pairs={{0,8},{8,0},{16,24},{24,16},{32,40},{40,32},{48,56},{56,48},{64,72... | collective-permute-start | bytes 712712 | tf_op jit(solution)/shard_map/ppermute | solution.py:450
  59.8 24.4 %copy-start.2 = (bf16[3584,512]{1,0:T(8,128)(2,1)S(1)}, bf16[3584,512]{1,0:T(8,128)(2,1)}, u32[]{:S(2)}) copy-start(bf16[3584,512]{1,0:T(8,128)(2,1)} %w_down.3) | copy-start | bytes 11010052
  81.7 3.6 %collective-permute-start.5 = (bf16[8,16,512]{2,1,0:T(8,128)(2,1)S(1)}, bf16[8,16,512]{2,1,0:T(8,128)(2,1)S(1)}, u32[]{:S(2)}, u32[]{:S(2)}) collective-permute-start(bf16[8,16,512]{2,1,0:T(8,128)(2,1)S(1)} %all_to_all.34.acts), channel_id=1, source_target_pairs={{0,8},{8,0},{16,24},{24,16},{32,40},{40,32},{48,56},{56,48},{64,72... | collective-permute-start | bytes 393224 | tf_op jit(solution)/shard_map/ppermute | solution.py:450

commit v4 on v3

--- a/solution.py
+++ b/solution.py
@@ -22,16 +22,15 @@
 HBM = pl.BlockSpec(memory_space=pltpu.HBM)
 
 
-def call(kernel, out_shape, in_specs, scratch=(), limit=4, moved=0):
+def call(kernel, out_shape, in_specs, scratch=(), limit=4, out_specs=None):
     many = isinstance(out_shape, (tuple, list))
     inner = pl.pallas_call(
         kernel,
         out_shape=out_shape,
         in_specs=in_specs,
-        out_specs=[VMEM] * len(out_shape) if many else VMEM,
+        out_specs=out_specs or ([VMEM] * len(out_shape) if many else VMEM),
         scratch_shapes=list(scratch),
         compiler_params=pltpu.CompilerParams(vmem_limit_bytes=limit << 20),
-        cost_estimate=pl.CostEstimate(flops=0, bytes_accessed=moved, transcendentals=0) if moved else None,
     )
 
     def run(*args):
@@ -116,13 +115,18 @@
     x32 = x_buf[...].astype(F32)
     x = (x32 * gain_buf[...].astype(F32)[None, :]).astype(BF16)
     square = jnp.broadcast_to(jnp.sum(x32 * x32, axis=1, keepdims=True), (32, LANES))
-    for load in loads[3:]:
-        load.wait()
+    loads[3].wait()
+    loads[4].wait()
     for target, half in ((keep, mine), (send, 1 - mine)):
-        cols = pl.ds(pl.multiple_of(half * 512, LANES), 512)
-        target[:, 0:512] = dot(x, q_buf[:, cols])
         target[:, 512:640] = dot(x, kv_buf[half])
         target[:, 640:768] = square
+    total = jnp.zeros((32, 1024), F32)
+    for i in range(4):
+        loads[5 + i].wait()
+        total += dot(x[:, i * 128 : (i + 1) * 128], q_buf[i * 128 : (i + 1) * 128, :])
+    first, second = total[:, 0:512], total[:, 512:1024]
+    keep[:, 0:512] = jnp.where(mine == 0, first, second)
+    send[:, 0:512] = jnp.where(mine == 0, second, first)
 
 
 def project_pair_kernel(own, other, w1, w2, w3, copies):
@@ -158,12 +162,13 @@
     rows += [jnp.exp2(tail[11:12]) * (inv / FULL) for tail in tails]
     turned = jnp.transpose(jnp.concatenate(rows + [jnp.zeros((112, LANES), F32)], axis=0))
     steps[...] = turned[0:32]
+    wide = [jnp.broadcast_to(turned[0:32, j : j + 1], (32, LANES)) for j in range(8)]
 
     for g in range(4):
         x = jnp.zeros((32, LANES), F32)
         for j in range(8):
             head = parts[j, g * 32 : (g + 1) * 32, :].astype(jnp.int32).astype(F32)
-            x += head * steps[:, j : j + 1]
+            x += head * wide[j]
         out[g * 32 : (g + 1) * 32, :] = (x * cos[...] + pltpu.roll(x, LANES // 2, 1) * sin[...]).astype(BF16)
 
     chip = chip_index()
@@ -260,6 +265,22 @@
         def _():
             run(pl.multiple_of(jnp.where(half_full, CHUNK, 0), CHUNK), CHUNK // PIECE, True)
 
+    def finish():
+        l_old = jnp.sum(total_l[...], axis=0, keepdims=True)
+        lse_old = shift[0:1, :] * math.log(2.0) + jnp.log(l_old)
+        lse_new = new_lse[0:1, :]
+        high = jnp.maximum(lse_old, lse_new)
+        f_old = jnp.exp(lse_old - high)
+        f_new = jnp.exp(lse_new - high)
+        both = f_old + f_new
+        o = total_o[...] * (f_old / (l_old * both)) + new_o[...] * (f_new / both)
+        lse = jnp.broadcast_to(high + jnp.log(both), (8, 256))
+        for target, first in ((keep, mine == 0), (send, mine != 0)):
+            target[0:128, :] = jnp.where(first, o[:, 0:128], o[:, 128:256])
+            target[128:136, :] = jnp.where(first, lse[:, 0:128], lse[:, 128:256])
+
+    finish()
+
     @pl.when(jnp.logical_not(jnp.max(total_l[...]) < 1e30))
     def _():
         pieces = lax.div(length + (PIECE - 1), PIECE)
@@ -277,19 +298,7 @@
         def _(c):
             run(pl.multiple_of(c * PIECE, PIECE), 1, True)
 
-    l_old = jnp.sum(total_l[...], axis=0, keepdims=True)
-    lse_old = shift[0:1, :] * math.log(2.0) + jnp.log(l_old)
-
-    lse_new = new_lse[0:1, :]
-    high = jnp.maximum(lse_old, lse_new)
-    f_old = jnp.exp(lse_old - high)
-    f_new = jnp.exp(lse_new - high)
-    both = f_old + f_new
-    o = total_o[...] * (f_old / (l_old * both)) + new_o[...] * (f_new / both)
-    lse = jnp.broadcast_to(high + jnp.log(both), (8, 256))
-    for target, first in ((keep, mine == 0), (send, mine != 0)):
-        target[0:128, :] = jnp.where(first, o[:, 0:128], o[:, 128:256])
-        target[128:136, :] = jnp.where(first, lse[:, 0:128], lse[:, 128:256])
+        finish()
 
 
 def merge_pair_kernel(own, other, copies):
@@ -351,9 +360,9 @@
         target[:, 1792 + i * 896 : 1792 + (i + 1) * 896] = dot(x, w_up[:, cols]).astype(target.dtype)
 
 
-def gate_up_send_kernel(parts, resid, gain, w_gate, w_up, attn_out, mid, normed, square, send):
+def gate_up_send_kernel(parts, resid, gain, w_gate, w_up, branch_out, mid, normed, square, send):
     branch = sum_parts(parts).astype(BF16)
-    attn_out[...] = branch
+    branch_out[...] = branch
     hidden = (resid[...].astype(F32) + branch.astype(F32)).astype(BF16)
     mid[...] = hidden
     x32 = hidden.astype(F32)
@@ -365,8 +374,11 @@
     send[:, 3584:3712] = lane_split(total)
 
 
-def gate_up_keep_kernel(normed, w_gate, w_up, keep):
+def gate_up_keep_kernel(normed, branch, w_gate, w_up, keep, attn_out, sem):
+    out = pltpu.make_async_copy(branch, attn_out, sem)
+    out.start()
     gate_up(normed[...], w_gate, w_up, core_index(), keep)
+    out.wait()
 
 
 def gate_up_pair_kernel(keep, own_square, got, pieces):
@@ -495,14 +507,21 @@
     copies = call(out_kernel, near((8, 32, 512), BF16), [VMEM] * 3)(attn, to_other_core(attn), w_out)
     parts = over_tp(copies)
 
-    attn_out, mid, normed, square, send = call(
+    branch, mid, normed, square, send = call(
         gate_up_send_kernel,
-        (shape((32, 512), BF16), near((32, 512), BF16), near((32, 512), BF16), table, near((32, 3712), BF16)),
+        (near((32, 512), BF16), near((32, 512), BF16), near((32, 512), BF16), table, near((32, 3712), BF16)),
         [VMEM] * 5,
         limit=12,
     )(parts, resid, ffn_gain, w_gate, w_up)
     got = to_other_core(send)
-    keep = call(gate_up_keep_kernel, near((32, 3584), F32), [VMEM] * 3, limit=12)(normed, w_gate, w_up)
+    keep, attn_out = call(
+        gate_up_keep_kernel,
+        (near((32, 3584), F32), shape((32, 512), BF16)),
+        [VMEM] * 4,
+        scratch=[pltpu.SemaphoreType.DMA],
+        limit=12,
+        out_specs=[VMEM, HBM],
+    )(normed, branch, w_gate, w_up)
     pieces = call(gate_up_pair_kernel, near((8, 16, 1024), BF16), [VMEM] * 3)(keep, square, got)
     parts = over_chips(pieces)
     copies = call(act_kernel, near((8, 16, 512), BF16), [VMEM])(parts)

time: 96.2 us -> 95.3 us (level)
  starting transfers between devices: 11.5 us -> 9.02 us
  Pallas kernels: 10.5 us -> 11.9 us
    ppermute x6, starting transfers between devices: 11.5 us -> 9.02 us  [to_other_core(): return lax.ppermute(x, 'seq', swap)]
    pallas_call x14, Pallas kernels: 10.5 us -> 11.9 us  [run(): inner(*(pltpu.with_memory_space_constraint(x, pltpu.HBM) if s is HBM else...]
where the time goes in v4:
time: 95.3 us; the launch traced here: 94.9 us
  blocking collectives  68.3 us (72%)
  Pallas kernels  11.9 us (12%)
  starting transfers between devices  9.02 us (9%)
  waiting for transfers between devices  4.2 us (4%)
  between operations  1.43 us (2%)
    all_to_all x4, blocking collectives, over_chips(): return lax.all_to_all(x, 'seq', 0, 0, axis_index_groups=same_core)  47.3 us
    all_to_all x2, blocking collectives, over_tp(): return lax.all_to_all(x, 'tp', 0, 0)  21 us
    pallas_call x14, Pallas kernels, run(): inner(*(pltpu.with_memory_space_constraint(x, pltpu.HBM) if s is HBM else...  11.9 us
    ppermute x6, starting transfers between devices, to_other_core(): return lax.ppermute(x, 'seq', swap)  9.02 us
    ppermute x6, waiting for transfers between devices, to_other_core(): return lax.ppermute(x, 'seq', swap)  4.2 us
  transfers between devices with their start and end apart: 6, of which 6 were waited for; matrix products, arithmetic and copies ran while one was open for 0% of the time, Pallas kernels for 1%

profile of v4, /device:TPU:1, one launch (start us, length us, event | category | flops | bytes accessed | tf_op | source)
XLA Modules:
  0.0 94.9 jit_solution(6665659767141767002)
XLA Ops:
  0.6 1.6 %shard_map.158 = (f32[32,768]{1,0:T(8,128)S(1)}, f32[32,768]{1,0:T(8,128)S(1)}, f32[32,128]{1,0:T(8,128)S(1)}, f32[32,128]{1,0:T(8,128)S(1)}) custom-call(bf16[32,512]{1,0:T(8,128)(2,1)} %resid.3, bf16[512]{0:T(512)(128)(2,1)} %gain.2, bf16[512,1024]{1,0:T(8,128)(2,1)} %w_query.1, bf16[512,128]{1,0:T(8,128)(2,1)} %w_key.1, bf16[512,128]{1,0:T(8,128)(2,1)} %w_value.1, ...), custom_call_target="tpu_custom_call" | custom-call | tf_op jit(solution)/shard_map/pallas_call | solution.py:37
  2.3 1.5 %collective-permute-start = (f32[32,768]{1,0:T(8,128)S(1)}, f32[32,768]{1,0:T(8,128)S(1)}, u32[]{:S(2)}, u32[]{:S(2)}) collective-permute-start(f32[32,768]{1,0:T(8,128)S(1)} %get-tuple-element.16), channel_id=1, source_target_pairs={{0,8},{8,0},{16,24},{24,16},{32,40},{40,32},{48,56},{56,48},{64,72... | collective-permute-start | bytes 294920 | tf_op jit(solution)/shard_map/ppermute | solution.py:462
  3.8 0.9 collective-permute-done.other
  4.7 0.0 copy-start.3
  4.7 0.0 copy-start.4
  4.7 0.0 copy-start.8
  4.7 0.2 shard_map.159
  4.9 15.5 %all_to_all.30.parts = s16[8,144,128]{2,1,0:T(8,128)(2,1)S(1)} all-to-all(s16[8,144,128]{2,1,0:T(8,128)(2,1)S(1)} %shard_map.159), channel_id=1, replica_groups={{0,16,32,48,64,80,96,112},{8,24,40,56,72,88,104,120},{1,17,33,49,65,81,..., dimensions={0} | all-to-all | bytes 589824 | tf_op jit(solution)/shard_map/all_to_all | solution.py:465
  20.3 0.3 shard_map.160.own
  20.7 1.7 %collective-permute-start.1 = (bf16[144,128]{1,0:T(8,128)(2,1)S(1)}, bf16[144,128]{1,0:T(8,128)(2,1)S(1)}, u32[]{:S(2)}, u32[]{:S(2)}) collective-permute-start(bf16[144,128]{1,0:T(8,128)(2,1)S(1)} %shard_map.160.own), channel_id=1, source_target_pairs={{0,8},{8,0},{16,24},{24,16},{32,40},{40,32},{48,56},{56,48},{64,72... | collective-permute-start | bytes 110600 | tf_op jit(solution)/shard_map/ppermute | solution.py:462
  23.0 0.0 copy-start.5
  23.0 0.0 copy-start.6
  23.0 0.0 copy-start.7
  23.0 0.2 collective-permute-done.1.other
  23.2 0.0 copy-done.3
  23.2 0.0 copy-done.4
  23.2 0.0 copy-done.8
  23.2 0.0 copy-start
  23.2 0.0 copy-start.1
  23.2 6.2 %shard_map.161 = (f32[136,128]{1,0:T(8,128)S(1)}, f32[136,128]{1,0:T(8,128)S(1)}) custom-call(bf16[144,128]{1,0:T(8,128)(2,1)S(1)} %shard_map.160.own, bf16[144,128]{1,0:T(8,128)(2,1)S(1)} %collective-permute-done.1.other, s32[32]{0:T(128)S(1)} %copy-done.8, s32[1]{0:T(128)S(6)} %copy.17.valid, bf16[1,16384,128]{2,1,0:T(8,128)(2,1)S(1)} %copy-done.3, ...), custom_call_target="tpu_custom_call" | custom-call | tf_op jit(solution)/shard_map/pallas_call | solution.py:37
  29.4 0.1 collective-permute-start.2
  29.5 1.2 %collective-permute-done.2.other = f32[136,128]{1,0:T(8,128)S(1)} collective-permute-done((f32[136,128]{1,0:T(8,128)S(1)}, f32[136,128]{1,0:T(8,128)S(1)}, u32[]{:S(2)}, u32[]{:S(2)}) %collective-permute-start.2) | collective-permute-done | bytes 69664 | tf_op jit(solution)/shard_map/ppermute | solution.py:462
  30.8 11.3 %all_to_all.31.parts = bf16[8,144,128]{2,1,0:T(8,128)(2,1)S(1)} all-to-all(bf16[8,144,128]{2,1,0:T(8,128)(2,1)S(1)} %shard_map.162), channel_id=1, replica_groups={{0,16,32,48,64,80,96,112},{8,24,40,56,72,88,104,120},{1,17,33,49,65,81,..., dimensions={0} | all-to-all | bytes 589824 | tf_op jit(solution)/shard_map/all_to_all | solution.py:465
  42.1 0.2 shard_map.163.own
  42.3 1.6 %collective-permute-start.3 = (bf16[32,512]{1,0:T(8,128)(2,1)S(1)}, bf16[32,512]{1,0:T(8,128)(2,1)S(1)}, u32[]{:S(2)}, u32[]{:S(2)}) collective-permute-start(bf16[32,512]{1,0:T(8,128)(2,1)S(1)} %shard_map.163.own), channel_id=1, source_target_pairs={{0,8},{8,0},{16,24},{24,16},{32,40},{40,32},{48,56},{56,48},{64,72... | collective-permute-start | bytes 98312 | tf_op jit(solution)/shard_map/ppermute | solution.py:462
  43.9 0.9 collective-permute-done.3.other
  44.7 0.0 copy-done.5
  44.7 0.3 shard_map.164
  45.1 11.6 %all_to_all.32.parts = bf16[8,32,512]{2,1,0:T(8,128)(2,1)S(1)} all-to-all(bf16[8,32,512]{2,1,0:T(8,128)(2,1)S(1)} %shard_map.164), channel_id=1, replica_groups=mesh['seq'=16,'tp'=8] {'tp'}, dimensions={0} | all-to-all | bytes 524288 | tf_op jit(solution)/shard_map/all_to_all | solution.py:468
  56.6 0.0 copy-done.6
  56.6 0.0 copy-done.7
  56.6 0.0 copy-done
  56.7 0.0 copy-done.1
  56.7 0.7 shard_map.165
  57.4 1.6 %collective-permute-start.4 = (bf16[32,3712]{1,0:T(8,128)(2,1)S(1)}, bf16[32,3712]{1,0:T(8,128)(2,1)S(1)}, u32[]{:S(2)}, u32[]{:S(2)}) collective-permute-start(bf16[32,3712]{1,0:T(8,128)(2,1)S(1)} %get-tuple-element.26), channel_id=1, source_target_pairs={{0,8},{8,0},{16,24},{24,16},{32,40},{40,32},{48,56},{56,48},{64,72... | collective-permute-start | bytes 712712 | tf_op jit(solution)/shard_map/ppermute | solution.py:462
  59.0 0.0 copy-start.2
  59.0 0.7 shard_map.166
  59.7 0.4 collective-permute-done.4.got
  60.1 0.1 shard_map.167
  60.2 10.5 %all_to_all.33.parts = bf16[8,16,1024]{2,1,0:T(8,128)(2,1)S(1)} all-to-all(bf16[8,16,1024]{2,1,0:T(8,128)(2,1)S(1)} %shard_map.167), channel_id=1, replica_groups={{0,16,32,48,64,80,96,112},{8,24,40,56,72,88,104,120},{1,17,33,49,65,81,..., dimensions={0} | all-to-all | bytes 524288 | tf_op jit(solution)/shard_map/all_to_all | solution.py:465
  70.7 0.1 shard_map.168
  70.8 10.0 %all_to_all.34.acts = bf16[8,16,512]{2,1,0:T(8,128)(2,1)S(1)} all-to-all(bf16[8,16,512]{2,1,0:T(8,128)(2,1)S(1)} %shard_map.168), channel_id=1, replica_groups={{0,16,32,48,64,80,96,112},{8,24,40,56,72,88,104,120},{1,17,33,49,65,81,..., dimensions={0} | all-to-all | bytes 262144 | tf_op jit(solution)/shard_map/all_to_all | solution.py:465
  80.8 2.6 %collective-permute-start.5 = (bf16[8,16,512]{2,1,0:T(8,128)(2,1)S(1)}, bf16[8,16,512]{2,1,0:T(8,128)(2,1)S(1)}, u32[]{:S(2)}, u32[]{:S(2)}) collective-permute-start(bf16[8,16,512]{2,1,0:T(8,128)(2,1)S(1)} %all_to_all.34.acts), channel_id=1, source_target_pairs={{0,8},{8,0},{16,24},{24,16},{32,40},{40,32},{48,56},{56,48},{64,72... | collective-permute-start | bytes 393224 | tf_op jit(solution)/shard_map/ppermute | solution.py:462
  83.4 0.0 copy-done.2
  83.4 0.4 shard_map.169.own
  83.8 0.6 collective-permute-done.5.acts
  84.4 0.4 shard_map.170
  84.8 9.5 %all_to_all.35.parts = bf16[8,32,512]{2,1,0:T(8,128)(2,1)S(1)} all-to-all(bf16[8,32,512]{2,1,0:T(8,128)(2,1)S(1)} %shard_map.170), channel_id=1, replica_groups=mesh['seq'=16,'tp'=8] {'tp'}, dimensions={0} | all-to-all | bytes 524288 | tf_op jit(solution)/shard_map/all_to_all | solution.py:468
  94.3 0.7 shard_map.171
  (1 shorter events, 0.0 us)
Async XLA Ops:
  2.3 2.4 %collective-permute-start = (f32[32,768]{1,0:T(8,128)S(1)}, f32[32,768]{1,0:T(8,128)S(1)}, u32[]{:S(2)}, u32[]{:S(2)}) collective-permute-start(f32[32,768]{1,0:T(8,128)S(1)} %get-tuple-element.16), channel_id=1, source_target_pairs={{0,8},{8,0},{16,24},{24,16},{32,40},{40,32},{48,56},{56,48},{64,72... | collective-permute-start | bytes 294920 | tf_op jit(solution)/shard_map/ppermute | solution.py:462
  4.7 18.5 %copy-start.3 = (bf16[1,16384,128]{2,1,0:T(8,128)(2,1)S(1)}, bf16[1,16384,128]{2,1,0:T(8,128)(2,1)}, u32[]{:S(2)}) copy-start(bf16[1,16384,128]{2,1,0:T(8,128)(2,1)} %keys.1) | copy-start | bytes 12582916
  4.7 18.5 %copy-start.4 = (bf16[1,16384,128]{2,1,0:T(8,128)(2,1)S(1)}, bf16[1,16384,128]{2,1,0:T(8,128)(2,1)}, u32[]{:S(2)}) copy-start(bf16[1,16384,128]{2,1,0:T(8,128)(2,1)} %values.1) | copy-start | bytes 12582916
  4.7 18.5 %copy-start.8 = (s32[32]{0:T(128)S(1)}, s32[32]{0:T(128)}, u32[]{:S(2)}) copy-start(s32[32]{0:T(128)} %positions.1) | copy-start | bytes 388
  20.7 2.5 %collective-permute-start.1 = (bf16[144,128]{1,0:T(8,128)(2,1)S(1)}, bf16[144,128]{1,0:T(8,128)(2,1)S(1)}, u32[]{:S(2)}, u32[]{:S(2)}) collective-permute-start(bf16[144,128]{1,0:T(8,128)(2,1)S(1)} %shard_map.160.own), channel_id=1, source_target_pairs={{0,8},{8,0},{16,24},{24,16},{32,40},{40,32},{48,56},{56,48},{64,72... | collective-permute-start | bytes 110600 | tf_op jit(solution)/shard_map/ppermute | solution.py:462
  23.0 21.7 %copy-start.5 = (bf16[1024,512]{1,0:T(8,128)(2,1)S(1)}, bf16[1024,512]{1,0:T(8,128)(2,1)}, u32[]{:S(2)}) copy-start(bf16[1024,512]{1,0:T(8,128)(2,1)} %w_out.1) | copy-start | bytes 3145732
  23.0 33.6 %copy-start.6 = (bf16[32,512]{1,0:T(8,128)(2,1)S(1)}, bf16[32,512]{1,0:T(8,128)(2,1)}, u32[]{:S(2)}) copy-start(bf16[32,512]{1,0:T(8,128)(2,1)} %resid.3) | copy-start | bytes 98308
  23.0 33.6 %copy-start.7 = (bf16[512]{0:T(512)(128)(2,1)S(1)}, bf16[512]{0:T(512)(128)(2,1)}, u32[]{:S(2)}) copy-start(bf16[512]{0:T(512)(128)(2,1)} %gain.3) | copy-start | bytes 3076
  23.2 33.4 %copy-start = (bf16[512,3584]{1,0:T(8,128)(2,1)S(1)}, bf16[512,3584]{1,0:T(8,128)(2,1)}, u32[]{:S(2)}) copy-start(bf16[512,3584]{1,0:T(8,128)(2,1)} %w_gate.3) | copy-start | bytes 11010052
  23.2 33.4 %copy-start.1 = (bf16[512,3584]{1,0:T(8,128)(2,1)S(1)}, bf16[512,3584]{1,0:T(8,128)(2,1)}, u32[]{:S(2)}) copy-start(bf16[512,3584]{1,0:T(8,128)(2,1)} %w_up.3) | copy-start | bytes 11010052
  29.4 1.3 %collective-permute-start.2 = (f32[136,128]{1,0:T(8,128)S(1)}, f32[136,128]{1,0:T(8,128)S(1)}, u32[]{:S(2)}, u32[]{:S(2)}) collective-permute-start(f32[136,128]{1,0:T(8,128)S(1)} %get-tuple-element.20), channel_id=1, source_target_pairs={{0,8},{8,0},{16,24},{24,16},{32,40},{40,32},{48,56},{56,48},{64,72... | collective-permute-start | bytes 208904 | tf_op jit(solution)/shard_map/ppermute | solution.py:462
  42.3 2.4 %collective-permute-start.3 = (bf16[32,512]{1,0:T(8,128)(2,1)S(1)}, bf16[32,512]{1,0:T(8,128)(2,1)S(1)}, u32[]{:S(2)}, u32[]{:S(2)}) collective-permute-start(bf16[32,512]{1,0:T(8,128)(2,1)S(1)} %shard_map.163.own), channel_id=1, source_target_pairs={{0,8},{8,0},{16,24},{24,16},{32,40},{40,32},{48,56},{56,48},{64,72... | collective-permute-start | bytes 98312 | tf_op jit(solution)/shard_map/ppermute | solution.py:462
  57.4 2.7 %collective-permute-start.4 = (bf16[32,3712]{1,0:T(8,128)(2,1)S(1)}, bf16[32,3712]{1,0:T(8,128)(2,1)S(1)}, u32[]{:S(2)}, u32[]{:S(2)}) collective-permute-start(bf16[32,3712]{1,0:T(8,128)(2,1)S(1)} %get-tuple-element.26), channel_id=1, source_target_pairs={{0,8},{8,0},{16,24},{24,16},{32,40},{40,32},{48,56},{56,48},{64,72... | collective-permute-start | bytes 712712 | tf_op jit(solution)/shard_map/ppermute | solution.py:462
  59.0 24.4 %copy-start.2 = (bf16[3584,512]{1,0:T(8,128)(2,1)S(1)}, bf16[3584,512]{1,0:T(8,128)(2,1)}, u32[]{:S(2)}) copy-start(bf16[3584,512]{1,0:T(8,128)(2,1)} %w_down.3) | copy-start | bytes 11010052
  80.8 3.6 %collective-permute-start.5 = (bf16[8,16,512]{2,1,0:T(8,128)(2,1)S(1)}, bf16[8,16,512]{2,1,0:T(8,128)(2,1)S(1)}, u32[]{:S(2)}, u32[]{:S(2)}) collective-permute-start(bf16[8,16,512]{2,1,0:T(8,128)(2,1)S(1)} %all_to_all.34.acts), channel_id=1, source_target_pairs={{0,8},{8,0},{16,24},{24,16},{32,40},{40,32},{48,56},{56,48},{64,72... | collective-permute-start | bytes 393224 | tf_op jit(solution)/shard_map/ppermute | solution.py:462

commit v5 on v4

--- a/solution.py
+++ b/solution.py
@@ -10,8 +10,6 @@
 
 EPS = 1e-05
 LOW = -1e30
-TINY = 1e-30
-FULL = 32766.0
 F32 = jnp.float32
 BF16 = jnp.bfloat16
 LANES = 128
@@ -131,44 +129,25 @@
 
 def project_pair_kernel(own, other, w1, w2, w3, copies):
     total = own[...] + other[...]
-    row_log = jnp.log2(total[:, 640:768] + TINY)
-    meta = [jnp.floor(row_log * 256 + 0.5)]
-    meta.append(jnp.floor((row_log * 256 - meta[0]) * 16384 + 0.5))
-    coded = []
-    for cols in (slice(0, 512), slice(512, 640)):
-        x = total[:, cols]
-        grade = jnp.ceil(jnp.log2(jnp.max(jnp.abs(x), axis=1, keepdims=True) + TINY))
-        coded.append(jnp.floor(x * (FULL * jnp.exp2(-grade)) + 0.5))
-        meta.append(jnp.broadcast_to(grade, (32, LANES)))
-    lane = lax.broadcasted_iota(jnp.int32, (32, LANES), 1)
-    last = jnp.where(lane < 2, jnp.where(lane == 0, meta[0], meta[1]), jnp.where(lane == 2, meta[2], meta[3]))
-    last = jnp.transpose(jnp.concatenate([last, jnp.zeros((96, LANES), F32)], axis=0))[0:8]
-    heads = jnp.concatenate([coded[0][:, g * 128 : (g + 1) * 128] for g in range(4)], axis=0)
-    heads = heads.astype(jnp.int32).astype(jnp.int16)
-    for j in range(8):
-        four = coded[1][j // 2 * 8 : j // 2 * 8 + 8]
+    square = jnp.transpose(jnp.concatenate([total[:, 640:768], jnp.zeros((96, LANES), F32)], axis=0))[0:8]
+    heads = jnp.concatenate([total[:, g * 128 : (g + 1) * 128] for g in range(4)], axis=0)
+    row = lax.broadcasted_iota(jnp.int32, (8, LANES), 0)
+    for j in range(8):
+        four = total[j // 2 * 8 : j // 2 * 8 + 8, 512:640]
         four = pltpu.roll(four, 4, 0) if j % 2 else four
         copies[j, 0:128, :] = heads
-        copies[j, 128:144, :] = jnp.concatenate([four, last], axis=0).astype(jnp.int32).astype(jnp.int16)
-
-
-def rotate_kernel(parts, cos, sin, out, steps):
-    tails = [parts[j, 128:144, :].astype(jnp.int32).astype(F32) for j in range(8)]
-    square = jnp.zeros((1, LANES), F32)
-    for tail in tails:
-        square += jnp.exp2(tail[8:9] / 256 + tail[9:10] / (256 * 16384))
-    inv = lax.rsqrt(square / 8192 + EPS)
-    rows = [jnp.exp2(tail[10:11]) * (inv / FULL) for tail in tails]
-    rows += [jnp.exp2(tail[11:12]) * (inv / FULL) for tail in tails]
-    turned = jnp.transpose(jnp.concatenate(rows + [jnp.zeros((112, LANES), F32)], axis=0))
-    steps[...] = turned[0:32]
-    wide = [jnp.broadcast_to(turned[0:32, j : j + 1], (32, LANES)) for j in range(8)]
+        copies[j, 128:136, :] = jnp.where(row < 4, four, square)
+
+
+def rotate_kernel(parts, cos, sin, out, factor):
+    total = sum_parts(parts)
+    tail = total[128:136]
+    inv = jnp.broadcast_to(lax.rsqrt(tail[4:5] / 8192 + EPS), (LANES, LANES))
+    inv = jnp.transpose(inv)[0:32]
+    factor[...] = inv
 
     for g in range(4):
-        x = jnp.zeros((32, LANES), F32)
-        for j in range(8):
-            head = parts[j, g * 32 : (g + 1) * 32, :].astype(jnp.int32).astype(F32)
-            x += head * wide[j]
+        x = total[g * 32 : (g + 1) * 32] * inv
         out[g * 32 : (g + 1) * 32, :] = (x * cos[...] + pltpu.roll(x, LANES // 2, 1) * sin[...]).astype(BF16)
 
     chip = chip_index()
@@ -178,10 +157,7 @@
         x = ref[base, :]
         return jnp.where(lax.rem(chip, 2) == 0, x, pltpu.roll(x, 4, 0))
 
-    step = four(steps)
-    x = jnp.zeros((8, LANES), F32)
-    for j in range(8):
-        x += tails[j][0:8] * step[:, 8 + j : 9 + j]
+    x = tail * four(factor)
     key = x * four(cos) + pltpu.roll(x, LANES // 2, 1) * four(sin)
     x = jnp.where(core_index() == 0, key, x)
     out[128:144, :] = jnp.concatenate([x, jnp.zeros((8, LANES), F32)], axis=0).astype(BF16)
@@ -336,12 +312,16 @@
         attn[:, g * 128 : (g + 1) * 128] = total[g * 32 : (g + 1) * 32].astype(BF16)
 
 
-def out_kernel(own, other, w_out, copies):
-    mine = core_index()
-    total = jnp.zeros((32, 512), F32)
-    for source, half in ((own, mine), (other, 1 - mine)):
-        total += dot(source[...], w_out[pl.ds(pl.multiple_of(half * 512, LANES), 512), :])
-    part = total.astype(BF16)
+def out_half(attn, w_out, half):
+    return dot(attn[...], w_out[pl.ds(pl.multiple_of(half * 512, LANES), 512), :])
+
+
+def out_own_kernel(attn, w_out, part):
+    part[...] = out_half(attn, w_out, core_index())
+
+
+def out_other_kernel(own, attn, w_out, copies):
+    part = (own[...] + out_half(attn, w_out, 1 - core_index())).astype(BF16)
     for j in range(8):
         copies[j] = part
 
@@ -481,7 +461,7 @@
             pltpu.SemaphoreType.DMA((9,)),
         ],
     )(resid, attn_gain, w_query, w_key, w_value, rope_angle)
-    copies = call(project_pair_kernel, near((8, 144, LANES), jnp.int16), [VMEM] * 2 + [HBM] * 3)(
+    copies = call(project_pair_kernel, near((8, 136, LANES), F32), [VMEM] * 2 + [HBM] * 3)(
         keep, to_other_core(send), w_gate, w_up, w_down
     )
     turned = call(rotate_kernel, near((144, LANES), BF16), [VMEM] * 3, scratch=[pltpu.VMEM((32, LANES), F32)])(
@@ -504,7 +484,9 @@
     )(turned, to_other_core(turned), positions, valid_lengths, cache_keys, cache_values)
     copies = call(merge_pair_kernel, near((8, 144, LANES), BF16), [VMEM] * 2)(keep, to_other_core(send))
     attn = call(merge_kernel, near((32, 512), BF16), [VMEM])(over_chips(copies))
-    copies = call(out_kernel, near((8, 32, 512), BF16), [VMEM] * 3)(attn, to_other_core(attn), w_out)
+    got = to_other_core(attn)
+    part = call(out_own_kernel, near((32, 512), F32), [VMEM] * 2)(attn, w_out)
+    copies = call(out_other_kernel, near((8, 32, 512), BF16), [VMEM] * 3)(part, got, w_out)
     parts = over_tp(copies)
 
     branch, mid, normed, square, send = call(

time: 95.3 us -> 97.8 us (1.026)
  blocking collectives: 68.3 us -> 71.2 us
  starting transfers between devices: 9.02 us -> 10.2 us
  Pallas kernels: 11.9 us -> 10.9 us
    all_to_all x4, blocking collectives: 47.3 us -> 50.2 us  [over_chips(): return lax.all_to_all(x, 'seq', 0, 0, axis_index_groups=same_core)]
    ppermute x6, starting transfers between devices: 9.02 us -> 10.2 us  [to_other_core(): return lax.ppermute(x, 'seq', swap)]
    pallas_call x14 -> x15, Pallas kernels: 11.9 us -> 10.9 us  [run(): inner(*(pltpu.with_memory_space_constraint(x, pltpu.HBM) if s is HBM else...]
where the time goes in v5:
time: 97.8 us; the launch traced here: 97.5 us
  blocking collectives  71.2 us (73%)
  Pallas kernels  10.9 us (11%)
  starting transfers between devices  10.2 us (10%)
  waiting for transfers between devices  3.7 us (4%)
  between operations  1.42 us (1%)
    all_to_all x4, blocking collectives, over_chips(): return lax.all_to_all(x, 'seq', 0, 0, axis_index_groups=same_core)  50.2 us
    all_to_all x2, blocking collectives, over_tp(): return lax.all_to_all(x, 'tp', 0, 0)  21 us
    pallas_call x15, Pallas kernels, run(): inner(*(pltpu.with_memory_space_constraint(x, pltpu.HBM) if s is HBM else...  10.9 us
    ppermute x6, starting transfers between devices, to_other_core(): return lax.ppermute(x, 'seq', swap)  10.2 us
    ppermute x6, waiting for transfers between devices, to_other_core(): return lax.ppermute(x, 'seq', swap)  3.7 us
  transfers between devices with their start and end apart: 6, of which 6 were waited for; matrix products, arithmetic and copies ran while one was open for 0% of the time, Pallas kernels for 1%

profile of v5, /device:TPU:1, one launch (start us, length us, event | category | flops | bytes accessed | tf_op | source)
XLA Modules:
  0.0 97.5 jit_solution(1648157343189545416)
XLA Ops:
  0.6 1.6 %shard_map.158 = (f32[32,768]{1,0:T(8,128)S(1)}, f32[32,768]{1,0:T(8,128)S(1)}, f32[32,128]{1,0:T(8,128)S(1)}, f32[32,128]{1,0:T(8,128)S(1)}) custom-call(bf16[32,512]{1,0:T(8,128)(2,1)} %resid.3, bf16[512]{0:T(512)(128)(2,1)} %gain.2, bf16[512,1024]{1,0:T(8,128)(2,1)} %w_query.1, bf16[512,128]{1,0:T(8,128)(2,1)} %w_key.1, bf16[512,128]{1,0:T(8,128)(2,1)} %w_value.1, ...), custom_call_target="tpu_custom_call" | custom-call | tf_op jit(solution)/shard_map/pallas_call | solution.py:35
  2.3 1.5 %collective-permute-start = (f32[32,768]{1,0:T(8,128)S(1)}, f32[32,768]{1,0:T(8,128)S(1)}, u32[]{:S(2)}, u32[]{:S(2)}) collective-permute-start(f32[32,768]{1,0:T(8,128)S(1)} %get-tuple-element.16), channel_id=1, source_target_pairs={{0,8},{8,0},{16,24},{24,16},{32,40},{40,32},{48,56},{56,48},{64,72... | collective-permute-start | bytes 294920 | tf_op jit(solution)/shard_map/ppermute | solution.py:442
  3.8 0.9 collective-permute-done.other
  4.7 0.0 copy-start.3
  4.7 0.0 copy-start.4
  4.7 0.0 copy-start.8
  4.7 0.1 shard_map.159
  4.8 18.3 %all_to_all.30.parts = f32[8,136,128]{2,1,0:T(8,128)S(1)} all-to-all(f32[8,136,128]{2,1,0:T(8,128)S(1)} %shard_map.159), channel_id=1, replica_groups={{0,16,32,48,64,80,96,112},{8,24,40,56,72,88,104,120},{1,17,33,49,65,81,..., dimensions={0} | all-to-all | bytes 1114112 | tf_op jit(solution)/shard_map/all_to_all | solution.py:445
  23.1 0.2 shard_map.160.own
  23.3 1.7 %collective-permute-start.1 = (bf16[144,128]{1,0:T(8,128)(2,1)S(1)}, bf16[144,128]{1,0:T(8,128)(2,1)S(1)}, u32[]{:S(2)}, u32[]{:S(2)}) collective-permute-start(bf16[144,128]{1,0:T(8,128)(2,1)S(1)} %shard_map.160.own), channel_id=1, source_target_pairs={{0,8},{8,0},{16,24},{24,16},{32,40},{40,32},{48,56},{56,48},{64,72... | collective-permute-start | bytes 110600 | tf_op jit(solution)/shard_map/ppermute | solution.py:442
  25.6 0.0 copy-start.5
  25.6 0.2 collective-permute-done.1.other
  25.8 0.0 copy-done.3
  25.8 0.0 copy-done.4
  25.8 0.0 copy-done.8
  25.8 0.0 copy-start.1
  25.8 5.3 %shard_map.161 = (f32[136,128]{1,0:T(8,128)S(1)}, f32[136,128]{1,0:T(8,128)S(1)}) custom-call(bf16[144,128]{1,0:T(8,128)(2,1)S(1)} %shard_map.160.own, bf16[144,128]{1,0:T(8,128)(2,1)S(1)} %collective-permute-done.1.other, s32[32]{0:T(128)S(1)} %copy-done.8, s32[1]{0:T(128)S(6)} %copy.17.valid, bf16[1,16384,128]{2,1,0:T(8,128)(2,1)S(1)} %copy-done.3, ...), custom_call_target="tpu_custom_call" | custom-call | tf_op jit(solution)/shard_map/pallas_call | solution.py:35
  31.1 0.0 copy-start
  31.1 0.0 copy-start.6
  31.1 0.0 copy-start.7
  31.1 1.3 %collective-permute-start.2 = (f32[136,128]{1,0:T(8,128)S(1)}, f32[136,128]{1,0:T(8,128)S(1)}, u32[]{:S(2)}, u32[]{:S(2)}) collective-permute-start(f32[136,128]{1,0:T(8,128)S(1)} %get-tuple-element.20), channel_id=1, source_target_pairs={{0,8},{8,0},{16,24},{24,16},{32,40},{40,32},{48,56},{56,48},{64,72... | collective-permute-start | bytes 208904 | tf_op jit(solution)/shard_map/ppermute | solution.py:442
  32.5 0.9 collective-permute-done.2.other
  33.4 11.4 %all_to_all.31.parts = bf16[8,144,128]{2,1,0:T(8,128)(2,1)S(1)} all-to-all(bf16[8,144,128]{2,1,0:T(8,128)(2,1)S(1)} %shard_map.162), channel_id=1, replica_groups={{0,16,32,48,64,80,96,112},{8,24,40,56,72,88,104,120},{1,17,33,49,65,81,..., dimensions={0} | all-to-all | bytes 589824 | tf_op jit(solution)/shard_map/all_to_all | solution.py:445
  44.8 0.2 shard_map.163.attn
  45.0 1.5 %collective-permute-start.3 = (bf16[32,512]{1,0:T(8,128)(2,1)S(1)}, bf16[32,512]{1,0:T(8,128)(2,1)S(1)}, u32[]{:S(2)}, u32[]{:S(2)}) collective-permute-start(bf16[32,512]{1,0:T(8,128)(2,1)S(1)} %shard_map.163.attn), channel_id=1, source_target_pairs={{0,8},{8,0},{16,24},{24,16},{32,40},{40,32},{48,56},{56,48},{64,72... | collective-permute-start | bytes 98312 | tf_op jit(solution)/shard_map/ppermute | solution.py:442
  46.5 0.0 copy-done.5
  46.5 0.2 shard_map.164.own
  46.7 0.7 collective-permute-done.3.attn
  47.4 0.2 shard_map.165
  47.6 11.6 %all_to_all.32.parts = bf16[8,32,512]{2,1,0:T(8,128)(2,1)S(1)} all-to-all(bf16[8,32,512]{2,1,0:T(8,128)(2,1)S(1)} %shard_map.165), channel_id=1, replica_groups=mesh['seq'=16,'tp'=8] {'tp'}, dimensions={0} | all-to-all | bytes 524288 | tf_op jit(solution)/shard_map/all_to_all | solution.py:448
  59.2 0.0 copy-done.1
  59.2 0.0 copy-done
  59.2 0.0 copy-done.6
  59.2 0.0 copy-done.7
  59.2 0.7 shard_map.166
  59.9 1.6 %collective-permute-start.4 = (bf16[32,3712]{1,0:T(8,128)(2,1)S(1)}, bf16[32,3712]{1,0:T(8,128)(2,1)S(1)}, u32[]{:S(2)}, u32[]{:S(2)}) collective-permute-start(bf16[32,3712]{1,0:T(8,128)(2,1)S(1)} %get-tuple-element.26), channel_id=1, source_target_pairs={{0,8},{8,0},{16,24},{24,16},{32,40},{40,32},{48,56},{56,48},{64,72... | collective-permute-start | bytes 712712 | tf_op jit(solution)/shard_map/ppermute | solution.py:442
  61.5 0.0 copy-start.2
  61.5 0.7 shard_map.167
  62.2 0.4 collective-permute-done.4.got
  62.6 0.1 shard_map.168
  62.7 10.5 %all_to_all.33.parts = bf16[8,16,1024]{2,1,0:T(8,128)(2,1)S(1)} all-to-all(bf16[8,16,1024]{2,1,0:T(8,128)(2,1)S(1)} %shard_map.168), channel_id=1, replica_groups={{0,16,32,48,64,80,96,112},{8,24,40,56,72,88,104,120},{1,17,33,49,65,81,..., dimensions={0} | all-to-all | bytes 524288 | tf_op jit(solution)/shard_map/all_to_all | solution.py:445
  73.2 0.1 shard_map.169
  73.4 10.0 %all_to_all.34.acts = bf16[8,16,512]{2,1,0:T(8,128)(2,1)S(1)} all-to-all(bf16[8,16,512]{2,1,0:T(8,128)(2,1)S(1)} %shard_map.169), channel_id=1, replica_groups={{0,16,32,48,64,80,96,112},{8,24,40,56,72,88,104,120},{1,17,33,49,65,81,..., dimensions={0} | all-to-all | bytes 262144 | tf_op jit(solution)/shard_map/all_to_all | solution.py:445
  83.3 2.6 %collective-permute-start.5 = (bf16[8,16,512]{2,1,0:T(8,128)(2,1)S(1)}, bf16[8,16,512]{2,1,0:T(8,128)(2,1)S(1)}, u32[]{:S(2)}, u32[]{:S(2)}) collective-permute-start(bf16[8,16,512]{2,1,0:T(8,128)(2,1)S(1)} %all_to_all.34.acts), channel_id=1, source_target_pairs={{0,8},{8,0},{16,24},{24,16},{32,40},{40,32},{48,56},{56,48},{64,72... | collective-permute-start | bytes 393224 | tf_op jit(solution)/shard_map/ppermute | solution.py:442
  85.9 0.0 copy-done.2
  85.9 0.4 shard_map.170.own
  86.3 0.6 collective-permute-done.5.acts
  86.9 0.4 shard_map.171
  87.3 9.5 %all_to_all.35.parts = bf16[8,32,512]{2,1,0:T(8,128)(2,1)S(1)} all-to-all(bf16[8,32,512]{2,1,0:T(8,128)(2,1)S(1)} %shard_map.171), channel_id=1, replica_groups=mesh['seq'=16,'tp'=8] {'tp'}, dimensions={0} | all-to-all | bytes 524288 | tf_op jit(solution)/shard_map/all_to_all | solution.py:448
  96.8 0.7 shard_map.172
  (1 shorter events, 0.0 us)
Async XLA Ops:
  2.3 2.4 %collective-permute-start = (f32[32,768]{1,0:T(8,128)S(1)}, f32[32,768]{1,0:T(8,128)S(1)}, u32[]{:S(2)}, u32[]{:S(2)}) collective-permute-start(f32[32,768]{1,0:T(8,128)S(1)} %get-tuple-element.16), channel_id=1, source_target_pairs={{0,8},{8,0},{16,24},{24,16},{32,40},{40,32},{48,56},{56,48},{64,72... | collective-permute-start | bytes 294920 | tf_op jit(solution)/shard_map/ppermute | solution.py:442
  4.7 21.1 %copy-start.3 = (bf16[1,16384,128]{2,1,0:T(8,128)(2,1)S(1)}, bf16[1,16384,128]{2,1,0:T(8,128)(2,1)}, u32[]{:S(2)}) copy-start(bf16[1,16384,128]{2,1,0:T(8,128)(2,1)} %keys.1) | copy-start | bytes 12582916
  4.7 21.1 %copy-start.4 = (bf16[1,16384,128]{2,1,0:T(8,128)(2,1)S(1)}, bf16[1,16384,128]{2,1,0:T(8,128)(2,1)}, u32[]{:S(2)}) copy-start(bf16[1,16384,128]{2,1,0:T(8,128)(2,1)} %values.1) | copy-start | bytes 12582916
  4.7 21.1 %copy-start.8 = (s32[32]{0:T(128)S(1)}, s32[32]{0:T(128)}, u32[]{:S(2)}) copy-start(s32[32]{0:T(128)} %positions.1) | copy-start | bytes 388
  23.3 2.5 %collective-permute-start.1 = (bf16[144,128]{1,0:T(8,128)(2,1)S(1)}, bf16[144,128]{1,0:T(8,128)(2,1)S(1)}, u32[]{:S(2)}, u32[]{:S(2)}) collective-permute-start(bf16[144,128]{1,0:T(8,128)(2,1)S(1)} %shard_map.160.own), channel_id=1, source_target_pairs={{0,8},{8,0},{16,24},{24,16},{32,40},{40,32},{48,56},{56,48},{64,72... | collective-permute-start | bytes 110600 | tf_op jit(solution)/shard_map/ppermute | solution.py:442
  25.6 20.9 %copy-start.5 = (bf16[1024,512]{1,0:T(8,128)(2,1)S(1)}, bf16[1024,512]{1,0:T(8,128)(2,1)}, u32[]{:S(2)}) copy-start(bf16[1024,512]{1,0:T(8,128)(2,1)} %w_out.3) | copy-start | bytes 3145732
  25.8 33.4 %copy-start.1 = (bf16[512,3584]{1,0:T(8,128)(2,1)S(1)}, bf16[512,3584]{1,0:T(8,128)(2,1)}, u32[]{:S(2)}) copy-start(bf16[512,3584]{1,0:T(8,128)(2,1)} %w_up.3) | copy-start | bytes 11010052
  31.1 28.1 %copy-start = (bf16[512,3584]{1,0:T(8,128)(2,1)S(1)}, bf16[512,3584]{1,0:T(8,128)(2,1)}, u32[]{:S(2)}) copy-start(bf16[512,3584]{1,0:T(8,128)(2,1)} %w_gate.3) | copy-start | bytes 11010052
  31.1 28.1 %copy-start.6 = (bf16[32,512]{1,0:T(8,128)(2,1)S(1)}, bf16[32,512]{1,0:T(8,128)(2,1)}, u32[]{:S(2)}) copy-start(bf16[32,512]{1,0:T(8,128)(2,1)} %resid.3) | copy-start | bytes 98308
  31.1 28.0 %copy-start.7 = (bf16[512]{0:T(512)(128)(2,1)S(1)}, bf16[512]{0:T(512)(128)(2,1)}, u32[]{:S(2)}) copy-start(bf16[512]{0:T(512)(128)(2,1)} %gain.3) | copy-start | bytes 3076
  31.1 2.2 %collective-permute-start.2 = (f32[136,128]{1,0:T(8,128)S(1)}, f32[136,128]{1,0:T(8,128)S(1)}, u32[]{:S(2)}, u32[]{:S(2)}) collective-permute-start(f32[136,128]{1,0:T(8,128)S(1)} %get-tuple-element.20), channel_id=1, source_target_pairs={{0,8},{8,0},{16,24},{24,16},{32,40},{40,32},{48,56},{56,48},{64,72... | collective-permute-start | bytes 208904 | tf_op jit(solution)/shard_map/ppermute | solution.py:442
  45.0 2.4 %collective-permute-start.3 = (bf16[32,512]{1,0:T(8,128)(2,1)S(1)}, bf16[32,512]{1,0:T(8,128)(2,1)S(1)}, u32[]{:S(2)}, u32[]{:S(2)}) collective-permute-start(bf16[32,512]{1,0:T(8,128)(2,1)S(1)} %shard_map.163.attn), channel_id=1, source_target_pairs={{0,8},{8,0},{16,24},{24,16},{32,40},{40,32},{48,56},{56,48},{64,72... | collective-permute-start | bytes 98312 | tf_op jit(solution)/shard_map/ppermute | solution.py:442
  59.9 2.7 %collective-permute-start.4 = (bf16[32,3712]{1,0:T(8,128)(2,1)S(1)}, bf16[32,3712]{1,0:T(8,128)(2,1)S(1)}, u32[]{:S(2)}, u32[]{:S(2)}) collective-permute-start(bf16[32,3712]{1,0:T(8,128)(2,1)S(1)} %get-tuple-element.26), channel_id=1, source_target_pairs={{0,8},{8,0},{16,24},{24,16},{32,40},{40,32},{48,56},{56,48},{64,72... | collective-permute-start | bytes 712712 | tf_op jit(solution)/shard_map/ppermute | solution.py:442
  61.5 24.4 %copy-start.2 = (bf16[3584,512]{1,0:T(8,128)(2,1)S(1)}, bf16[3584,512]{1,0:T(8,128)(2,1)}, u32[]{:S(2)}) copy-start(bf16[3584,512]{1,0:T(8,128)(2,1)} %w_down.3) | copy-start | bytes 11010052
  83.3 3.6 %collective-permute-start.5 = (bf16[8,16,512]{2,1,0:T(8,128)(2,1)S(1)}, bf16[8,16,512]{2,1,0:T(8,128)(2,1)S(1)}, u32[]{:S(2)}, u32[]{:S(2)}) collective-permute-start(bf16[8,16,512]{2,1,0:T(8,128)(2,1)S(1)} %all_to_all.34.acts), channel_id=1, source_target_pairs={{0,8},{8,0},{16,24},{24,16},{32,40},{40,32},{48,56},{56,48},{64,72... | collective-permute-start | bytes 393224 | tf_op jit(solution)/shard_map/ppermute | solution.py:442

commit v6 on v4

--- a/solution.py
+++ b/solution.py
@@ -336,12 +336,16 @@
         attn[:, g * 128 : (g + 1) * 128] = total[g * 32 : (g + 1) * 32].astype(BF16)
 
 
-def out_kernel(own, other, w_out, copies):
-    mine = core_index()
-    total = jnp.zeros((32, 512), F32)
-    for source, half in ((own, mine), (other, 1 - mine)):
-        total += dot(source[...], w_out[pl.ds(pl.multiple_of(half * 512, LANES), 512), :])
-    part = total.astype(BF16)
+def out_half(attn, w_out, half):
+    return dot(attn[...], w_out[pl.ds(pl.multiple_of(half * 512, LANES), 512), :])
+
+
+def out_own_kernel(attn, w_out, part):
+    part[...] = out_half(attn, w_out, core_index())
+
+
+def out_other_kernel(own, attn, w_out, copies):
+    part = (own[...] + out_half(attn, w_out, 1 - core_index())).astype(BF16)
     for j in range(8):
         copies[j] = part
 
@@ -504,7 +508,9 @@
     )(turned, to_other_core(turned), positions, valid_lengths, cache_keys, cache_values)
     copies = call(merge_pair_kernel, near((8, 144, LANES), BF16), [VMEM] * 2)(keep, to_other_core(send))
     attn = call(merge_kernel, near((32, 512), BF16), [VMEM])(over_chips(copies))
-    copies = call(out_kernel, near((8, 32, 512), BF16), [VMEM] * 3)(attn, to_other_core(attn), w_out)
+    got = to_other_core(attn)
+    part = call(out_own_kernel, near((32, 512), F32), [VMEM] * 2)(attn, w_out)
+    copies = call(out_other_kernel, near((8, 32, 512), BF16), [VMEM] * 3)(part, got, w_out)
     parts = over_tp(copies)
 
     branch, mid, normed, square, send = call(

time: 95.3 us -> 95.2 us (level)
  starting transfers between devices: 9.02 us -> 10.2 us
    ppermute x6, starting transfers between devices: 9.02 us -> 10.2 us  [to_other_core(): return lax.ppermute(x, 'seq', swap)]
    pallas_call x14 -> x15, Pallas kernels: 11.9 us -> 11.1 us  [run(): inner(*(pltpu.with_memory_space_constraint(x, pltpu.HBM) if s is HBM else...]
where the time goes in v6:
time: 95.2 us; the launch traced here: 94.9 us
  blocking collectives  68.4 us (72%)
  Pallas kernels  11.1 us (12%)
  starting transfers between devices  10.2 us (11%)
  waiting for transfers between devices  3.7 us (4%)
  between operations  1.42 us (1%)
    all_to_all x4, blocking collectives, over_chips(): return lax.all_to_all(x, 'seq', 0, 0, axis_index_groups=same_core)  47.4 us
    all_to_all x2, blocking collectives, over_tp(): return lax.all_to_all(x, 'tp', 0, 0)  21 us
    pallas_call x15, Pallas kernels, run(): inner(*(pltpu.with_memory_space_constraint(x, pltpu.HBM) if s is HBM else...  11.1 us
    ppermute x6, starting transfers between devices, to_other_core(): return lax.ppermute(x, 'seq', swap)  10.2 us
    ppermute x6, waiting for transfers between devices, to_other_core(): return lax.ppermute(x, 'seq', swap)  3.7 us
  transfers between devices with their start and end apart: 6, of which 6 were waited for; matrix products, arithmetic and copies ran while one was open for 0% of the time, Pallas kernels for 1%

profile of v6, /device:TPU:1, one launch (start us, length us, event | category | flops | bytes accessed | tf_op | source)
XLA Modules:
  0.0 94.9 jit_solution(16390012469894200176)
XLA Ops:
  0.6 1.6 %shard_map.158 = (f32[32,768]{1,0:T(8,128)S(1)}, f32[32,768]{1,0:T(8,128)S(1)}, f32[32,128]{1,0:T(8,128)S(1)}, f32[32,128]{1,0:T(8,128)S(1)}) custom-call(bf16[32,512]{1,0:T(8,128)(2,1)} %resid.3, bf16[512]{0:T(512)(128)(2,1)} %gain.2, bf16[512,1024]{1,0:T(8,128)(2,1)} %w_query.1, bf16[512,128]{1,0:T(8,128)(2,1)} %w_key.1, bf16[512,128]{1,0:T(8,128)(2,1)} %w_value.1, ...), custom_call_target="tpu_custom_call" | custom-call | tf_op jit(solution)/shard_map/pallas_call | solution.py:37
  2.3 1.5 %collective-permute-start = (f32[32,768]{1,0:T(8,128)S(1)}, f32[32,768]{1,0:T(8,128)S(1)}, u32[]{:S(2)}, u32[]{:S(2)}) collective-permute-start(f32[32,768]{1,0:T(8,128)S(1)} %get-tuple-element.16), channel_id=1, source_target_pairs={{0,8},{8,0},{16,24},{24,16},{32,40},{40,32},{48,56},{56,48},{64,72... | collective-permute-start | bytes 294920 | tf_op jit(solution)/shard_map/ppermute | solution.py:466
  3.8 0.9 collective-permute-done.other
  4.7 0.0 copy-start.3
  4.7 0.0 copy-start.4
  4.7 0.0 copy-start.8
  4.7 0.2 shard_map.159
  4.9 15.5 %all_to_all.30.parts = s16[8,144,128]{2,1,0:T(8,128)(2,1)S(1)} all-to-all(s16[8,144,128]{2,1,0:T(8,128)(2,1)S(1)} %shard_map.159), channel_id=1, replica_groups={{0,16,32,48,64,80,96,112},{8,24,40,56,72,88,104,120},{1,17,33,49,65,81,..., dimensions={0} | all-to-all | bytes 589824 | tf_op jit(solution)/shard_map/all_to_all | solution.py:469
  20.3 0.3 shard_map.160.own
  20.7 1.7 %collective-permute-start.1 = (bf16[144,128]{1,0:T(8,128)(2,1)S(1)}, bf16[144,128]{1,0:T(8,128)(2,1)S(1)}, u32[]{:S(2)}, u32[]{:S(2)}) collective-permute-start(bf16[144,128]{1,0:T(8,128)(2,1)S(1)} %shard_map.160.own), channel_id=1, source_target_pairs={{0,8},{8,0},{16,24},{24,16},{32,40},{40,32},{48,56},{56,48},{64,72... | collective-permute-start | bytes 110600 | tf_op jit(solution)/shard_map/ppermute | solution.py:466
  23.0 0.0 copy-start.5
  23.0 0.2 collective-permute-done.1.other
  23.2 0.0 copy-done.3
  23.2 0.0 copy-done.4
  23.2 0.0 copy-done.8
  23.2 0.0 copy-start.1
  23.2 5.3 %shard_map.161 = (f32[136,128]{1,0:T(8,128)S(1)}, f32[136,128]{1,0:T(8,128)S(1)}) custom-call(bf16[144,128]{1,0:T(8,128)(2,1)S(1)} %shard_map.160.own, bf16[144,128]{1,0:T(8,128)(2,1)S(1)} %collective-permute-done.1.other, s32[32]{0:T(128)S(1)} %copy-done.8, s32[1]{0:T(128)S(6)} %copy.17.valid, bf16[1,16384,128]{2,1,0:T(8,128)(2,1)S(1)} %copy-done.3, ...), custom_call_target="tpu_custom_call" | custom-call | tf_op jit(solution)/shard_map/pallas_call | solution.py:37
  28.5 0.0 copy-start
  28.5 0.0 copy-start.6
  28.5 0.0 copy-start.7
  28.6 1.3 %collective-permute-start.2 = (f32[136,128]{1,0:T(8,128)S(1)}, f32[136,128]{1,0:T(8,128)S(1)}, u32[]{:S(2)}, u32[]{:S(2)}) collective-permute-start(f32[136,128]{1,0:T(8,128)S(1)} %get-tuple-element.20), channel_id=1, source_target_pairs={{0,8},{8,0},{16,24},{24,16},{32,40},{40,32},{48,56},{56,48},{64,72... | collective-permute-start | bytes 208904 | tf_op jit(solution)/shard_map/ppermute | solution.py:466
  29.9 0.9 collective-permute-done.2.other
  30.8 11.4 %all_to_all.31.parts = bf16[8,144,128]{2,1,0:T(8,128)(2,1)S(1)} all-to-all(bf16[8,144,128]{2,1,0:T(8,128)(2,1)S(1)} %shard_map.162), channel_id=1, replica_groups={{0,16,32,48,64,80,96,112},{8,24,40,56,72,88,104,120},{1,17,33,49,65,81,..., dimensions={0} | all-to-all | bytes 589824 | tf_op jit(solution)/shard_map/all_to_all | solution.py:469
  42.2 0.2 shard_map.163.attn
  42.4 1.5 %collective-permute-start.3 = (bf16[32,512]{1,0:T(8,128)(2,1)S(1)}, bf16[32,512]{1,0:T(8,128)(2,1)S(1)}, u32[]{:S(2)}, u32[]{:S(2)}) collective-permute-start(bf16[32,512]{1,0:T(8,128)(2,1)S(1)} %shard_map.163.attn), channel_id=1, source_target_pairs={{0,8},{8,0},{16,24},{24,16},{32,40},{40,32},{48,56},{56,48},{64,72... | collective-permute-start | bytes 98312 | tf_op jit(solution)/shard_map/ppermute | solution.py:466
  43.9 0.0 copy-done.5
  43.9 0.2 shard_map.164.own
  44.1 0.7 collective-permute-done.3.attn
  44.8 0.2 shard_map.165
  45.0 11.6 %all_to_all.32.parts = bf16[8,32,512]{2,1,0:T(8,128)(2,1)S(1)} all-to-all(bf16[8,32,512]{2,1,0:T(8,128)(2,1)S(1)} %shard_map.165), channel_id=1, replica_groups=mesh['seq'=16,'tp'=8] {'tp'}, dimensions={0} | all-to-all | bytes 524288 | tf_op jit(solution)/shard_map/all_to_all | solution.py:472
  56.6 0.0 copy-done.1
  56.6 0.0 copy-done
  56.6 0.0 copy-done.6
  56.6 0.0 copy-done.7
  56.6 0.7 shard_map.166
  57.3 1.6 %collective-permute-start.4 = (bf16[32,3712]{1,0:T(8,128)(2,1)S(1)}, bf16[32,3712]{1,0:T(8,128)(2,1)S(1)}, u32[]{:S(2)}, u32[]{:S(2)}) collective-permute-start(bf16[32,3712]{1,0:T(8,128)(2,1)S(1)} %get-tuple-element.26), channel_id=1, source_target_pairs={{0,8},{8,0},{16,24},{24,16},{32,40},{40,32},{48,56},{56,48},{64,72... | collective-permute-start | bytes 712712 | tf_op jit(solution)/shard_map/ppermute | solution.py:466
  58.9 0.0 copy-start.2
  58.9 0.7 shard_map.167
  59.6 0.4 collective-permute-done.4.got
  60.0 0.1 shard_map.168
  60.1 10.5 %all_to_all.33.parts = bf16[8,16,1024]{2,1,0:T(8,128)(2,1)S(1)} all-to-all(bf16[8,16,1024]{2,1,0:T(8,128)(2,1)S(1)} %shard_map.168), channel_id=1, replica_groups={{0,16,32,48,64,80,96,112},{8,24,40,56,72,88,104,120},{1,17,33,49,65,81,..., dimensions={0} | all-to-all | bytes 524288 | tf_op jit(solution)/shard_map/all_to_all | solution.py:469
  70.6 0.1 shard_map.169
  70.8 10.0 %all_to_all.34.acts = bf16[8,16,512]{2,1,0:T(8,128)(2,1)S(1)} all-to-all(bf16[8,16,512]{2,1,0:T(8,128)(2,1)S(1)} %shard_map.169), channel_id=1, replica_groups={{0,16,32,48,64,80,96,112},{8,24,40,56,72,88,104,120},{1,17,33,49,65,81,..., dimensions={0} | all-to-all | bytes 262144 | tf_op jit(solution)/shard_map/all_to_all | solution.py:469
  80.7 2.6 %collective-permute-start.5 = (bf16[8,16,512]{2,1,0:T(8,128)(2,1)S(1)}, bf16[8,16,512]{2,1,0:T(8,128)(2,1)S(1)}, u32[]{:S(2)}, u32[]{:S(2)}) collective-permute-start(bf16[8,16,512]{2,1,0:T(8,128)(2,1)S(1)} %all_to_all.34.acts), channel_id=1, source_target_pairs={{0,8},{8,0},{16,24},{24,16},{32,40},{40,32},{48,56},{56,48},{64,72... | collective-permute-start | bytes 393224 | tf_op jit(solution)/shard_map/ppermute | solution.py:466
  83.3 0.0 copy-done.2
  83.3 0.4 shard_map.170.own
  83.7 0.6 collective-permute-done.5.acts
  84.3 0.4 shard_map.171
  84.8 9.5 %all_to_all.35.parts = bf16[8,32,512]{2,1,0:T(8,128)(2,1)S(1)} all-to-all(bf16[8,32,512]{2,1,0:T(8,128)(2,1)S(1)} %shard_map.171), channel_id=1, replica_groups=mesh['seq'=16,'tp'=8] {'tp'}, dimensions={0} | all-to-all | bytes 524288 | tf_op jit(solution)/shard_map/all_to_all | solution.py:472
  94.2 0.7 shard_map.172
  (1 shorter events, 0.0 us)
Async XLA Ops:
  2.3 2.4 %collective-permute-start = (f32[32,768]{1,0:T(8,128)S(1)}, f32[32,768]{1,0:T(8,128)S(1)}, u32[]{:S(2)}, u32[]{:S(2)}) collective-permute-start(f32[32,768]{1,0:T(8,128)S(1)} %get-tuple-element.16), channel_id=1, source_target_pairs={{0,8},{8,0},{16,24},{24,16},{32,40},{40,32},{48,56},{56,48},{64,72... | collective-permute-start | bytes 294920 | tf_op jit(solution)/shard_map/ppermute | solution.py:466
  4.7 18.5 %copy-start.3 = (bf16[1,16384,128]{2,1,0:T(8,128)(2,1)S(1)}, bf16[1,16384,128]{2,1,0:T(8,128)(2,1)}, u32[]{:S(2)}) copy-start(bf16[1,16384,128]{2,1,0:T(8,128)(2,1)} %keys.1) | copy-start | bytes 12582916
  4.7 18.5 %copy-start.4 = (bf16[1,16384,128]{2,1,0:T(8,128)(2,1)S(1)}, bf16[1,16384,128]{2,1,0:T(8,128)(2,1)}, u32[]{:S(2)}) copy-start(bf16[1,16384,128]{2,1,0:T(8,128)(2,1)} %values.1) | copy-start | bytes 12582916
  4.7 18.5 %copy-start.8 = (s32[32]{0:T(128)S(1)}, s32[32]{0:T(128)}, u32[]{:S(2)}) copy-start(s32[32]{0:T(128)} %positions.1) | copy-start | bytes 388
  20.7 2.5 %collective-permute-start.1 = (bf16[144,128]{1,0:T(8,128)(2,1)S(1)}, bf16[144,128]{1,0:T(8,128)(2,1)S(1)}, u32[]{:S(2)}, u32[]{:S(2)}) collective-permute-start(bf16[144,128]{1,0:T(8,128)(2,1)S(1)} %shard_map.160.own), channel_id=1, source_target_pairs={{0,8},{8,0},{16,24},{24,16},{32,40},{40,32},{48,56},{56,48},{64,72... | collective-permute-start | bytes 110600 | tf_op jit(solution)/shard_map/ppermute | solution.py:466
  23.0 20.9 %copy-start.5 = (bf16[1024,512]{1,0:T(8,128)(2,1)S(1)}, bf16[1024,512]{1,0:T(8,128)(2,1)}, u32[]{:S(2)}) copy-start(bf16[1024,512]{1,0:T(8,128)(2,1)} %w_out.3) | copy-start | bytes 3145732
  23.2 33.4 %copy-start.1 = (bf16[512,3584]{1,0:T(8,128)(2,1)S(1)}, bf16[512,3584]{1,0:T(8,128)(2,1)}, u32[]{:S(2)}) copy-start(bf16[512,3584]{1,0:T(8,128)(2,1)} %w_up.3) | copy-start | bytes 11010052
  28.5 28.1 %copy-start = (bf16[512,3584]{1,0:T(8,128)(2,1)S(1)}, bf16[512,3584]{1,0:T(8,128)(2,1)}, u32[]{:S(2)}) copy-start(bf16[512,3584]{1,0:T(8,128)(2,1)} %w_gate.3) | copy-start | bytes 11010052
  28.5 28.1 %copy-start.6 = (bf16[32,512]{1,0:T(8,128)(2,1)S(1)}, bf16[32,512]{1,0:T(8,128)(2,1)}, u32[]{:S(2)}) copy-start(bf16[32,512]{1,0:T(8,128)(2,1)} %resid.3) | copy-start | bytes 98308
  28.5 28.0 %copy-start.7 = (bf16[512]{0:T(512)(128)(2,1)S(1)}, bf16[512]{0:T(512)(128)(2,1)}, u32[]{:S(2)}) copy-start(bf16[512]{0:T(512)(128)(2,1)} %gain.3) | copy-start | bytes 3076
  28.6 2.2 %collective-permute-start.2 = (f32[136,128]{1,0:T(8,128)S(1)}, f32[136,128]{1,0:T(8,128)S(1)}, u32[]{:S(2)}, u32[]{:S(2)}) collective-permute-start(f32[136,128]{1,0:T(8,128)S(1)} %get-tuple-element.20), channel_id=1, source_target_pairs={{0,8},{8,0},{16,24},{24,16},{32,40},{40,32},{48,56},{56,48},{64,72... | collective-permute-start | bytes 208904 | tf_op jit(solution)/shard_map/ppermute | solution.py:466
  42.4 2.4 %collective-permute-start.3 = (bf16[32,512]{1,0:T(8,128)(2,1)S(1)}, bf16[32,512]{1,0:T(8,128)(2,1)S(1)}, u32[]{:S(2)}, u32[]{:S(2)}) collective-permute-start(bf16[32,512]{1,0:T(8,128)(2,1)S(1)} %shard_map.163.attn), channel_id=1, source_target_pairs={{0,8},{8,0},{16,24},{24,16},{32,40},{40,32},{48,56},{56,48},{64,72... | collective-permute-start | bytes 98312 | tf_op jit(solution)/shard_map/ppermute | solution.py:466
  57.3 2.7 %collective-permute-start.4 = (bf16[32,3712]{1,0:T(8,128)(2,1)S(1)}, bf16[32,3712]{1,0:T(8,128)(2,1)S(1)}, u32[]{:S(2)}, u32[]{:S(2)}) collective-permute-start(bf16[32,3712]{1,0:T(8,128)(2,1)S(1)} %get-tuple-element.26), channel_id=1, source_target_pairs={{0,8},{8,0},{16,24},{24,16},{32,40},{40,32},{48,56},{56,48},{64,72... | collective-permute-start | bytes 712712 | tf_op jit(solution)/shard_map/ppermute | solution.py:466
  58.9 24.4 %copy-start.2 = (bf16[3584,512]{1,0:T(8,128)(2,1)S(1)}, bf16[3584,512]{1,0:T(8,128)(2,1)}, u32[]{:S(2)}) copy-start(bf16[3584,512]{1,0:T(8,128)(2,1)} %w_down.3) | copy-start | bytes 11010052
  80.7 3.6 %collective-permute-start.5 = (bf16[8,16,512]{2,1,0:T(8,128)(2,1)S(1)}, bf16[8,16,512]{2,1,0:T(8,128)(2,1)S(1)}, u32[]{:S(2)}, u32[]{:S(2)}) collective-permute-start(bf16[8,16,512]{2,1,0:T(8,128)(2,1)S(1)} %all_to_all.34.acts), channel_id=1, source_target_pairs={{0,8},{8,0},{16,24},{24,16},{32,40},{40,32},{48,56},{56,48},{64,72... | collective-permute-start | bytes 393224 | tf_op jit(solution)/shard_map/ppermute | solution.py:466

commit v7 on v4

--- a/solution.py
+++ b/solution.py
@@ -247,7 +247,7 @@
         total_l[...] = jnp.zeros((8, 256), F32)
         total_o[...] = jnp.zeros((LANES, 256), F32)
 
-    restart(jnp.max(only_valid(score(0, 256), 0), axis=0, keepdims=True))
+    restart(jnp.max(only_valid(score(0, 128), 0), axis=0, keepdims=True))
 
     @pl.when(length == 16384)
     def _():

time: 95.3 us -> 95.3 us (level)
  starting transfers between devices: 9.02 us -> 11.7 us
  Pallas kernels: 11.9 us -> 9.52 us
    ppermute x6, starting transfers between devices: 9.02 us -> 11.7 us  [to_other_core(): return lax.ppermute(x, 'seq', swap)]
    pallas_call x14, Pallas kernels: 11.9 us -> 9.52 us  [run(): inner(*(pltpu.with_memory_space_constraint(x, pltpu.HBM) if s is HBM else...]
where the time goes in v7:
time: 95.3 us; the launch traced here: 94.9 us
  blocking collectives  68.4 us (72%)
  starting transfers between devices  11.7 us (12%)
  Pallas kernels  9.52 us (10%)
  waiting for transfers between devices  3.86 us (4%)
  between operations  1.42 us (1%)
    all_to_all x4, blocking collectives, over_chips(): return lax.all_to_all(x, 'seq', 0, 0, axis_index_groups=same_core)  47.4 us
    all_to_all x2, blocking collectives, over_tp(): return lax.all_to_all(x, 'tp', 0, 0)  21 us
    ppermute x6, starting transfers between devices, to_other_core(): return lax.ppermute(x, 'seq', swap)  11.7 us
    pallas_call x14, Pallas kernels, run(): inner(*(pltpu.with_memory_space_constraint(x, pltpu.HBM) if s is HBM else...  9.52 us
    ppermute x6, waiting for transfers between devices, to_other_core(): return lax.ppermute(x, 'seq', swap)  3.86 us
  transfers between devices with their start and end apart: 6, of which 6 were waited for; matrix products, arithmetic and copies ran while one was open for 0% of the time, Pallas kernels for 1%

profile of v7, /device:TPU:1, one launch (start us, length us, event | category | flops | bytes accessed | tf_op | source)
XLA Modules:
  0.0 94.9 jit_solution(3399137012869081996)
XLA Ops:
  0.6 1.6 %shard_map.158 = (f32[32,768]{1,0:T(8,128)S(1)}, f32[32,768]{1,0:T(8,128)S(1)}, f32[32,128]{1,0:T(8,128)S(1)}, f32[32,128]{1,0:T(8,128)S(1)}) custom-call(bf16[32,512]{1,0:T(8,128)(2,1)} %resid.3, bf16[512]{0:T(512)(128)(2,1)} %gain.2, bf16[512,1024]{1,0:T(8,128)(2,1)} %w_query.1, bf16[512,128]{1,0:T(8,128)(2,1)} %w_key.1, bf16[512,128]{1,0:T(8,128)(2,1)} %w_value.1, ...), custom_call_target="tpu_custom_call" | custom-call | tf_op jit(solution)/shard_map/pallas_call | solution.py:37
  2.3 1.5 %collective-permute-start = (f32[32,768]{1,0:T(8,128)S(1)}, f32[32,768]{1,0:T(8,128)S(1)}, u32[]{:S(2)}, u32[]{:S(2)}) collective-permute-start(f32[32,768]{1,0:T(8,128)S(1)} %get-tuple-element.16), channel_id=1, source_target_pairs={{0,8},{8,0},{16,24},{24,16},{32,40},{40,32},{48,56},{56,48},{64,72... | collective-permute-start | bytes 294920 | tf_op jit(solution)/shard_map/ppermute | solution.py:462
  3.8 0.9 collective-permute-done.other
  4.7 0.0 copy-start.3
  4.7 0.0 copy-start.4
  4.7 0.0 copy-start.8
  4.7 0.2 shard_map.159
  4.9 15.5 %all_to_all.30.parts = s16[8,144,128]{2,1,0:T(8,128)(2,1)S(1)} all-to-all(s16[8,144,128]{2,1,0:T(8,128)(2,1)S(1)} %shard_map.159), channel_id=1, replica_groups={{0,16,32,48,64,80,96,112},{8,24,40,56,72,88,104,120},{1,17,33,49,65,81,..., dimensions={0} | all-to-all | bytes 589824 | tf_op jit(solution)/shard_map/all_to_all | solution.py:465
  20.3 0.3 shard_map.160.own
  20.7 1.7 %collective-permute-start.1 = (bf16[144,128]{1,0:T(8,128)(2,1)S(1)}, bf16[144,128]{1,0:T(8,128)(2,1)S(1)}, u32[]{:S(2)}, u32[]{:S(2)}) collective-permute-start(bf16[144,128]{1,0:T(8,128)(2,1)S(1)} %shard_map.160.own), channel_id=1, source_target_pairs={{0,8},{8,0},{16,24},{24,16},{32,40},{40,32},{48,56},{56,48},{64,72... | collective-permute-start | bytes 110600 | tf_op jit(solution)/shard_map/ppermute | solution.py:462
  23.0 0.0 copy-start.5
  23.0 0.0 copy-start.6
  23.0 0.0 copy-start.7
  23.0 0.2 collective-permute-done.1.other
  23.2 0.0 copy-done.3
  23.2 0.0 copy-done.4
  23.2 0.0 copy-done.8
  23.2 0.0 copy-start
  23.2 0.0 copy-start.1
  23.2 3.8 %shard_map.161 = (f32[136,128]{1,0:T(8,128)S(1)}, f32[136,128]{1,0:T(8,128)S(1)}) custom-call(bf16[144,128]{1,0:T(8,128)(2,1)S(1)} %shard_map.160.own, bf16[144,128]{1,0:T(8,128)(2,1)S(1)} %collective-permute-done.1.other, s32[32]{0:T(128)S(1)} %copy-done.8, s32[1]{0:T(128)S(6)} %copy.17.valid, bf16[1,16384,128]{2,1,0:T(8,128)(2,1)S(1)} %copy-done.3, ...), custom_call_target="tpu_custom_call" | custom-call | tf_op jit(solution)/shard_map/pallas_call | solution.py:37
  27.0 2.8 %collective-permute-start.2 = (f32[136,128]{1,0:T(8,128)S(1)}, f32[136,128]{1,0:T(8,128)S(1)}, u32[]{:S(2)}, u32[]{:S(2)}) collective-permute-start(f32[136,128]{1,0:T(8,128)S(1)} %get-tuple-element.20), channel_id=1, source_target_pairs={{0,8},{8,0},{16,24},{24,16},{32,40},{40,32},{48,56},{56,48},{64,72... | collective-permute-start | bytes 208904 | tf_op jit(solution)/shard_map/ppermute | solution.py:462
  29.8 0.9 collective-permute-done.2.other
  30.8 11.4 %all_to_all.31.parts = bf16[8,144,128]{2,1,0:T(8,128)(2,1)S(1)} all-to-all(bf16[8,144,128]{2,1,0:T(8,128)(2,1)S(1)} %shard_map.162), channel_id=1, replica_groups={{0,16,32,48,64,80,96,112},{8,24,40,56,72,88,104,120},{1,17,33,49,65,81,..., dimensions={0} | all-to-all | bytes 589824 | tf_op jit(solution)/shard_map/all_to_all | solution.py:465
  42.2 0.2 shard_map.163.own
  42.3 1.5 %collective-permute-start.3 = (bf16[32,512]{1,0:T(8,128)(2,1)S(1)}, bf16[32,512]{1,0:T(8,128)(2,1)S(1)}, u32[]{:S(2)}, u32[]{:S(2)}) collective-permute-start(bf16[32,512]{1,0:T(8,128)(2,1)S(1)} %shard_map.163.own), channel_id=1, source_target_pairs={{0,8},{8,0},{16,24},{24,16},{32,40},{40,32},{48,56},{56,48},{64,72... | collective-permute-start | bytes 98312 | tf_op jit(solution)/shard_map/ppermute | solution.py:462
  43.9 0.9 collective-permute-done.3.other
  44.7 0.0 copy-done.5
  44.7 0.3 shard_map.164
  45.0 11.6 %all_to_all.32.parts = bf16[8,32,512]{2,1,0:T(8,128)(2,1)S(1)} all-to-all(bf16[8,32,512]{2,1,0:T(8,128)(2,1)S(1)} %shard_map.164), channel_id=1, replica_groups=mesh['seq'=16,'tp'=8] {'tp'}, dimensions={0} | all-to-all | bytes 524288 | tf_op jit(solution)/shard_map/all_to_all | solution.py:468
  56.6 0.0 copy-done.6
  56.6 0.0 copy-done.7
  56.6 0.0 copy-done
  56.6 0.0 copy-done.1
  56.6 0.7 shard_map.165
  57.4 1.6 %collective-permute-start.4 = (bf16[32,3712]{1,0:T(8,128)(2,1)S(1)}, bf16[32,3712]{1,0:T(8,128)(2,1)S(1)}, u32[]{:S(2)}, u32[]{:S(2)}) collective-permute-start(bf16[32,3712]{1,0:T(8,128)(2,1)S(1)} %get-tuple-element.26), channel_id=1, source_target_pairs={{0,8},{8,0},{16,24},{24,16},{32,40},{40,32},{48,56},{56,48},{64,72... | collective-permute-start | bytes 712712 | tf_op jit(solution)/shard_map/ppermute | solution.py:462
  58.9 0.0 copy-start.2
  58.9 0.7 shard_map.166
  59.7 0.4 collective-permute-done.4.got
  60.1 0.1 shard_map.167
  60.2 10.5 %all_to_all.33.parts = bf16[8,16,1024]{2,1,0:T(8,128)(2,1)S(1)} all-to-all(bf16[8,16,1024]{2,1,0:T(8,128)(2,1)S(1)} %shard_map.167), channel_id=1, replica_groups={{0,16,32,48,64,80,96,112},{8,24,40,56,72,88,104,120},{1,17,33,49,65,81,..., dimensions={0} | all-to-all | bytes 524288 | tf_op jit(solution)/shard_map/all_to_all | solution.py:465
  70.7 0.1 shard_map.168
  70.8 10.0 %all_to_all.34.acts = bf16[8,16,512]{2,1,0:T(8,128)(2,1)S(1)} all-to-all(bf16[8,16,512]{2,1,0:T(8,128)(2,1)S(1)} %shard_map.168), channel_id=1, replica_groups={{0,16,32,48,64,80,96,112},{8,24,40,56,72,88,104,120},{1,17,33,49,65,81,..., dimensions={0} | all-to-all | bytes 262144 | tf_op jit(solution)/shard_map/all_to_all | solution.py:465
  80.8 2.6 %collective-permute-start.5 = (bf16[8,16,512]{2,1,0:T(8,128)(2,1)S(1)}, bf16[8,16,512]{2,1,0:T(8,128)(2,1)S(1)}, u32[]{:S(2)}, u32[]{:S(2)}) collective-permute-start(bf16[8,16,512]{2,1,0:T(8,128)(2,1)S(1)} %all_to_all.34.acts), channel_id=1, source_target_pairs={{0,8},{8,0},{16,24},{24,16},{32,40},{40,32},{48,56},{56,48},{64,72... | collective-permute-start | bytes 393224 | tf_op jit(solution)/shard_map/ppermute | solution.py:462
  83.4 0.0 copy-done.2
  83.4 0.4 shard_map.169.own
  83.8 0.6 collective-permute-done.5.acts
  84.4 0.4 shard_map.170
  84.8 9.5 %all_to_all.35.parts = bf16[8,32,512]{2,1,0:T(8,128)(2,1)S(1)} all-to-all(bf16[8,32,512]{2,1,0:T(8,128)(2,1)S(1)} %shard_map.170), channel_id=1, replica_groups=mesh['seq'=16,'tp'=8] {'tp'}, dimensions={0} | all-to-all | bytes 524288 | tf_op jit(solution)/shard_map/all_to_all | solution.py:468
  94.3 0.7 shard_map.171
  (1 shorter events, 0.0 us)
Async XLA Ops:
  2.3 2.4 %collective-permute-start = (f32[32,768]{1,0:T(8,128)S(1)}, f32[32,768]{1,0:T(8,128)S(1)}, u32[]{:S(2)}, u32[]{:S(2)}) collective-permute-start(f32[32,768]{1,0:T(8,128)S(1)} %get-tuple-element.16), channel_id=1, source_target_pairs={{0,8},{8,0},{16,24},{24,16},{32,40},{40,32},{48,56},{56,48},{64,72... | collective-permute-start | bytes 294920 | tf_op jit(solution)/shard_map/ppermute | solution.py:462
  4.7 18.5 %copy-start.3 = (bf16[1,16384,128]{2,1,0:T(8,128)(2,1)S(1)}, bf16[1,16384,128]{2,1,0:T(8,128)(2,1)}, u32[]{:S(2)}) copy-start(bf16[1,16384,128]{2,1,0:T(8,128)(2,1)} %keys.1) | copy-start | bytes 12582916
  4.7 18.5 %copy-start.4 = (bf16[1,16384,128]{2,1,0:T(8,128)(2,1)S(1)}, bf16[1,16384,128]{2,1,0:T(8,128)(2,1)}, u32[]{:S(2)}) copy-start(bf16[1,16384,128]{2,1,0:T(8,128)(2,1)} %values.1) | copy-start | bytes 12582916
  4.7 18.5 %copy-start.8 = (s32[32]{0:T(128)S(1)}, s32[32]{0:T(128)}, u32[]{:S(2)}) copy-start(s32[32]{0:T(128)} %positions.1) | copy-start | bytes 388
  20.7 2.5 %collective-permute-start.1 = (bf16[144,128]{1,0:T(8,128)(2,1)S(1)}, bf16[144,128]{1,0:T(8,128)(2,1)S(1)}, u32[]{:S(2)}, u32[]{:S(2)}) collective-permute-start(bf16[144,128]{1,0:T(8,128)(2,1)S(1)} %shard_map.160.own), channel_id=1, source_target_pairs={{0,8},{8,0},{16,24},{24,16},{32,40},{40,32},{48,56},{56,48},{64,72... | collective-permute-start | bytes 110600 | tf_op jit(solution)/shard_map/ppermute | solution.py:462
  23.0 21.7 %copy-start.5 = (bf16[1024,512]{1,0:T(8,128)(2,1)S(1)}, bf16[1024,512]{1,0:T(8,128)(2,1)}, u32[]{:S(2)}) copy-start(bf16[1024,512]{1,0:T(8,128)(2,1)} %w_out.1) | copy-start | bytes 3145732
  23.0 33.6 %copy-start.6 = (bf16[32,512]{1,0:T(8,128)(2,1)S(1)}, bf16[32,512]{1,0:T(8,128)(2,1)}, u32[]{:S(2)}) copy-start(bf16[32,512]{1,0:T(8,128)(2,1)} %resid.3) | copy-start | bytes 98308
  23.0 33.6 %copy-start.7 = (bf16[512]{0:T(512)(128)(2,1)S(1)}, bf16[512]{0:T(512)(128)(2,1)}, u32[]{:S(2)}) copy-start(bf16[512]{0:T(512)(128)(2,1)} %gain.3) | copy-start | bytes 3076
  23.2 33.4 %copy-start = (bf16[512,3584]{1,0:T(8,128)(2,1)S(1)}, bf16[512,3584]{1,0:T(8,128)(2,1)}, u32[]{:S(2)}) copy-start(bf16[512,3584]{1,0:T(8,128)(2,1)} %w_gate.3) | copy-start | bytes 11010052
  23.2 33.4 %copy-start.1 = (bf16[512,3584]{1,0:T(8,128)(2,1)S(1)}, bf16[512,3584]{1,0:T(8,128)(2,1)}, u32[]{:S(2)}) copy-start(bf16[512,3584]{1,0:T(8,128)(2,1)} %w_up.3) | copy-start | bytes 11010052
  27.0 3.7 %collective-permute-start.2 = (f32[136,128]{1,0:T(8,128)S(1)}, f32[136,128]{1,0:T(8,128)S(1)}, u32[]{:S(2)}, u32[]{:S(2)}) collective-permute-start(f32[136,128]{1,0:T(8,128)S(1)} %get-tuple-element.20), channel_id=1, source_target_pairs={{0,8},{8,0},{16,24},{24,16},{32,40},{40,32},{48,56},{56,48},{64,72... | collective-permute-start | bytes 208904 | tf_op jit(solution)/shard_map/ppermute | solution.py:462
  42.3 2.4 %collective-permute-start.3 = (bf16[32,512]{1,0:T(8,128)(2,1)S(1)}, bf16[32,512]{1,0:T(8,128)(2,1)S(1)}, u32[]{:S(2)}, u32[]{:S(2)}) collective-permute-start(bf16[32,512]{1,0:T(8,128)(2,1)S(1)} %shard_map.163.own), channel_id=1, source_target_pairs={{0,8},{8,0},{16,24},{24,16},{32,40},{40,32},{48,56},{56,48},{64,72... | collective-permute-start | bytes 98312 | tf_op jit(solution)/shard_map/ppermute | solution.py:462
  57.4 2.7 %collective-permute-start.4 = (bf16[32,3712]{1,0:T(8,128)(2,1)S(1)}, bf16[32,3712]{1,0:T(8,128)(2,1)S(1)}, u32[]{:S(2)}, u32[]{:S(2)}) collective-permute-start(bf16[32,3712]{1,0:T(8,128)(2,1)S(1)} %get-tuple-element.26), channel_id=1, source_target_pairs={{0,8},{8,0},{16,24},{24,16},{32,40},{40,32},{48,56},{56,48},{64,72... | collective-permute-start | bytes 712712 | tf_op jit(solution)/shard_map/ppermute | solution.py:462
  58.9 24.4 %copy-start.2 = (bf16[3584,512]{1,0:T(8,128)(2,1)S(1)}, bf16[3584,512]{1,0:T(8,128)(2,1)}, u32[]{:S(2)}) copy-start(bf16[3584,512]{1,0:T(8,128)(2,1)} %w_down.3) | copy-start | bytes 11010052
  80.8 3.6 %collective-permute-start.5 = (bf16[8,16,512]{2,1,0:T(8,128)(2,1)S(1)}, bf16[8,16,512]{2,1,0:T(8,128)(2,1)S(1)}, u32[]{:S(2)}, u32[]{:S(2)}) collective-permute-start(bf16[8,16,512]{2,1,0:T(8,128)(2,1)S(1)} %all_to_all.34.acts), channel_id=1, source_target_pairs={{0,8},{8,0},{16,24},{24,16},{32,40},{40,32},{48,56},{56,48},{64,72... | collective-permute-start | bytes 393224 | tf_op jit(solution)/shard_map/ppermute | solution.py:462
